TPU v7x, 256 devices: a whole 4x4x8 slice. The times are simulated.
256 devices in a mesh: dp: 8 (over x, z_hi), tensor: 32 (over z_lo, y, core).
Axes of the slice: x: 4, y: 4, z: 8 (z_hi: 2, z_lo: 4; z = z_hi * 4 + z_lo), core: 2. Of those that a mesh axis runs over, the one named last changes fastest.
Arguments:
- tokens: bfloat16 [2048, 4096], P('dp', 'tensor'), may hold values from -6 to 6
- cotangent: bfloat16 [2048, 4096], P('dp', 'tensor'), may hold values from -6 to 6
- gu_master: float32 [2, 4096, 8192], P(None, 'dp', 'tensor'), may hold values from -0.09375 to 0.09375
- gu_first: float32 [2, 4096, 8192], P(None, 'dp', 'tensor'), may hold values from -0.046875 to 0.046875
- gu_second: float32 [2, 4096, 8192], P(None, 'dp', 'tensor'), may hold values from 1e-06 to 0.0001
- gu_codes: int32 [2, 1024, 8192], P(None, 'dp', 'tensor'), may hold values from 0 to 5
- gu_expo: int32 [2, 8192], P(None, 'tensor'), may hold values from -6 to -4
- down_master: float32 [8192, 4096], P('tensor', 'dp'), may hold values from -0.0625 to 0.0625
- down_first: float32 [8192, 4096], P('tensor', 'dp'), may hold values from -0.046875 to 0.046875
- down_second: float32 [8192, 4096], P('tensor', 'dp'), may hold values from 1e-06 to 0.0001
- down_codes: int32 [2048, 4096], P('tensor', 'dp'), may hold values from 0 to 5
- down_expo: int32 [4096], P('dp'), may hold values from -7 to -5
Outputs:
- mixed: bfloat16 [2048, 4096], P('dp', 'tensor')
- token_grad: bfloat16 [2048, 4096], P('dp', 'tensor')
- gu_new: float32 [2, 4096, 8192], P(None, 'dp', 'tensor')
- gu_first_new: float32 [2, 4096, 8192], P(None, 'dp', 'tensor')
- gu_second_new: float32 [2, 4096, 8192], P(None, 'dp', 'tensor')
- gu_copy: bfloat16 [2, 4096, 8192], P(None, 'dp', 'tensor')
- down_new: float32 [8192, 4096], P('tensor', 'dp')
- down_first_new: float32 [8192, 4096], P('tensor', 'dp')
- down_second_new: float32 [8192, 4096], P('tensor', 'dp')
- down_copy: bfloat16 [8192, 4096], P('tensor', 'dp')
Inputs may be any that keep to these rules, and one draw needn't show every extreme that they name: `gu_codes`: code of which two of the four rows of a group are kept: 0 (0,1), 1 (0,2), 2 (0,3), 3 (1,2), 4 (1,3), 5 (2,3). `down_codes`: code of which two of the four hidden units of a group are kept, numbered as for gu_codes.
All inputs are finite; a program needn't handle non-finite values.
Results may differ from a plain program's by a relative error of at most 0.03.
Values may be sent and summed in bfloat16 or wider, within the bound.
No kernel may reach another device: no remote copies, remote signals or barrier semaphores. Data moves between devices by JAX's collectives and lax.ppermute only.
A program may use at most 128 MiB of HBM per device.

v0:
```python
import jax
import jax.numpy as jnp
from jax import lax
from jax.sharding import PartitionSpec as P

BETA_ONE = 0.9
BETA_TWO = 0.95
ADAM_EPS = 1e-08
LEARN_RATE = 0.002
CORRECT_ONE = 1.0 - 0.9**10
CORRECT_TWO = 1.0 - 0.95**10


def power_of_two(expo):
    result = jnp.zeros(expo.shape, jnp.float32)
    for level in range(-8, 0):
        result = jnp.where(expo == level, jnp.float32(2.0**level), result)
    return result


def expand_codes(codes):
    first = jnp.where(codes < 3, 0, jnp.where(codes < 5, 1, 2))
    second = jnp.where(codes == 0, 1, jnp.where((codes == 1) | (codes == 3), 2, 3))
    place = jnp.arange(4, dtype=jnp.int32).reshape(4, 1)
    keeper = (place == first[..., :, None, :]) | (place == second[..., :, None, :])
    shape = codes.shape[:-2] + (codes.shape[-2] * 4, codes.shape[-1])
    return keeper.reshape(shape).astype(jnp.float32)


def quantize(master, keeper, scale):
    inner = jnp.clip(master / scale, -1.0, 1.0) * keeper
    return inner.astype(jnp.bfloat16) * scale.astype(jnp.bfloat16)


def adam_update(master, first, second, grad):
    first = BETA_ONE * first + (1.0 - BETA_ONE) * grad
    second = BETA_TWO * second + (1.0 - BETA_TWO) * grad * grad
    update = first / CORRECT_ONE / (jnp.sqrt(second / CORRECT_TWO) + ADAM_EPS)
    return (master - LEARN_RATE * update, first, second)


def contract_rows(left, right):
    return lax.dot_general(
        left, right, (((0,), (0,)), ((), ())), preferred_element_type=jnp.float32
    )


def shards(
    tokens,
    cotangent,
    gu_master,
    gu_first,
    gu_second,
    gu_codes,
    gu_expo,
    down_master,
    down_first,
    down_second,
    down_codes,
    down_expo,
):
    gu_keep = expand_codes(gu_codes)
    gu_scale = power_of_two(gu_expo)[:, None, :]
    dn_keep = expand_codes(down_codes)
    dn_scale = power_of_two(down_expo)[None, :]
    gu_quant = quantize(gu_master, gu_keep, gu_scale)
    down_quant = quantize(down_master, dn_keep, dn_scale)
    whole = lax.all_gather(tokens, "tensor", axis=1, tiled=True)
    rows_here = whole.shape[0]
    both = jnp.einsum(
        "td,kdf->ktf",
        whole,
        lax.all_gather(gu_quant, "dp", axis=1, tiled=True),
        preferred_element_type=jnp.float32,
    )
    gate = both[0]
    up = both[1]
    sig = jax.nn.sigmoid(gate)
    act = gate * sig
    hidden_state = (act * up).astype(jnp.bfloat16)
    down_whole = lax.all_gather(down_quant, "dp", axis=1, tiled=True)
    partial_value = jnp.dot(hidden_state, down_whole, preferred_element_type=jnp.float32)
    mixed = lax.psum_scatter(
        partial_value.astype(jnp.bfloat16), "tensor", scatter_dimension=1, tiled=True
    )
    upstream = lax.all_gather(cotangent, "tensor", axis=1, tiled=True)
    dhid = jnp.dot(upstream, down_whole.T, preferred_element_type=jnp.float32)
    dgate = (dhid * up * sig * (1.0 + gate * (1.0 - sig))).astype(jnp.bfloat16)
    dup = (dhid * act).astype(jnp.bfloat16)
    piece = lax.all_gather(gu_quant, "dp", axis=1, tiled=True)
    input_part = jnp.dot(dgate, piece[0].T, preferred_element_type=jnp.float32) + jnp.dot(
        dup, piece[1].T, preferred_element_type=jnp.float32
    )
    token_grad = lax.psum_scatter(
        input_part.astype(jnp.bfloat16), "tensor", scatter_dimension=1, tiled=True
    )
    inverse_scale = 1.0 / (rows_here * lax.axis_size("dp"))

    def reduce_rows(left, right):
        return lax.psum_scatter(
            (contract_rows(left, right) * inverse_scale).astype(jnp.bfloat16),
            "dp",
            scatter_dimension=0,
            tiled=True,
        ).astype(jnp.float32)

    grad_gate = reduce_rows(whole, dgate)
    grad_up = reduce_rows(whole, dup)
    grad_down = reduce_rows(upstream, hidden_state).T
    gu_inside = (jnp.abs(gu_master / gu_scale) <= 1.0).astype(jnp.float32)
    dn_inside = (jnp.abs(down_master / dn_scale) <= 1.0).astype(jnp.float32)
    gu_grad = jnp.stack([grad_gate, grad_up]) * gu_keep * gu_inside
    dn_grad = grad_down * dn_keep * dn_inside
    gu_new, gu_first_new, gu_second_new = adam_update(gu_master, gu_first, gu_second, gu_grad)
    down_new, down_first_new, down_second_new = adam_update(
        down_master, down_first, down_second, dn_grad
    )
    gu_copy = quantize(gu_new, gu_keep, gu_scale)
    down_copy = quantize(down_new, dn_keep, dn_scale)
    return (
        mixed,
        token_grad,
        gu_new,
        gu_first_new,
        gu_second_new,
        gu_copy,
        down_new,
        down_first_new,
        down_second_new,
        down_copy,
    )


def solution(mesh):
    in_specs = (
        P("dp", "tensor"),
        P("dp", "tensor"),
        P(None, "dp", "tensor"),
        P(None, "dp", "tensor"),
        P(None, "dp", "tensor"),
        P(None, "dp", "tensor"),
        P(None, "tensor"),
        P("tensor", "dp"),
        P("tensor", "dp"),
        P("tensor", "dp"),
        P("tensor", "dp"),
        P("dp"),
    )
    out_specs = (
        P("dp", "tensor"),
        P("dp", "tensor"),
        P(None, "dp", "tensor"),
        P(None, "dp", "tensor"),
        P(None, "dp", "tensor"),
        P(None, "dp", "tensor"),
        P("tensor", "dp"),
        P("tensor", "dp"),
        P("tensor", "dp"),
        P("tensor", "dp"),
    )
    return jax.shard_map(shards, mesh=mesh, in_specs=in_specs, out_specs=out_specs, check_vma=False)
```

profile of v0, /device:TPU:2, one launch (start us, length us, event | category | flops | bytes accessed | tf_op | source)
XLA Modules:
  0.0 918.5 jit_solution(11346063206938686760)
XLA Ops:
  7.2 0.0 all-gather.7.cloned.1.call-start
  7.2 0.7 all-gather.7.cloned.1.call-update
  7.9 0.0 all-gather.5.cloned.1.call-start
  8.0 0.1 eq.199
  8.1 1.0 select_select_fusion.2
  9.1 0.2 copy.44
  9.3 0.2 copy.46
  9.5 0.3 eq.207
  9.8 0.8 copy.47
  10.6 0.3 eq.201
  10.9 0.8 copy.45
  11.7 1.6 copy.48
  13.3 1.2 fusion.15
  14.5 0.0 all-gather.5.cloned.1.call-update
  14.5 0.0 all-gather.11.cloned.1.call-start
  14.6 0.7 all-gather.11.cloned.1.call-update
  15.3 0.0 reduce-scatter.14.cloned.1.call-start
  15.3 61.4 %all-gather.7.cloned.1.call-done = bf16[256,4096]{1,0:T(8,128)(2,1)} async-done(((bf16[256,128]{1,0:T(8,128)(2,1)}), bf16[256,4096]{1,0:T(8,128)(2,1)}) %all-gather.7.cloned.1.call-update) | async-done | bytes 2097168 | tf_op jit(solution)/shard_map/all_gather | solution.py:68
  76.8 112.9 %all-gather.5.cloned.1.call-done = bf16[2,4096,256]{1,2,0:T(8,128)(2,1)} async-done(((bf16[2,512,256]{1,2,0:T(8,128)(2,1)}), bf16[2,4096,256]{1,2,0:T(8,128)(2,1)}) %all-gather.5.cloned.1.call-update) | async-done | bytes 4194320 | tf_op jit(solution)/shard_map/all_gather | solution.py:73
  189.7 4.1 fusion.10
  193.8 0.8 copy-done.8
  194.6 0.1 multiply_convert_fusion.2
  194.7 56.8 %all-gather.11.cloned.1.call-done = bf16[256,4096]{1,0:T(8,128)(2,1)} async-done(((bf16[256,128]{1,0:T(8,128)(2,1)}), bf16[256,4096]{1,0:T(8,128)(2,1)}) %all-gather.11.cloned.1.call-update) | async-done | bytes 2097168 | tf_op jit(solution)/shard_map/all_gather | solution.py:86
  251.5 3.7 fusion.4
  255.2 0.0 all-gather.9.cloned.1.call-start
  255.3 0.1 eq.227
  255.4 0.7 copy-done.9
  256.1 0.1 eq.229
  256.2 0.2 eq.230
  256.4 0.1 eq.235
  256.5 0.2 eq.236
  256.7 92.6 %reduce-scatter.14.cloned.1.call-done = bf16[512,256]{0,1:T(8,128)(2,1)} async-done(((bf16[4096,256]{0,1:T(8,128)(2,1)}), bf16[512,256]{0,1:T(8,128)(2,1)}) %reduce-scatter.14.cloned.1.call-update) | async-done | bytes 262160 | tf_op jit(solution)/shard_map/reduce_scatter | solution.py:100
  349.3 3.1 fusion.20
  352.4 0.8 fusion.18
  353.3 0.0 reduce-scatter.16.cloned.1.call-start
  353.3 72.3 %all-gather.9.cloned.1.call-done = bf16[256,4096]{1,0:T(8,128)(2,1)} async-done(((bf16[256,512]{1,0:T(8,128)(2,1)}), bf16[256,4096]{1,0:T(8,128)(2,1)}) %all-gather.9.cloned.1.call-update) | async-done | bytes 2097168 | tf_op jit(solution)/shard_map/all_gather | solution.py:81
  425.6 2.3 convolution_convert_fusion
  427.9 2.5 copy.56
  430.5 0.0 reduce-scatter.10.cloned.1.call-start
  430.6 3.2 multiply_convert_fusion
  433.8 0.6 copy-done.6
  434.4 2.1 fusion.6
  436.5 0.0 reduce-scatter.12.cloned.1.call-start
  436.6 2.1 fusion.5
  438.7 0.2 reduce-scatter.18.cloned.1.call-start
  438.9 0.6 copy-done.7
  439.6 2.5 fusion.7
  442.0 0.3 copy-done.1
  442.4 0.7 fusion
  443.1 2.5 copy.58
  445.6 1.2 copy-done.5
  446.8 0.3 copy.49
  447.2 1.6 copy.50
  448.8 125.3 %reduce-scatter.16.cloned.1.call-done = bf16[128,256]{1,0:T(8,128)(2,1)} async-done(((bf16[4096,256]{1,0:T(8,128)(2,1)}), bf16[128,256]{1,0:T(8,128)(2,1)}) %reduce-scatter.16.cloned.1.call-update) | async-done | bytes 65552
  574.0 1.6 copy.57
  575.6 93.8 %reduce-scatter.10.cloned.1.call-done = bf16[512,256]{0,1:T(8,128)(2,1)} async-done(((bf16[4096,256]{0,1:T(8,128)(2,1)}), bf16[512,256]{0,1:T(8,128)(2,1)}) %reduce-scatter.10.cloned.1.call-update) | async-done | bytes 262160 | tf_op jit(solution)/shard_map/reduce_scatter | solution.py:100
  669.4 95.8 %reduce-scatter.12.cloned.1.call-done = bf16[512,256]{0,1:T(8,128)(2,1)} async-done(((bf16[4096,256]{0,1:T(8,128)(2,1)}), bf16[512,256]{0,1:T(8,128)(2,1)}) %reduce-scatter.12.cloned.1.call-update) | async-done | bytes 262160 | tf_op jit(solution)/shard_map/reduce_scatter | solution.py:100
  765.1 4.1 fusion.17
  769.3 2.1 copy.55
  771.4 2.6 copy.52
  774.0 1.3 copy.53
  775.3 1.3 copy.54
  776.6 133.8 %reduce-scatter.18.cloned.1.call-done = bf16[128,256]{1,0:T(8,128)(2,1)} async-done(((bf16[4096,256]{1,0:T(8,128)(2,1)}), bf16[128,256]{1,0:T(8,128)(2,1)}) %reduce-scatter.18.cloned.1.call-update) | async-done | bytes 65552
  910.4 1.6 copy.59
  (29 shorter events, 0.2 us)
Async XLA Ops:
  7.2 69.6 %all-gather.7.cloned.1.call-start = ((), (), s32[]{:S(2)}) async-start(), calls=%async_computation.6 | async-start | bytes 2162688 | tf_op jit(solution)/shard_map/all_gather | solution.py:68
  7.9 181.8 %all-gather.5.cloned.1.call-start = ((), (), s32[]{:S(2)}) async-start(), calls=%async_computation.5 | async-start | bytes 4718592 | tf_op jit(solution)/shard_map/all_gather | solution.py:73
  10.9 2.4 copy-start.10
  14.5 237.0 %all-gather.11.cloned.1.call-start = ((), (), s32[]{:S(2)}) async-start(), calls=%async_computation.8 | async-start | bytes 2162688 | tf_op jit(solution)/shard_map/all_gather | solution.py:86
  15.3 334.0 %reduce-scatter.14.cloned.1.call-start = ((), (), s32[]{:S(2)}) async-start(), calls=%async_computation.11 | async-start | bytes 2359296 | tf_op jit(solution)/shard_map/reduce_scatter | solution.py:100
  193.8 0.8 copy-start.8
  255.2 0.9 copy-start.9
  255.2 1.5 copy-start.11
  255.2 94.1 %copy-start.4 = (f32[256,512]{1,0:T(8,128)S(1)}, f32[256,512]{1,0:T(8,128)}, u32[]{:S(2)}) copy-start(f32[256,512]{1,0:T(8,128)} %param.19) | copy-start | bytes 1572868
  255.2 170.4 %all-gather.9.cloned.1.call-start = ((), (), s32[]{:S(2)}) async-start(), calls=%async_computation.7 | async-start | bytes 2359296 | tf_op jit(solution)/shard_map/all_gather | solution.py:81
  353.3 220.7 %reduce-scatter.16.cloned.1.call-start = ((), (), s32[]{:S(2)}) async-start(), calls=%async_computation.12 | async-start | bytes 2162688
  430.5 3.9 copy-start
  430.5 238.9 %reduce-scatter.10.cloned.1.call-start = ((), (), s32[]{:S(2)}) async-start(), calls=%async_computation.9 | async-start | bytes 2359296 | tf_op jit(solution)/shard_map/reduce_scatter | solution.py:100
  433.7 0.7 copy-start.6
  436.5 328.6 %reduce-scatter.12.cloned.1.call-start = ((), (), s32[]{:S(2)}) async-start(), calls=%async_computation.10 | async-start | bytes 2359296 | tf_op jit(solution)/shard_map/reduce_scatter | solution.py:100
  438.7 0.9 copy-start.7
  438.7 471.7 %reduce-scatter.18.cloned.1.call-start = ((), (), s32[]{:S(2)}) async-start(), calls=%async_computation.13 | async-start | bytes 2162688
  439.6 2.8 copy-start.1
  445.6 1.2 copy-start.5
  769.3 4.8 copy-start.3
  771.4 3.9 copy-start.2
Sparse Core Ops, SparseCore 0:
  9.8 66.9 all-gather.6
  79.8 109.8 all-gather.4
  191.4 59.9 all-gather.10
  255.4 93.8 reduce-scatter.13
  353.4 72.1 all-gather.8
  430.6 143.3 reduce-scatter.15
  578.1 91.2 reduce-scatter.9
  674.0 91.1 reduce-scatter.11
  767.7 142.7 reduce-scatter.17
where the time goes:
time: 919 us
  waiting for transfers between devices  846 us (92%)
  local copies, waits for them, and re-layouts  26.7 us (3%)
  matrix products  20.7 us (2%)
  between operations  14.1 us (2%)
  other arithmetic  10.4 us (1%)
    reduce_scatter x3, waiting for transfers between devices, reduce_rows(): lax.psum_scatter((contract_rows(left, right) * inverse_scale).astype(jnp....  282 us
    unnamed x11, waiting for transfers between devices  261 us
    all_gather x1, waiting for transfers between devices, shards(): lax.all_gather(gu_quant, 'dp', axis=1, tiled=True)  113 us
    all_gather x1, waiting for transfers between devices, shards(): down_whole = lax.all_gather(down_quant, 'dp', axis=1, tiled=True)  72.3 us
    all_gather x1, waiting for transfers between devices, shards(): whole = lax.all_gather(tokens, 'tensor', axis=1, tiled=True)  61.4 us
    all_gather x1, waiting for transfers between devices, shards(): upstream = lax.all_gather(cotangent, 'tensor', axis=1, tiled=True)  56.8 us
    unnamed x35, local copies, waits for them, and re-layouts  23.3 us
  transfers between devices with their start and end apart: 9, of which 9 were waited for; matrix products, arithmetic and copies ran while one was open for 4% of the time, Pallas kernels for 0%

commit v1 on v0

v1 whole, which is shorter than its diff:
```python
import jax
import jax.numpy as jnp
from jax import lax
from jax.experimental import pallas as pl
from jax.experimental.pallas import tpu as pltpu
from jax.sharding import PartitionSpec as P

BETA_ONE = 0.9
BETA_TWO = 0.95
ADAM_EPS = 1e-08
LEARN_RATE = 0.002
CORRECT_ONE = 1.0 - 0.9**10
CORRECT_TWO = 1.0 - 0.95**10

ALL = ("dp", "tensor")
F32 = jnp.float32
BF16 = jnp.bfloat16
VMEM = pl.BlockSpec(memory_space=pltpu.VMEM)
SMEM = pl.BlockSpec(memory_space=pltpu.SMEM)
X_GROUPS = [[hi + 2 * x for x in range(4)] for hi in range(2)]
Y_OFFSETS = (0, 3, 1, 2)


def device_number(x, hi, lo, y, core):
    return (x * 2 + hi) * 32 + lo * 8 + y * 2 + core


def move(value, target):
    pairs = []
    for x in range(4):
        for hi in range(2):
            for lo in range(4):
                for y in range(4):
                    for core in range(2):
                        here = device_number(x, hi, lo, y, core)
                        pairs.append((here, device_number(*target(x, hi, lo, y, core))))
    return lax.ppermute(value, ALL, pairs)


def along_y(step):
    return lambda x, hi, lo, y, core: (x, hi, lo, (y + step) % 4, core)


def along_lo(step):
    return lambda x, hi, lo, y, core: (x, hi, (lo + step) % 4, y, core)


def other_hi(x, hi, lo, y, core):
    return (x, 1 - hi, lo, y, core)


def other_core(x, hi, lo, y, core):
    return (x, hi, lo, y, 1 - core)


def swap_hi_y(x, hi, lo, y, core):
    return (x, y >> 1, lo, hi * 2 + (y & 1), core)


def power_of_two(expo, sign):
    result = jnp.zeros(expo.shape, F32)
    for level in range(-8, 0):
        result = jnp.where(expo == level, jnp.float32(2.0 ** (sign * level)), result)
    return result


def expand_codes(codes):
    groups = codes.shape[0]
    rows = groups * 4
    spread = (
        (lax.broadcasted_iota(jnp.int32, (rows, groups), 0) >> 2)
        == lax.broadcasted_iota(jnp.int32, (rows, groups), 1)
    ).astype(F32).astype(BF16)
    code = jnp.dot(spread, codes.astype(F32).astype(BF16), preferred_element_type=F32)
    place = (lax.broadcasted_iota(jnp.int32, code.shape, 0) & 3).astype(F32)
    first = jnp.where(code < 2.5, 0.0, jnp.where(code < 4.5, 1.0, 2.0))
    second = jnp.where(
        code == 0.0, 1.0, jnp.where((code == 1.0) | (code == 3.0), 2.0, 3.0)
    )
    return ((place == first) | (place == second)).astype(F32)


def quantize(master, keeper, scale, inverse):
    inner = jnp.clip(master * inverse, -1.0, 1.0) * keeper
    return inner.astype(BF16) * scale.astype(BF16)


def quantize_kernel(gu_ref, gu_codes, gu_expo, dn_ref, dn_codes, dn_expo, out_ref):
    for part in range(2):
        expo = gu_expo[part : part + 1, :]
        out_ref[part] = quantize(
            gu_ref[part],
            expand_codes(gu_codes[part]),
            power_of_two(expo, 1),
            power_of_two(expo, -1),
        )
    expo = dn_expo[...]
    down = jnp.clip(dn_ref[...] * power_of_two(expo, -1), -1.0, 1.0) * expand_codes(dn_codes[...])
    down = down.astype(BF16) * power_of_two(expo, 1).astype(BF16)
    out_ref[2] = down.astype(F32).T.astype(BF16)


def adam(master, first, second, grad, codes, expo):
    keeper = expand_codes(codes)
    inverse = power_of_two(expo, -1)
    inside = (jnp.abs(master * inverse) <= 1.0).astype(F32)
    grad = grad * keeper * inside
    first = BETA_ONE * first + (1.0 - BETA_ONE) * grad
    second = BETA_TWO * second + (1.0 - BETA_TWO) * grad * grad
    update = first / CORRECT_ONE / (jnp.sqrt(second / CORRECT_TWO) + ADAM_EPS)
    master = master - LEARN_RATE * update
    return master, first, second, quantize(master, keeper, power_of_two(expo, 1), inverse)


def gu_adam_kernel(grad, master, first, second, codes, expo, new, new_first, new_second, copy):
    which = pl.program_id(0)
    chosen = jnp.where(which == 0, expo[0:1, :], expo[1:2, :])
    result = adam(
        master[0], first[0], second[0], grad[0].astype(F32), codes[0], chosen
    )
    new[0], new_first[0], new_second[0], copy[0] = result


def down_adam_kernel(grad, master, first, second, codes, expo, new, new_first, new_second, copy):
    result = adam(
        master[...], first[...], second[...], grad[0].astype(F32).T, codes[...], expo[...]
    )
    new[...], new_first[...], new_second[...], copy[...] = result


def gu_update(grads, master, first, second, codes, expo):
    parts, rows, cols = master.shape
    size = rows // 2
    block = pl.BlockSpec((1, size, cols), lambda i, j: (i, j, 0))
    narrow = pl.BlockSpec((1, size // 4, cols), lambda i, j: (i, j, 0))
    whole = pl.BlockSpec((parts, cols), lambda i, j: (0, 0))
    like = jax.ShapeDtypeStruct(master.shape, F32)
    return pl.pallas_call(
        gu_adam_kernel,
        grid=(parts, 2),
        in_specs=[block, block, block, block, narrow, whole],
        out_specs=[block] * 4,
        out_shape=[like, like, like, jax.ShapeDtypeStruct(master.shape, BF16)],
        name="gu_adam",
    )(grads, master, first, second, codes, expo)


def down_update(grads, master, first, second, codes, expo):
    rows, cols = master.shape
    size = rows // 2
    block = pl.BlockSpec((size, cols), lambda i: (i, 0))
    narrow = pl.BlockSpec((size // 4, cols), lambda i: (i, 0))
    whole = pl.BlockSpec((1, cols), lambda i: (0, 0))
    like = jax.ShapeDtypeStruct(master.shape, F32)
    return pl.pallas_call(
        down_adam_kernel,
        grid=(2,),
        in_specs=[
            pl.BlockSpec((1, cols, size), lambda i: (2, 0, i)),
            block,
            block,
            block,
            narrow,
            whole,
        ],
        out_specs=[block] * 4,
        out_shape=[like, like, like, jax.ShapeDtypeStruct(master.shape, BF16)],
        name="down_adam",
    )(grads, master, first, second, codes, expo)


def piece_rows(pieces, ring, lo_step, side):
    own, other = pieces
    if ring < 3:
        return jnp.concatenate([own[ring][lo_step, side], other[ring][lo_step, side]], axis=1)
    half, at = lo_step // 2, lo_step % 2
    return jnp.concatenate(
        [own[3 + half][at, side], other[3 + half][at, side]], axis=1
    )


def weight_rows(weights, block, which, low, core):
    start = pl.multiple_of(low * 256 + core * 128, 128)
    second = pl.multiple_of(low * 256 + (1 - core) * 128, 128)
    return jnp.concatenate(
        [weights[block, which, pl.ds(start, 128), :], weights[block, which, pl.ds(second, 128), :]],
        axis=0,
    )


def partial_kernel(mine, place, *refs):
    own, other, weights, out = refs[:5], refs[5:10], refs[10], refs[11]
    acc = refs[12]
    hi, lo, y, core = place[1], place[2], place[3], place[4]
    target = hi if mine else 1 - hi
    acc[...] = jnp.zeros_like(acc)
    for ring, offset in enumerate(Y_OFFSETS):
        from_y = (y + offset) & 3

        @pl.when((from_y >> 1) == target)
        def _():
            for lo_step in range(4):
                block = (lo - lo_step) & 3
                for which in range(3):
                    left = piece_rows((own, other), ring, lo_step, which // 2)
                    right = weight_rows(weights, block, which, from_y & 1, core)
                    acc[which] += jnp.dot(left, right, preferred_element_type=F32)

    out[...] = acc[...].astype(out.dtype)


def partial(mine, place, pieces, weights):
    return pl.pallas_call(
        lambda *refs: partial_kernel(mine, *refs),
        in_specs=[SMEM] + [VMEM] * 11,
        out_specs=VMEM,
        out_shape=jax.ShapeDtypeStruct((3, 256, 256), F32 if mine else BF16),
        scratch_shapes=[pltpu.VMEM((3, 256, 256), F32)],
        compiler_params=pltpu.CompilerParams(vmem_limit_bytes=40 * 2**20),
        name="partial_own" if mine else "partial_sent",
    )(place, *pieces, weights)


def gated_kernel(own, sent, out):
    gate = own[0] + sent[0].astype(F32)
    up = own[1] + sent[1].astype(F32)
    dh = own[2] + sent[2].astype(F32)
    sig = jax.nn.sigmoid(gate)
    act = gate * sig
    out[0] = (dh * up * sig * (1.0 + gate * (1.0 - sig))).astype(BF16)
    out[1] = (dh * act).astype(BF16)
    out[2] = (act * up).astype(BF16)


def gated(own, sent):
    return pl.pallas_call(
        gated_kernel,
        in_specs=[VMEM] * 2,
        out_specs=VMEM,
        out_shape=jax.ShapeDtypeStruct((3, 256, 256), BF16),
        name="gated",
    )(own, sent)


def cross(left, right, left_dim, right_dim):
    return lax.dot_general(
        left, right, (((left_dim,), (right_dim,)), ((), ())), preferred_element_type=F32
    )


def outputs_kernel(mine, place, rows_own, rows_other, weights, out):
    hi, lo, y, core = place[1], place[2], place[3], place[4]
    core = core if mine else 1 - core
    for ring in range(4):
        to_y = (y + ring) & 3
        start = pl.multiple_of((to_y & 1) * 256 + core * 128, 128)

        def fill(rows):
            for lo_step in range(4):
                block = (lo + lo_step) & 3
                parts = [weights[block, which, pl.ds(start, 128), :] for which in range(3)]
                out[ring, lo_step, 0] = cross(rows[2], parts[2], 1, 1).astype(out.dtype)
                out[ring, lo_step, 1] = (
                    cross(rows[0], parts[0], 1, 1) + cross(rows[1], parts[1], 1, 1)
                ).astype(out.dtype)

        @pl.when((to_y >> 1) == hi)
        def _():
            fill(rows_own)

        @pl.when((to_y >> 1) != hi)
        def _():
            fill(rows_other)


def outputs(mine, place, rows_own, rows_other, weights):
    return pl.pallas_call(
        lambda *refs: outputs_kernel(mine, *refs),
        in_specs=[SMEM] + [VMEM] * 3,
        out_specs=VMEM,
        out_shape=jax.ShapeDtypeStruct((4, 4, 2, 256, 128), BF16),
        compiler_params=pltpu.CompilerParams(vmem_limit_bytes=40 * 2**20),
        name="outputs_kept" if mine else "outputs_sent",
    )(place, rows_own, rows_other, weights)


def grads_kernel(inverse_scale, place, *refs):
    own, other, rows_own, rows_other, out, acc = refs[:5], refs[5:10], refs[10], refs[11], refs[12], refs[13]
    hi, lo, y, core = place[1], place[2], place[3], place[4]
    for ring, offset in enumerate(Y_OFFSETS):
        from_y = (y + offset) & 3
        low = from_y & 1

        def add(rows):
            for lo_step in range(4):
                block = (lo - lo_step) & 3
                for which in range(3):
                    left = piece_rows((own, other), ring, lo_step, which // 2)
                    term = cross(left, rows[which], 0, 0)
                    start = pl.multiple_of(low * 256 + core * 128, 128)
                    second = pl.multiple_of(low * 256 + (1 - core) * 128, 128)
                    acc[block, which, pl.ds(start, 128), :] += term[:128]
                    acc[block, which, pl.ds(second, 128), :] += term[128:]

        if ring == 0:
            acc[...] = jnp.zeros_like(acc)

        @pl.when((from_y >> 1) == hi)
        def _():
            add(rows_own)

        @pl.when((from_y >> 1) != hi)
        def _():
            add(rows_other)

    out[...] = (acc[...] * inverse_scale).astype(out.dtype)


def grads(inverse_scale, place, pieces, rows_own, rows_other):
    return pl.pallas_call(
        lambda *refs: grads_kernel(inverse_scale, *refs),
        in_specs=[SMEM] + [VMEM] * 12,
        out_specs=VMEM,
        out_shape=jax.ShapeDtypeStruct((4, 3, 512, 256), BF16),
        scratch_shapes=[pltpu.VMEM((4, 3, 512, 256), F32)],
        compiler_params=pltpu.CompilerParams(vmem_limit_bytes=48 * 2**20),
        name="grads",
    )(place, *pieces, rows_own, rows_other)


def gather_pieces(tokens, cotangent):
    start = move(jnp.stack([tokens, cotangent]), swap_hi_y)
    line = jnp.stack([start] + [move(start, along_lo(step)) for step in (1, 2, 3)])
    before = move(line, along_y(1))
    after = move(line, along_y(-1))
    far_low = move(before[:2], along_y(1))
    far_high = move(after[2:], along_y(-1))
    own = (line, before, after, far_low, far_high)
    return own + tuple(move(piece, other_core) for piece in own)


def scatter_outputs(kept, sent):
    f32 = lambda value: value.astype(F32)
    arrived = move(sent, other_core)
    total = (f32(kept) + f32(arrived)).astype(BF16)
    low = move(total[2, :2], along_y(1))
    high = move(total[2, 2:], along_y(-1))
    ahead = jnp.concatenate([(f32(total[1, :2]) + f32(low)).astype(BF16), total[1, 2:]])
    behind = jnp.concatenate([total[3, :2], (f32(total[3, 2:]) + f32(high)).astype(BF16)])
    from_before = move(ahead, along_y(1))
    from_after = move(behind, along_y(-1))
    line = f32(total[0]) + f32(from_before) + f32(from_after)
    leaving = line[1:].astype(BF16)
    result = line[0]
    for step in (1, 2, 3):
        result = result + f32(move(leaving[step - 1], along_lo(step)))
    return move(result.astype(BF16), swap_hi_y)


def shards(
    tokens,
    cotangent,
    gu_master,
    gu_first,
    gu_second,
    gu_codes,
    gu_expo,
    down_master,
    down_first,
    down_second,
    down_codes,
    down_expo,
):
    dp, tensor = lax.axis_index("dp"), lax.axis_index("tensor")
    place = jnp.stack([dp >> 1, dp & 1, tensor >> 3, (tensor >> 1) & 3, tensor & 1])
    down_expo = down_expo.reshape(1, -1)
    quant = pl.pallas_call(
        quantize_kernel,
        in_specs=[VMEM] * 6,
        out_specs=VMEM,
        out_shape=jax.ShapeDtypeStruct((3, 512, 256), BF16),
        name="quantize",
    )(gu_master, gu_codes, gu_expo, down_master, down_codes, down_expo)
    weights = lax.all_gather(
        quant.reshape(1536, 256), "dp", axis=0, tiled=True, axis_index_groups=X_GROUPS
    ).reshape(4, 3, 512, 256)
    pieces = gather_pieces(tokens, cotangent)
    sent = partial(False, place, pieces, weights)
    arrived = move(sent, other_hi)
    kept = partial(True, place, pieces, weights)
    rows_own = gated(kept, arrived)
    rows_other = move(rows_own, other_hi)
    out_sent = outputs(False, place, rows_own, rows_other, weights)
    out_kept = outputs(True, place, rows_own, rows_other, weights)
    inverse_scale = 1.0 / (tokens.shape[0] * lax.axis_size("dp"))
    grad = grads(inverse_scale, place, pieces, rows_own, rows_other)
    grad = lax.psum_scatter(
        grad.reshape(6144, 256), "dp", scatter_dimension=0, tiled=True, axis_index_groups=X_GROUPS
    ).reshape(3, 512, 256)
    both = scatter_outputs(out_kept, out_sent)
    gu_new, gu_first_new, gu_second_new, gu_copy = gu_update(
        grad, gu_master, gu_first, gu_second, gu_codes, gu_expo
    )
    down_new, down_first_new, down_second_new, down_copy = down_update(
        grad, down_master, down_first, down_second, down_codes, down_expo
    )
    return (
        both[0],
        both[1],
        gu_new,
        gu_first_new,
        gu_second_new,
        gu_copy,
        down_new,
        down_first_new,
        down_second_new,
        down_copy,
    )


def solution(mesh):
    in_specs = (
        P("dp", "tensor"),
        P("dp", "tensor"),
        P(None, "dp", "tensor"),
        P(None, "dp", "tensor"),
        P(None, "dp", "tensor"),
        P(None, "dp", "tensor"),
        P(None, "tensor"),
        P("tensor", "dp"),
        P("tensor", "dp"),
        P("tensor", "dp"),
        P("tensor", "dp"),
        P("dp"),
    )
    out_specs = (
        P("dp", "tensor"),
        P("dp", "tensor"),
        P(None, "dp", "tensor"),
        P(None, "dp", "tensor"),
        P(None, "dp", "tensor"),
        P(None, "dp", "tensor"),
        P("tensor", "dp"),
        P("tensor", "dp"),
        P("tensor", "dp"),
        P("tensor", "dp"),
    )
    return jax.shard_map(shards, mesh=mesh, in_specs=in_specs, out_specs=out_specs, check_vma=False)
```

time: 919 us -> 202 us (0.22)
  the two profiles are of different devices: /device:TPU:2 before, /device:TPU:224 now
where the time goes in v1:
time: 202 us; the launch traced here: 201 us
  waiting for transfers between devices  97.1 us (48%)
  starting transfers between devices  49 us (24%)
  Pallas kernels  31 us (15%)
  between operations  14.3 us (7%)
  local copies, waits for them, and re-layouts  8.46 us (4%)
    ppermute x24, waiting for transfers between devices, move(): return lax.ppermute(value, ALL, pairs)  97.1 us
    ppermute x24, starting transfers between devices, move(): return lax.ppermute(value, ALL, pairs)  48.9 us
    unnamed x22, local copies, waits for them, and re-layouts  7.58 us
    pallas_call x1, Pallas kernels, grads(): pl.pallas_call(lambda *refs: grads_kernel(inverse_scale, *refs), in_specs...  6.3 us
    pallas_call x2, Pallas kernels, outputs(): pl.pallas_call(lambda *refs: outputs_kernel(mine, *refs), in_specs=[SMEM]...  5.95 us
    pallas_call x1, Pallas kernels, gu_update(): pl.pallas_call(gu_adam_kernel, grid=(parts, 2), in_specs=[block, block, b...  5.25 us
    pallas_call x2, Pallas kernels, partial(): pl.pallas_call(lambda *refs: partial_kernel(mine, *refs), in_specs=[SMEM]...  4.72 us
  transfers between devices with their start and end apart: 26, of which 16 were waited for; matrix products, arithmetic and copies ran while one was open for 1% of the time, Pallas kernels for 4%

profile of v1, /device:TPU:224, one launch (start us, length us, event | category | flops | bytes accessed | tf_op | source)
XLA Modules:
  0.0 201.2 jit_solution(7423665758686905421)
XLA Ops:
  7.2 0.0 all-gather.2.cloned.1.call-start
  7.2 3.5 %quantize.1 = bf16[3,512,256]{2,1,0:T(8,128)(2,1)} custom-call(f32[2,512,256]{2,1,0:T(8,128)} %master.2, s32[2,128,256]{2,1,0:T(8,128)} %codes.2, s32[2,256]{1,0:T(2,128)} %expo.1, f32[256,512]{1,0:T(8,128)} %master.3, s32[64,512]{1,0:T(8,128)} %codes.3, s32[1,512]{1,0:T(1,128)} %bitcast.74), custom_call_target="tpu_custom_call" | custom-call | tf_op jit(solution)/shard_map/quantize/pallas_call | solution.py:377
  10.7 0.0 all-gather.2.cloned.1.call-update
  10.7 0.0 reduce-scatter.2.cloned.1.call-start
  10.8 6.0 %collective-permute-start = (bf16[2,256,128]{2,1,0:T(8,128)(2,1)S(1)}, bf16[2,256,128]{2,1,0:T(8,128)(2,1)S(1)}, u32[]{:S(2)}, u32[]{:S(2)}) collective-permute-start(bf16[2,256,128]{2,1,0:T(8,128)(2,1)S(1)} %pad_maximum_fusion.3), channel_id=1, source_target_pairs={{0,0},{1,1},{2,2},{3,3},{4,32},{5,33},{6,34},{7,35},{8,8},{9,9},{1... | collective-permute-start | bytes 393224 | tf_op jit(solution)/shard_map/ppermute | solution.py:37
  16.8 7.6 %collective-permute-done = bf16[2,256,128]{2,1,0:T(8,128)(2,1)S(1)} collective-permute-done((bf16[2,256,128]{2,1,0:T(8,128)(2,1)S(1)}, bf16[2,256,128]{2,1,0:T(8,128)(2,1)S(1)}, u32[]{:S(2)}, u32[]{:S(2)}) %collective-permute-start) | collective-permute-done | bytes 131104 | tf_op jit(solution)/shard_map/ppermute | solution.py:37
  24.4 3.8 %collective-permute-start.3 = (bf16[2,256,128]{2,1,0:T(8,128)(2,1)S(1)}, bf16[2,256,128]{2,1,0:T(8,128)(2,1)S(1)}, u32[]{:S(2)}, u32[]{:S(2)}) collective-permute-start(bf16[2,256,128]{2,1,0:T(8,128)(2,1)S(1)} %collective-permute-done), channel_id=1, source_target_pairs={{0,24},{1,25},{2,26},{3,27},{4,28},{5,29},{6,30},{7,31},{8,0},{9,1... | collective-permute-start | bytes 393224 | tf_op jit(solution)/shard_map/ppermute | solution.py:37
  28.2 1.0 collective-permute-start.2
  29.2 2.9 %collective-permute-start.1 = (bf16[2,256,128]{2,1,0:T(8,128)(2,1)S(1)}, bf16[2,256,128]{2,1,0:T(8,128)(2,1)S(1)}, u32[]{:S(2)}, u32[]{:S(2)}) collective-permute-start(bf16[2,256,128]{2,1,0:T(8,128)(2,1)S(1)} %collective-permute-done), channel_id=1, source_target_pairs={{0,8},{1,9},{2,10},{3,11},{4,12},{5,13},{6,14},{7,15},{8,16},{9,17... | collective-permute-start | bytes 393224 | tf_op jit(solution)/shard_map/ppermute | solution.py:37
  32.1 0.0 collective-permute-done.3
  32.1 4.7 %collective-permute-done.2 = bf16[2,256,128]{2,1,0:T(8,128)(2,1)S(1)} collective-permute-done((bf16[2,256,128]{2,1,0:T(8,128)(2,1)S(1)}, bf16[2,256,128]{2,1,0:T(8,128)(2,1)S(1)}, u32[]{:S(2)}, u32[]{:S(2)}) %collective-permute-start.2) | collective-permute-done | bytes 131104 | tf_op jit(solution)/shard_map/ppermute | solution.py:37
  36.9 0.1 pad_maximum_fusion.refs_1_
  36.9 0.1 collective-permute-start.5
  37.0 2.0 %collective-permute-start.4 = (bf16[4,2,256,128]{3,2,1,0:T(8,128)(2,1)S(1)}, bf16[4,2,256,128]{3,2,1,0:T(8,128)(2,1)S(1)}, u32[]{:S(2)}, u32[]{:S(2)}) collective-permute-start(bf16[4,2,256,128]{3,2,1,0:T(8,128)(2,1)S(1)} %pad_maximum_fusion.refs_1_), channel_id=1, source_target_pairs={{0,2},{1,3},{2,4},{3,5},{4,6},{5,7},{6,0},{7,1},{8,10},{9,11},{10,... | collective-permute-start | bytes 1572872 | tf_op jit(solution)/shard_map/ppermute | solution.py:37
  39.0 11.8 %collective-permute-done.5.refs_3_ = bf16[4,2,256,128]{3,2,1,0:T(8,128)(2,1)S(1)} collective-permute-done((bf16[4,2,256,128]{3,2,1,0:T(8,128)(2,1)S(1)}, bf16[4,2,256,128]{3,2,1,0:T(8,128)(2,1)S(1)}, u32[]{:S(2)}, u32[]{:S(2)}) %collective-permute-start.5) | collective-permute-done | bytes 524320 | tf_op jit(solution)/shard_map/ppermute | solution.py:37
  50.9 1.6 collective-permute-start.7
  52.5 0.6 collective-permute-start.6
  53.1 0.5 collective-permute-start.9
  53.6 4.8 %collective-permute-done.7.refs_5_ = bf16[2,2,256,128]{3,2,1,0:T(8,128)(2,1)S(1)} collective-permute-done((bf16[2,2,256,128]{3,2,1,0:T(8,128)(2,1)S(1)}, bf16[2,2,256,128]{3,2,1,0:T(8,128)(2,1)S(1)}, u32[]{:S(2)}, u32[]{:S(2)}) %collective-permute-start.7) | collective-permute-done | bytes 262176 | tf_op jit(solution)/shard_map/ppermute | solution.py:37
  58.4 2.9 %collective-permute-done.6.refs_4_ = bf16[2,2,256,128]{3,2,1,0:T(8,128)(2,1)} collective-permute-done((bf16[2,2,256,128]{3,2,1,0:T(8,128)(2,1)S(1)}, bf16[2,2,256,128]{3,2,1,0:T(8,128)(2,1)}, u32[]{:S(2)}, u32[]{:S(2)}) %collective-permute-start.6) | collective-permute-done | bytes 262176 | tf_op jit(solution)/shard_map/ppermute | solution.py:37
  61.4 0.1 stack.47.refs_0_
  61.5 1.8 collective-permute-done.11.refs_9_
  63.2 1.9 copy-done
  65.1 2.3 %partial_sent.1 = bf16[3,256,256]{2,1,0:T(8,128)(2,1)S(1)} custom-call(s32[5]{0:T(128)S(1)} %stack.47.refs_0_, bf16[4,2,256,128]{3,2,1,0:T(8,128)(2,1)S(1)} %pad_maximum_fusion.refs_1_, bf16[4,2,256,128]{3,2,1,0:T(8,128)(2,1)S(1)} %collective-permute-done.4.refs_2_, bf16[4,2,256,128]{3,2,1,0:T(8,128)(2,1)S(1)} %collective-permute-done.5.refs_3_, ...), custom_call_target="tpu_custom_call" | custom-call | tf_op jit(solution)/shard_map/partial_sent/pallas_call | solution.py:213
  67.5 3.7 %collective-permute-start.13 = (bf16[3,256,256]{2,1,0:T(8,128)(2,1)S(1)}, bf16[3,256,256]{2,1,0:T(8,128)(2,1)}, u32[]{:S(2)}, u32[]{:S(2)}) collective-permute-start(bf16[3,256,256]{2,1,0:T(8,128)(2,1)S(1)} %partial_sent.1), channel_id=1, source_target_pairs={{0,32},{1,33},{2,34},{3,35},{4,36},{5,37},{6,38},{7,39},{8,40},{9,... | collective-permute-start | bytes 1179656 | tf_op jit(solution)/shard_map/ppermute | solution.py:37
  71.2 2.4 %partial_own.1.own = f32[3,256,256]{2,1,0:T(8,128)S(1)} custom-call(s32[5]{0:T(128)S(1)} %stack.47.refs_0_, bf16[4,2,256,128]{3,2,1,0:T(8,128)(2,1)S(1)} %pad_maximum_fusion.refs_1_, bf16[4,2,256,128]{3,2,1,0:T(8,128)(2,1)S(1)} %collective-permute-done.4.refs_2_, bf16[4,2,256,128]{3,2,1,0:T(8,128)(2,1)S(1)} %collective-permute-done.5.refs_3_, ...), custom_call_target="tpu_custom_call" | custom-call | tf_op jit(solution)/shard_map/partial_own/pallas_call | solution.py:213
  73.6 0.9 copy-done.6
  74.4 11.5 %collective-permute-done.13.sent = bf16[3,256,256]{2,1,0:T(8,128)(2,1)} collective-permute-done((bf16[3,256,256]{2,1,0:T(8,128)(2,1)S(1)}, bf16[3,256,256]{2,1,0:T(8,128)(2,1)}, u32[]{:S(2)}, u32[]{:S(2)}) %collective-permute-start.13) | collective-permute-done | bytes 393248 | tf_op jit(solution)/shard_map/ppermute | solution.py:37
  86.0 2.2 %gated.1.refs_1_.refs_11_ = bf16[3,256,256]{2,1,0:T(8,128)(2,1)} custom-call(f32[3,256,256]{2,1,0:T(8,128)} %copy-done.6, bf16[3,256,256]{2,1,0:T(8,128)(2,1)} %collective-permute-done.13.sent), custom_call_target="tpu_custom_call" | custom-call | tf_op jit(solution)/shard_map/gated/pallas_call | solution.py:236
  88.1 4.7 %collective-permute-start.14 = (bf16[3,256,256]{2,1,0:T(8,128)(2,1)}, bf16[3,256,256]{2,1,0:T(8,128)(2,1)S(1)}, u32[]{:S(2)}, u32[]{:S(2)}) collective-permute-start(bf16[3,256,256]{2,1,0:T(8,128)(2,1)} %gated.1.refs_1_.refs_11_), channel_id=1, source_target_pairs={{0,32},{1,33},{2,34},{3,35},{4,36},{5,37},{6,38},{7,39},{8,40},{9,... | collective-permute-start | bytes 1179656 | tf_op jit(solution)/shard_map/ppermute | solution.py:37
  92.8 9.8 %collective-permute-done.14.refs_2_.refs_12_ = bf16[3,256,256]{2,1,0:T(8,128)(2,1)S(1)} collective-permute-done((bf16[3,256,256]{2,1,0:T(8,128)(2,1)}, bf16[3,256,256]{2,1,0:T(8,128)(2,1)S(1)}, u32[]{:S(2)}, u32[]{:S(2)}) %collective-permute-start.14) | collective-permute-done | bytes 393248 | tf_op jit(solution)/shard_map/ppermute | solution.py:37
  102.6 1.0 copy-done.2
  103.6 0.9 copy-done.8
  104.6 6.3 %grads.1 = bf16[4,3,512,256]{3,2,1,0:T(8,128)(2,1)} custom-call(s32[5]{0:T(128)S(1)} %stack.47.refs_0_, bf16[4,2,256,128]{3,2,1,0:T(8,128)(2,1)S(1)} %pad_maximum_fusion.refs_1_, bf16[4,2,256,128]{3,2,1,0:T(8,128)(2,1)S(1)} %collective-permute-done.4.refs_2_, bf16[4,2,256,128]{3,2,1,0:T(8,128)(2,1)S(1)} %collective-permute-done.5.refs_3_, ...), custom_call_target="tpu_custom_call" | custom-call | tf_op jit(solution)/shard_map/grads/pallas_call | solution.py:320
  110.9 0.0 reduce-scatter.2.cloned.1.call-update
  110.9 1.9 copy-done.1
  112.8 1.0 copy-done.5
  113.8 3.1 %outputs_sent.1 = bf16[4,4,2,256,128]{4,3,2,1,0:T(8,128)(2,1)S(1)} custom-call(s32[5]{0:T(128)S(1)} %stack.47.refs_0_, bf16[3,256,256]{2,1,0:T(8,128)(2,1)S(1)} %copy-done.3, bf16[3,256,256]{2,1,0:T(8,128)(2,1)S(1)} %copy-done.5, bf16[4,3,512,256]{3,2,1,0:T(8,128)(2,1)S(1)} %bitcast.62), custom_call_target="tpu_custom_call" | custom-call | tf_op jit(solution)/shard_map/outputs_sent/pallas_call | solution.py:277
  116.9 0.1 collective-permute-start.15
  117.0 2.9 %outputs_kept.1 = bf16[4,4,2,256,128]{4,3,2,1,0:T(8,128)(2,1)S(1)} custom-call(s32[5]{0:T(128)S(1)} %stack.47.refs_0_, bf16[3,256,256]{2,1,0:T(8,128)(2,1)S(1)} %copy-done.3, bf16[3,256,256]{2,1,0:T(8,128)(2,1)S(1)} %copy-done.5, bf16[4,3,512,256]{3,2,1,0:T(8,128)(2,1)S(1)} %bitcast.63), custom_call_target="tpu_custom_call" | custom-call | tf_op jit(solution)/shard_map/outputs_kept/pallas_call | solution.py:277
  119.8 1.3 collective-permute-done.15
  121.1 0.7 add_convert_fusion
  121.8 0.1 slice_bitcast_fusion.6
  121.9 0.1 collective-permute-start.16
  122.0 3.2 %collective-permute-start.18 = (bf16[2,2,256,128]{3,2,1,0:T(8,128)(2,1)S(1)}, bf16[2,2,256,128]{3,2,1,0:T(8,128)(2,1)S(1)}, u32[]{:S(2)}, u32[]{:S(2)}) collective-permute-start(bf16[2,2,256,128]{3,2,1,0:T(8,128)(2,1)S(1)} %get-tuple-element.31), channel_id=1, source_target_pairs={{0,6},{1,7},{2,0},{3,1},{4,2},{5,3},{6,4},{7,5},{8,14},{9,15},{10,... | collective-permute-start | bytes 786440 | tf_op jit(solution)/shard_map/ppermute | solution.py:37
  125.2 6.3 %collective-permute-done.16 = bf16[2,2,256,128]{3,2,1,0:T(8,128)(2,1)S(1)} collective-permute-done((bf16[2,2,256,128]{3,2,1,0:T(8,128)(2,1)S(1)}, bf16[2,2,256,128]{3,2,1,0:T(8,128)(2,1)S(1)}, u32[]{:S(2)}, u32[]{:S(2)}) %collective-permute-start.16) | collective-permute-done | bytes 262176 | tf_op jit(solution)/shard_map/ppermute | solution.py:37
  131.6 0.1 fusion.2
  131.8 3.0 %collective-permute-start.19 = (bf16[4,2,256,128]{3,2,1,0:T(8,128)(2,1)S(1)}, bf16[4,2,256,128]{3,2,1,0:T(8,128)(2,1)S(1)}, u32[]{:S(2)}, u32[]{:S(2)}) collective-permute-start(bf16[4,2,256,128]{3,2,1,0:T(8,128)(2,1)S(1)} %pad_maximum_fusion.2), channel_id=1, source_target_pairs={{0,6},{1,7},{2,0},{3,1},{4,2},{5,3},{6,4},{7,5},{8,14},{9,15},{10,... | collective-permute-start | bytes 1572872 | tf_op jit(solution)/shard_map/ppermute | solution.py:37
  134.8 0.1 collective-permute-start.17
  134.9 10.2 %collective-permute-done.19 = bf16[4,2,256,128]{3,2,1,0:T(8,128)(2,1)S(1)} collective-permute-done((bf16[4,2,256,128]{3,2,1,0:T(8,128)(2,1)S(1)}, bf16[4,2,256,128]{3,2,1,0:T(8,128)(2,1)S(1)}, u32[]{:S(2)}, u32[]{:S(2)}) %collective-permute-start.19) | collective-permute-done | bytes 524320 | tf_op jit(solution)/shard_map/ppermute | solution.py:37
  145.1 3.5 %collective-permute-done.17 = bf16[4,2,256,128]{3,2,1,0:T(8,128)(2,1)S(1)} collective-permute-done((bf16[4,2,256,128]{3,2,1,0:T(8,128)(2,1)S(1)}, bf16[4,2,256,128]{3,2,1,0:T(8,128)(2,1)S(1)}, u32[]{:S(2)}, u32[]{:S(2)}) %collective-permute-start.17) | collective-permute-done | bytes 524320 | tf_op jit(solution)/shard_map/ppermute | solution.py:37
  148.7 0.2 fusion.7
  148.9 3.3 %collective-permute-start.20 = (bf16[2,256,128]{2,1,0:T(8,128)(2,1)S(1)}, bf16[2,256,128]{2,1,0:T(8,128)(2,1)S(1)}, u32[]{:S(2)}, u32[]{:S(2)}) collective-permute-start(bf16[2,256,128]{2,1,0:T(8,128)(2,1)S(1)} %get-tuple-element.34), channel_id=1, source_target_pairs={{0,8},{1,9},{2,10},{3,11},{4,12},{5,13},{6,14},{7,15},{8,16},{9,17... | collective-permute-start | bytes 393224 | tf_op jit(solution)/shard_map/ppermute | solution.py:37
  152.2 8.5 %collective-permute-start.22 = (bf16[2,256,128]{2,1,0:T(8,128)(2,1)S(1)}, bf16[2,256,128]{2,1,0:T(8,128)(2,1)S(1)}, u32[]{:S(2)}, u32[]{:S(2)}) collective-permute-start(bf16[2,256,128]{2,1,0:T(8,128)(2,1)S(1)} %get-tuple-element.35), channel_id=1, source_target_pairs={{0,24},{1,25},{2,26},{3,27},{4,28},{5,29},{6,30},{7,31},{8,0},{9,1... | collective-permute-start | bytes 393224 | tf_op jit(solution)/shard_map/ppermute | solution.py:37
  160.8 1.4 collective-permute-start.21
  162.1 2.0 %collective-permute-done.20 = bf16[2,256,128]{2,1,0:T(8,128)(2,1)S(1)} collective-permute-done((bf16[2,256,128]{2,1,0:T(8,128)(2,1)S(1)}, bf16[2,256,128]{2,1,0:T(8,128)(2,1)S(1)}, u32[]{:S(2)}, u32[]{:S(2)}) %collective-permute-start.20) | collective-permute-done | bytes 131104 | tf_op jit(solution)/shard_map/ppermute | solution.py:37
  164.2 2.9 %collective-permute-done.22 = bf16[2,256,128]{2,1,0:T(8,128)(2,1)S(1)} collective-permute-done((bf16[2,256,128]{2,1,0:T(8,128)(2,1)S(1)}, bf16[2,256,128]{2,1,0:T(8,128)(2,1)S(1)}, u32[]{:S(2)}, u32[]{:S(2)}) %collective-permute-start.22) | collective-permute-done | bytes 131104 | tf_op jit(solution)/shard_map/ppermute | solution.py:37
  167.0 5.0 %collective-permute-done.21 = bf16[2,256,128]{2,1,0:T(8,128)(2,1)S(1)} collective-permute-done((bf16[2,256,128]{2,1,0:T(8,128)(2,1)S(1)}, bf16[2,256,128]{2,1,0:T(8,128)(2,1)S(1)}, u32[]{:S(2)}, u32[]{:S(2)}) %collective-permute-start.21) | collective-permute-done | bytes 131104 | tf_op jit(solution)/shard_map/ppermute | solution.py:37
  172.0 0.1 fusion.6
  172.1 2.3 %collective-permute-start.23 = (bf16[2,256,128]{2,1,0:T(8,128)(2,1)S(1)}, bf16[2,256,128]{2,1,0:T(8,128)(2,1)S(1)}, u32[]{:S(2)}, u32[]{:S(2)}) collective-permute-start(bf16[2,256,128]{2,1,0:T(8,128)(2,1)S(1)} %fusion.6), channel_id=1, source_target_pairs={{0,0},{1,1},{2,2},{3,3},{4,32},{5,33},{6,34},{7,35},{8,8},{9,9},{1... | collective-permute-start | bytes 393224 | tf_op jit(solution)/shard_map/ppermute | solution.py:37
  174.4 10.8 %collective-permute-done.23 = bf16[2,256,128]{2,1,0:T(8,128)(2,1)S(1)} collective-permute-done((bf16[2,256,128]{2,1,0:T(8,128)(2,1)S(1)}, bf16[2,256,128]{2,1,0:T(8,128)(2,1)S(1)}, u32[]{:S(2)}, u32[]{:S(2)}) %collective-permute-start.23) | collective-permute-done | bytes 131104 | tf_op jit(solution)/shard_map/ppermute | solution.py:37
  185.3 0.7 slice_bitcast_fusion.11
  185.9 3.2 %down_adam.1 = (f32[256,512]{1,0:T(8,128)}, f32[256,512]{1,0:T(8,128)}, f32[256,512]{1,0:T(8,128)}, bf16[256,512]{1,0:T(8,128)(2,1)}) custom-call(bf16[3,512,256]{2,1,0:T(8,128)(2,1)} %bitcast.66, f32[256,512]{1,0:T(8,128)} %master.3, f32[256,512]{1,0:T(8,128)} %first.3, f32[256,512]{1,0:T(8,128)} %second.3, s32[64,512]{1,0:T(8,128)} %codes.3, s32[1,512]{1,0:T(1,128)} %bitcast.75), custom_call_target="tpu_custom_call" | custom-call | tf_op jit(solution)/shard_map/down_adam/pallas_call | solution.py:155
  189.1 5.2 %gu_adam.1 = (f32[2,512,256]{2,1,0:T(8,128)}, f32[2,512,256]{2,1,0:T(8,128)}, f32[2,512,256]{2,1,0:T(8,128)}, bf16[2,512,256]{2,1,0:T(8,128)(2,1)}) custom-call(bf16[3,512,256]{2,1,0:T(8,128)(2,1)} %bitcast.67, f32[2,512,256]{2,1,0:T(8,128)} %master.2, f32[2,512,256]{2,1,0:T(8,128)} %first.2, f32[2,512,256]{2,1,0:T(8,128)} %second.2, s32[2,128,256]{2,1,0:T(8,128)} %codes.2, ...), custom_call_target="tpu_custom_call" | custom-call | tf_op jit(solution)/shard_map/gu_adam/pallas_call | solution.py:138
  (35 shorter events, 0.2 us)
Async XLA Ops:
  7.2 3.6 %copy-start.9 = (bf16[256,128]{1,0:T(8,128)(2,1)S(1)}, bf16[256,128]{1,0:T(8,128)(2,1)}, u32[]{:S(2)}) copy-start(bf16[256,128]{1,0:T(8,128)(2,1)} %param.13) | copy-start | bytes 196612
  7.2 3.6 %copy-start.10 = (bf16[256,128]{1,0:T(8,128)(2,1)S(1)}, bf16[256,128]{1,0:T(8,128)(2,1)}, u32[]{:S(2)}) copy-start(bf16[256,128]{1,0:T(8,128)(2,1)} %param.12) | copy-start | bytes 196612
  7.2 56.0 %all-gather.2.cloned.1.call-start = ((), (), s32[]{:S(2)}) async-start(), calls=%async_computation.1 | async-start | bytes 3932160 | tf_op jit(solution)/shard_map/all_gather | solution.py:384
  10.7 175.2 %reduce-scatter.2.cloned.1.call-start = ((), (), s32[]{:S(2)}) async-start(), calls=%async_computation.2 | async-start | bytes 3932160 | tf_op jit(solution)/shard_map/reduce_scatter | solution.py:397
  10.8 13.5 %collective-permute-start = (bf16[2,256,128]{2,1,0:T(8,128)(2,1)S(1)}, bf16[2,256,128]{2,1,0:T(8,128)(2,1)S(1)}, u32[]{:S(2)}, u32[]{:S(2)}) collective-permute-start(bf16[2,256,128]{2,1,0:T(8,128)(2,1)S(1)} %pad_maximum_fusion.3), channel_id=1, source_target_pairs={{0,0},{1,1},{2,2},{3,3},{4,32},{5,33},{6,34},{7,35},{8,8},{9,9},{1... | collective-permute-start | bytes 393224 | tf_op jit(solution)/shard_map/ppermute | solution.py:37
  24.4 7.8 %collective-permute-start.3 = (bf16[2,256,128]{2,1,0:T(8,128)(2,1)S(1)}, bf16[2,256,128]{2,1,0:T(8,128)(2,1)S(1)}, u32[]{:S(2)}, u32[]{:S(2)}) collective-permute-start(bf16[2,256,128]{2,1,0:T(8,128)(2,1)S(1)} %collective-permute-done), channel_id=1, source_target_pairs={{0,24},{1,25},{2,26},{3,27},{4,28},{5,29},{6,30},{7,31},{8,0},{9,1... | collective-permute-start | bytes 393224 | tf_op jit(solution)/shard_map/ppermute | solution.py:37
  28.2 8.7 %collective-permute-start.2 = (bf16[2,256,128]{2,1,0:T(8,128)(2,1)S(1)}, bf16[2,256,128]{2,1,0:T(8,128)(2,1)S(1)}, u32[]{:S(2)}, u32[]{:S(2)}) collective-permute-start(bf16[2,256,128]{2,1,0:T(8,128)(2,1)S(1)} %collective-permute-done), channel_id=1, source_target_pairs={{0,16},{1,17},{2,18},{3,19},{4,20},{5,21},{6,22},{7,23},{8,24},{9,... | collective-permute-start | bytes 393224 | tf_op jit(solution)/shard_map/ppermute | solution.py:37
  29.2 7.7 %collective-permute-start.1 = (bf16[2,256,128]{2,1,0:T(8,128)(2,1)S(1)}, bf16[2,256,128]{2,1,0:T(8,128)(2,1)S(1)}, u32[]{:S(2)}, u32[]{:S(2)}) collective-permute-start(bf16[2,256,128]{2,1,0:T(8,128)(2,1)S(1)} %collective-permute-done), channel_id=1, source_target_pairs={{0,8},{1,9},{2,10},{3,11},{4,12},{5,13},{6,14},{7,15},{8,16},{9,17... | collective-permute-start | bytes 393224 | tf_op jit(solution)/shard_map/ppermute | solution.py:37
  36.9 13.9 %collective-permute-start.5 = (bf16[4,2,256,128]{3,2,1,0:T(8,128)(2,1)S(1)}, bf16[4,2,256,128]{3,2,1,0:T(8,128)(2,1)S(1)}, u32[]{:S(2)}, u32[]{:S(2)}) collective-permute-start(bf16[4,2,256,128]{3,2,1,0:T(8,128)(2,1)S(1)} %pad_maximum_fusion.refs_1_), channel_id=1, source_target_pairs={{0,6},{1,7},{2,0},{3,1},{4,2},{5,3},{6,4},{7,5},{8,14},{9,15},{10,... | collective-permute-start | bytes 1572872 | tf_op jit(solution)/shard_map/ppermute | solution.py:37
  37.0 15.4 %collective-permute-start.4 = (bf16[4,2,256,128]{3,2,1,0:T(8,128)(2,1)S(1)}, bf16[4,2,256,128]{3,2,1,0:T(8,128)(2,1)S(1)}, u32[]{:S(2)}, u32[]{:S(2)}) collective-permute-start(bf16[4,2,256,128]{3,2,1,0:T(8,128)(2,1)S(1)} %pad_maximum_fusion.refs_1_), channel_id=1, source_target_pairs={{0,2},{1,3},{2,4},{3,5},{4,6},{5,7},{6,0},{7,1},{8,10},{9,11},{10,... | collective-permute-start | bytes 1572872 | tf_op jit(solution)/shard_map/ppermute | solution.py:37
  39.0 22.4 %collective-permute-start.8 = (bf16[4,2,256,128]{3,2,1,0:T(8,128)(2,1)S(1)}, bf16[4,2,256,128]{3,2,1,0:T(8,128)(2,1)S(1)}, u32[]{:S(2)}, u32[]{:S(2)}) collective-permute-start(bf16[4,2,256,128]{3,2,1,0:T(8,128)(2,1)S(1)} %pad_maximum_fusion.refs_1_), channel_id=1, source_target_pairs={{0,1},{1,0},{2,3},{3,2},{4,5},{5,4},{6,7},{7,6},{8,9},{9,8},{10,11... | collective-permute-start | bytes 1572872 | tf_op jit(solution)/shard_map/ppermute | solution.py:37
  50.9 7.5 %collective-permute-start.7 = (bf16[2,2,256,128]{3,2,1,0:T(8,128)(2,1)S(1)}, bf16[2,2,256,128]{3,2,1,0:T(8,128)(2,1)S(1)}, u32[]{:S(2)}, u32[]{:S(2)}) collective-permute-start(bf16[2,2,256,128]{3,2,1,0:T(8,128)(2,1)S(1)} %slice.66), channel_id=1, source_target_pairs={{0,6},{1,7},{2,0},{3,1},{4,2},{5,3},{6,4},{7,5},{8,14},{9,15},{10,... | collective-permute-start | bytes 786440 | tf_op jit(solution)/shard_map/ppermute | solution.py:37
  52.5 8.9 %collective-permute-start.6 = (bf16[2,2,256,128]{3,2,1,0:T(8,128)(2,1)S(1)}, bf16[2,2,256,128]{3,2,1,0:T(8,128)(2,1)}, u32[]{:S(2)}, u32[]{:S(2)}) collective-permute-start(bf16[2,2,256,128]{3,2,1,0:T(8,128)(2,1)S(1)} %slice.65), channel_id=1, source_target_pairs={{0,2},{1,3},{2,4},{3,5},{4,6},{5,7},{6,0},{7,1},{8,10},{9,11},{10,... | collective-permute-start | bytes 786440 | tf_op jit(solution)/shard_map/ppermute | solution.py:37
  53.1 8.4 %collective-permute-start.10 = (bf16[4,2,256,128]{3,2,1,0:T(8,128)(2,1)S(1)}, bf16[4,2,256,128]{3,2,1,0:T(8,128)(2,1)S(1)}, u32[]{:S(2)}, u32[]{:S(2)}) collective-permute-start(bf16[4,2,256,128]{3,2,1,0:T(8,128)(2,1)S(1)} %collective-permute-done.5.refs_3_), channel_id=1, source_target_pairs={{0,1},{1,0},{2,3},{3,2},{4,5},{5,4},{6,7},{7,6},{8,9},{9,8},{10,11... | collective-permute-start | bytes 1572872 | tf_op jit(solution)/shard_map/ppermute | solution.py:37
  53.1 10.2 %collective-permute-start.9 = (bf16[4,2,256,128]{3,2,1,0:T(8,128)(2,1)S(1)}, bf16[4,2,256,128]{3,2,1,0:T(8,128)(2,1)S(1)}, u32[]{:S(2)}, u32[]{:S(2)}) collective-permute-start(bf16[4,2,256,128]{3,2,1,0:T(8,128)(2,1)S(1)} %collective-permute-done.4.refs_2_), channel_id=1, source_target_pairs={{0,1},{1,0},{2,3},{3,2},{4,5},{5,4},{6,7},{7,6},{8,9},{9,8},{10,11... | collective-permute-start | bytes 1572872 | tf_op jit(solution)/shard_map/ppermute | solution.py:37
  58.4 12.8 %copy-start.7 = (bf16[2,2,256,128]{3,2,1,0:T(8,128)(2,1)}, bf16[2,2,256,128]{3,2,1,0:T(8,128)(2,1)S(1)}, u32[]{:S(2)}) copy-start(bf16[2,2,256,128]{3,2,1,0:T(8,128)(2,1)S(1)} %collective-permute-done.7.refs_5_) | copy-start | bytes 786436
  58.4 3.0 %collective-permute-start.12 = (bf16[2,2,256,128]{3,2,1,0:T(8,128)(2,1)S(1)}, bf16[2,2,256,128]{3,2,1,0:T(8,128)(2,1)}, u32[]{:S(2)}, u32[]{:S(2)}) collective-permute-start(bf16[2,2,256,128]{3,2,1,0:T(8,128)(2,1)S(1)} %collective-permute-done.7.refs_5_), channel_id=1, source_target_pairs={{0,1},{1,0},{2,3},{3,2},{4,5},{5,4},{6,7},{7,6},{8,9},{9,8},{10,11... | collective-permute-start | bytes 786440 | tf_op jit(solution)/shard_map/ppermute | solution.py:37
  61.4 1.9 collective-permute-start.11
  63.2 1.9 copy-start
  67.5 18.5 %collective-permute-start.13 = (bf16[3,256,256]{2,1,0:T(8,128)(2,1)S(1)}, bf16[3,256,256]{2,1,0:T(8,128)(2,1)}, u32[]{:S(2)}, u32[]{:S(2)}) collective-permute-start(bf16[3,256,256]{2,1,0:T(8,128)(2,1)S(1)} %partial_sent.1), channel_id=1, source_target_pairs={{0,32},{1,33},{2,34},{3,35},{4,36},{5,37},{6,38},{7,39},{8,40},{9,... | collective-permute-start | bytes 1179656 | tf_op jit(solution)/shard_map/ppermute | solution.py:37
  73.6 0.9 copy-start.6
  88.1 14.5 %collective-permute-start.14 = (bf16[3,256,256]{2,1,0:T(8,128)(2,1)}, bf16[3,256,256]{2,1,0:T(8,128)(2,1)S(1)}, u32[]{:S(2)}, u32[]{:S(2)}) collective-permute-start(bf16[3,256,256]{2,1,0:T(8,128)(2,1)} %gated.1.refs_1_.refs_11_), channel_id=1, source_target_pairs={{0,32},{1,33},{2,34},{3,35},{4,36},{5,37},{6,38},{7,39},{8,40},{9,... | collective-permute-start | bytes 1179656 | tf_op jit(solution)/shard_map/ppermute | solution.py:37
  102.6 1.0 copy-start.2
  103.6 0.9 copy-start.8
  104.6 6.3 %copy-start.4 = (bf16[3,256,256]{2,1,0:T(8,128)(2,1)}, bf16[3,256,256]{2,1,0:T(8,128)(2,1)S(1)}, u32[]{:S(2)}) copy-start(bf16[3,256,256]{2,1,0:T(8,128)(2,1)S(1)} %collective-permute-done.14.refs_2_.refs_12_) | copy-start | bytes 1179652
  104.6 6.3 %copy-start.3 = (bf16[3,256,256]{2,1,0:T(8,128)(2,1)S(1)}, bf16[3,256,256]{2,1,0:T(8,128)(2,1)}, u32[]{:S(2)}) copy-start(bf16[3,256,256]{2,1,0:T(8,128)(2,1)} %gated.1.refs_1_.refs_11_) | copy-start | bytes 1179652
  110.9 1.9 copy-start.1
  112.8 1.0 copy-start.5
  116.9 4.2 %collective-permute-start.15 = (bf16[4,4,2,256,128]{4,3,2,1,0:T(8,128)(2,1)S(1)}, bf16[4,4,2,256,128]{4,3,2,1,0:T(8,128)(2,1)S(1)}, u32[]{:S(2)}, u32[]{:S(2)}) collective-permute-start(bf16[4,4,2,256,128]{4,3,2,1,0:T(8,128)(2,1)S(1)} %outputs_sent.1), channel_id=1, source_target_pairs={{0,1},{1,0},{2,3},{3,2},{4,5},{5,4},{6,7},{7,6},{8,9},{9,8},{10,11... | collective-permute-start | bytes 6291464 | tf_op jit(solution)/shard_map/ppermute | solution.py:37
  121.9 9.6 %collective-permute-start.16 = (bf16[2,2,256,128]{3,2,1,0:T(8,128)(2,1)S(1)}, bf16[2,2,256,128]{3,2,1,0:T(8,128)(2,1)S(1)}, u32[]{:S(2)}, u32[]{:S(2)}) collective-permute-start(bf16[2,2,256,128]{3,2,1,0:T(8,128)(2,1)S(1)} %get-tuple-element.30), channel_id=1, source_target_pairs={{0,2},{1,3},{2,4},{3,5},{4,6},{5,7},{6,0},{7,1},{8,10},{9,11},{10,... | collective-permute-start | bytes 786440 | tf_op jit(solution)/shard_map/ppermute | solution.py:37
  122.0 9.5 %collective-permute-start.18 = (bf16[2,2,256,128]{3,2,1,0:T(8,128)(2,1)S(1)}, bf16[2,2,256,128]{3,2,1,0:T(8,128)(2,1)S(1)}, u32[]{:S(2)}, u32[]{:S(2)}) collective-permute-start(bf16[2,2,256,128]{3,2,1,0:T(8,128)(2,1)S(1)} %get-tuple-element.31), channel_id=1, source_target_pairs={{0,6},{1,7},{2,0},{3,1},{4,2},{5,3},{6,4},{7,5},{8,14},{9,15},{10,... | collective-permute-start | bytes 786440 | tf_op jit(solution)/shard_map/ppermute | solution.py:37
  131.8 13.4 %collective-permute-start.19 = (bf16[4,2,256,128]{3,2,1,0:T(8,128)(2,1)S(1)}, bf16[4,2,256,128]{3,2,1,0:T(8,128)(2,1)S(1)}, u32[]{:S(2)}, u32[]{:S(2)}) collective-permute-start(bf16[4,2,256,128]{3,2,1,0:T(8,128)(2,1)S(1)} %pad_maximum_fusion.2), channel_id=1, source_target_pairs={{0,6},{1,7},{2,0},{3,1},{4,2},{5,3},{6,4},{7,5},{8,14},{9,15},{10,... | collective-permute-start | bytes 1572872 | tf_op jit(solution)/shard_map/ppermute | solution.py:37
  134.8 13.8 %collective-permute-start.17 = (bf16[4,2,256,128]{3,2,1,0:T(8,128)(2,1)S(1)}, bf16[4,2,256,128]{3,2,1,0:T(8,128)(2,1)S(1)}, u32[]{:S(2)}, u32[]{:S(2)}) collective-permute-start(bf16[4,2,256,128]{3,2,1,0:T(8,128)(2,1)S(1)} %pad_maximum_fusion.1), channel_id=1, source_target_pairs={{0,2},{1,3},{2,4},{3,5},{4,6},{5,7},{6,0},{7,1},{8,10},{9,11},{10,... | collective-permute-start | bytes 1572872 | tf_op jit(solution)/shard_map/ppermute | solution.py:37
  148.9 15.2 %collective-permute-start.20 = (bf16[2,256,128]{2,1,0:T(8,128)(2,1)S(1)}, bf16[2,256,128]{2,1,0:T(8,128)(2,1)S(1)}, u32[]{:S(2)}, u32[]{:S(2)}) collective-permute-start(bf16[2,256,128]{2,1,0:T(8,128)(2,1)S(1)} %get-tuple-element.34), channel_id=1, source_target_pairs={{0,8},{1,9},{2,10},{3,11},{4,12},{5,13},{6,14},{7,15},{8,16},{9,17... | collective-permute-start | bytes 393224 | tf_op jit(solution)/shard_map/ppermute | solution.py:37
  152.2 14.8 %collective-permute-start.22 = (bf16[2,256,128]{2,1,0:T(8,128)(2,1)S(1)}, bf16[2,256,128]{2,1,0:T(8,128)(2,1)S(1)}, u32[]{:S(2)}, u32[]{:S(2)}) collective-permute-start(bf16[2,256,128]{2,1,0:T(8,128)(2,1)S(1)} %get-tuple-element.35), channel_id=1, source_target_pairs={{0,24},{1,25},{2,26},{3,27},{4,28},{5,29},{6,30},{7,31},{8,0},{9,1... | collective-permute-start | bytes 393224 | tf_op jit(solution)/shard_map/ppermute | solution.py:37
  160.8 11.3 %collective-permute-start.21 = (bf16[2,256,128]{2,1,0:T(8,128)(2,1)S(1)}, bf16[2,256,128]{2,1,0:T(8,128)(2,1)S(1)}, u32[]{:S(2)}, u32[]{:S(2)}) collective-permute-start(bf16[2,256,128]{2,1,0:T(8,128)(2,1)S(1)} %get-tuple-element.36), channel_id=1, source_target_pairs={{0,16},{1,17},{2,18},{3,19},{4,20},{5,21},{6,22},{7,23},{8,24},{9,... | collective-permute-start | bytes 393224 | tf_op jit(solution)/shard_map/ppermute | solution.py:37
  172.1 13.2 %collective-permute-start.23 = (bf16[2,256,128]{2,1,0:T(8,128)(2,1)S(1)}, bf16[2,256,128]{2,1,0:T(8,128)(2,1)S(1)}, u32[]{:S(2)}, u32[]{:S(2)}) collective-permute-start(bf16[2,256,128]{2,1,0:T(8,128)(2,1)S(1)} %fusion.6), channel_id=1, source_target_pairs={{0,0},{1,1},{2,2},{3,3},{4,32},{5,33},{6,34},{7,35},{8,8},{9,9},{1... | collective-permute-start | bytes 393224 | tf_op jit(solution)/shard_map/ppermute | solution.py:37
Sparse Core Ops, SparseCore 0:
  10.9 42.4 all-gather.1
  111.0 47.8 reduce-scatter.1

commit v2 on v1

--- a/solution.py
+++ b/solution.py
@@ -19,6 +19,10 @@
 SMEM = pl.BlockSpec(memory_space=pltpu.SMEM)
 X_GROUPS = [[hi + 2 * x for x in range(4)] for hi in range(2)]
 Y_OFFSETS = (0, 3, 1, 2)
+
+
+def limit(mebibytes):
+    return pltpu.CompilerParams(vmem_limit_bytes=mebibytes * 2**20)
 
 
 def device_number(x, hi, lo, y, core):
@@ -35,6 +39,10 @@
                         here = device_number(x, hi, lo, y, core)
                         pairs.append((here, device_number(*target(x, hi, lo, y, core))))
     return lax.ppermute(value, ALL, pairs)
+
+
+def after(value, *others):
+    return lax.optimization_barrier((value, *others))[0]
 
 
 def along_y(step):
@@ -107,8 +115,8 @@
     grad = grad * keeper * inside
     first = BETA_ONE * first + (1.0 - BETA_ONE) * grad
     second = BETA_TWO * second + (1.0 - BETA_TWO) * grad * grad
-    update = first / CORRECT_ONE / (jnp.sqrt(second / CORRECT_TWO) + ADAM_EPS)
-    master = master - LEARN_RATE * update
+    step = (LEARN_RATE / CORRECT_ONE) * first
+    master = master - step / (jnp.sqrt(second * (1.0 / CORRECT_TWO)) + ADAM_EPS)
     return master, first, second, quantize(master, keeper, power_of_two(expo, 1), inverse)
 
 
@@ -216,7 +224,7 @@
         out_specs=VMEM,
         out_shape=jax.ShapeDtypeStruct((3, 256, 256), F32 if mine else BF16),
         scratch_shapes=[pltpu.VMEM((3, 256, 256), F32)],
-        compiler_params=pltpu.CompilerParams(vmem_limit_bytes=40 * 2**20),
+        compiler_params=limit(16),
         name="partial_own" if mine else "partial_sent",
     )(place, *pieces, weights)
 
@@ -248,84 +256,93 @@
     )
 
 
-def outputs_kernel(mine, place, rows_own, rows_other, weights, out):
-    hi, lo, y, core = place[1], place[2], place[3], place[4]
-    core = core if mine else 1 - core
-    for ring in range(4):
-        to_y = (y + ring) & 3
-        start = pl.multiple_of((to_y & 1) * 256 + core * 128, 128)
-
-        def fill(rows):
+def outputs_kernel(sides, place, rows, weights, *outs):
+    lo, core = place[2], place[4]
+    for side, out in zip(sides, outs):
+        to_core = core if side == "kept" else 1 - core
+        for low in range(2):
+            start = pl.multiple_of(low * 256 + to_core * 128, 128)
             for lo_step in range(4):
                 block = (lo + lo_step) & 3
                 parts = [weights[block, which, pl.ds(start, 128), :] for which in range(3)]
-                out[ring, lo_step, 0] = cross(rows[2], parts[2], 1, 1).astype(out.dtype)
-                out[ring, lo_step, 1] = (
+                out[low, lo_step, 0] = cross(rows[2], parts[2], 1, 1).astype(out.dtype)
+                out[low, lo_step, 1] = (
                     cross(rows[0], parts[0], 1, 1) + cross(rows[1], parts[1], 1, 1)
                 ).astype(out.dtype)
 
+
+def outputs(sides, place, rows, weights):
+    return pl.pallas_call(
+        lambda *refs: outputs_kernel(sides, *refs),
+        in_specs=[SMEM] + [VMEM] * 2,
+        out_specs=[VMEM] * len(sides),
+        out_shape=[jax.ShapeDtypeStruct((2, 4, 2, 256, 128), BF16)] * len(sides),
+        compiler_params=limit(16),
+        name="outputs_" + "_".join(sides),
+    )(place, rows, weights)
+
+
+def combine_kernel(place, own_kept, own_got, arrived_kept, arrived_got, out):
+    hi, y = place[1], place[3]
+    for step in range(4):
+        to_y = (y + step) & 3
+        low = to_y & 1
+
         @pl.when((to_y >> 1) == hi)
         def _():
-            fill(rows_own)
+            out[step] = (own_kept[low].astype(F32) + own_got[low].astype(F32)).astype(BF16)
 
         @pl.when((to_y >> 1) != hi)
         def _():
-            fill(rows_other)
-
-
-def outputs(mine, place, rows_own, rows_other, weights):
-    return pl.pallas_call(
-        lambda *refs: outputs_kernel(mine, *refs),
-        in_specs=[SMEM] + [VMEM] * 3,
+            out[step] = (arrived_kept[low].astype(F32) + arrived_got[low].astype(F32)).astype(BF16)
+
+
+def combine(place, *halves):
+    return pl.pallas_call(
+        combine_kernel,
+        in_specs=[SMEM] + [VMEM] * 4,
         out_specs=VMEM,
         out_shape=jax.ShapeDtypeStruct((4, 4, 2, 256, 128), BF16),
-        compiler_params=pltpu.CompilerParams(vmem_limit_bytes=40 * 2**20),
-        name="outputs_kept" if mine else "outputs_sent",
-    )(place, rows_own, rows_other, weights)
-
-
-def grads_kernel(inverse_scale, place, *refs):
-    own, other, rows_own, rows_other, out, acc = refs[:5], refs[5:10], refs[10], refs[11], refs[12], refs[13]
+        compiler_params=limit(16),
+        name="combine",
+    )(place, *halves)
+
+
+def grads_kernel(own_rows, inverse_scale, place, *refs):
+    own, other, rows, out = refs[:5], refs[5:10], refs[10], refs[-1]
     hi, lo, y, core = place[1], place[2], place[3], place[4]
+    target = hi if own_rows else 1 - hi
     for ring, offset in enumerate(Y_OFFSETS):
         from_y = (y + offset) & 3
-        low = from_y & 1
-
-        def add(rows):
+
+        @pl.when((from_y >> 1) == target)
+        def _():
+            low = from_y & 1
+            first = pl.ds(pl.multiple_of(low * 256 + core * 128, 128), 128)
+            second = pl.ds(pl.multiple_of(low * 256 + (1 - core) * 128, 128), 128)
             for lo_step in range(4):
                 block = (lo - lo_step) & 3
                 for which in range(3):
                     left = piece_rows((own, other), ring, lo_step, which // 2)
-                    term = cross(left, rows[which], 0, 0)
-                    start = pl.multiple_of(low * 256 + core * 128, 128)
-                    second = pl.multiple_of(low * 256 + (1 - core) * 128, 128)
-                    acc[block, which, pl.ds(start, 128), :] += term[:128]
-                    acc[block, which, pl.ds(second, 128), :] += term[128:]
-
-        if ring == 0:
-            acc[...] = jnp.zeros_like(acc)
-
-        @pl.when((from_y >> 1) == hi)
-        def _():
-            add(rows_own)
-
-        @pl.when((from_y >> 1) != hi)
-        def _():
-            add(rows_other)
-
-    out[...] = (acc[...] * inverse_scale).astype(out.dtype)
-
-
-def grads(inverse_scale, place, pieces, rows_own, rows_other):
-    return pl.pallas_call(
-        lambda *refs: grads_kernel(inverse_scale, *refs),
-        in_specs=[SMEM] + [VMEM] * 12,
+                    term = cross(left, rows[which], 0, 0) * inverse_scale
+                    upper, lower = term[:128], term[128:]
+                    if not own_rows:
+                        before = refs[11]
+                        upper += before[block, which, first, :].astype(F32)
+                        lower += before[block, which, second, :].astype(F32)
+                    out[block, which, first, :] = upper.astype(BF16)
+                    out[block, which, second, :] = lower.astype(BF16)
+
+
+def grads(own_rows, inverse_scale, place, pieces, rows, *before):
+    return pl.pallas_call(
+        lambda *refs: grads_kernel(own_rows, inverse_scale, *refs),
+        in_specs=[SMEM] + [VMEM] * (11 + len(before)),
         out_specs=VMEM,
         out_shape=jax.ShapeDtypeStruct((4, 3, 512, 256), BF16),
-        scratch_shapes=[pltpu.VMEM((4, 3, 512, 256), F32)],
-        compiler_params=pltpu.CompilerParams(vmem_limit_bytes=48 * 2**20),
-        name="grads",
-    )(place, *pieces, rows_own, rows_other)
+        compiler_params=limit(24),
+        name="own_grads" if own_rows else "arrived_grads",
+    )(place, *pieces, rows, *before)
 
 
 def gather_pieces(tokens, cotangent):
@@ -339,10 +356,8 @@
     return own + tuple(move(piece, other_core) for piece in own)
 
 
-def scatter_outputs(kept, sent):
+def scatter_outputs(total):
     f32 = lambda value: value.astype(F32)
-    arrived = move(sent, other_core)
-    total = (f32(kept) + f32(arrived)).astype(BF16)
     low = move(total[2, :2], along_y(1))
     high = move(total[2, 2:], along_y(-1))
     ahead = jnp.concatenate([(f32(total[1, :2]) + f32(low)).astype(BF16), total[1, 2:]])
@@ -354,7 +369,7 @@
     result = line[0]
     for step in (1, 2, 3):
         result = result + f32(move(leaving[step - 1], along_lo(step)))
-    return move(result.astype(BF16), swap_hi_y)
+    return result.astype(BF16)
 
 
 def shards(
@@ -390,20 +405,27 @@
     kept = partial(True, place, pieces, weights)
     rows_own = gated(kept, arrived)
     rows_other = move(rows_own, other_hi)
-    out_sent = outputs(False, place, rows_own, rows_other, weights)
-    out_kept = outputs(True, place, rows_own, rows_other, weights)
     inverse_scale = 1.0 / (tokens.shape[0] * lax.axis_size("dp"))
-    grad = grads(inverse_scale, place, pieces, rows_own, rows_other)
+    grad = grads(True, inverse_scale, place, pieces, rows_own)
+    rows_own, grad = lax.optimization_barrier((rows_own, grad))
+    own_sent, own_kept = outputs(("sent", "kept"), place, rows_own, weights)
+    own_got = move(own_sent, other_core)
+    rows_other, own_kept = lax.optimization_barrier((rows_other, own_kept))
+    grad = grads(False, inverse_scale, place, pieces, rows_other, grad)
     grad = lax.psum_scatter(
         grad.reshape(6144, 256), "dp", scatter_dimension=0, tiled=True, axis_index_groups=X_GROUPS
     ).reshape(3, 512, 256)
-    both = scatter_outputs(out_kept, out_sent)
+    (sent,) = outputs(("sent",), place, rows_other, weights)
+    got = move(sent, other_core)
+    (kept,) = outputs(("kept",), place, rows_other, weights)
+    both = scatter_outputs(combine(place, own_kept, own_got, kept, got))
     gu_new, gu_first_new, gu_second_new, gu_copy = gu_update(
         grad, gu_master, gu_first, gu_second, gu_codes, gu_expo
     )
     down_new, down_first_new, down_second_new, down_copy = down_update(
         grad, down_master, down_first, down_second, down_codes, down_expo
     )
+    both = after(move(both, swap_hi_y), gu_copy, down_copy)
     return (
         both[0],
         both[1],

time: 202 us -> 192 us (0.950)
  the two profiles are of different devices: /device:TPU:224 before, /device:TPU:22 now
where the time goes in v2:
time: 192 us; the launch traced here: 191 us
  waiting for transfers between devices  73.3 us (38%)
  starting transfers between devices  56.8 us (30%)
  Pallas kernels  30.2 us (16%)
  local copies, waits for them, and re-layouts  15.4 us (8%)
  between operations  14.5 us (8%)
    ppermute x25, waiting for transfers between devices, move(): return lax.ppermute(value, ALL, pairs)  73.3 us
    ppermute x25, starting transfers between devices, move(): return lax.ppermute(value, ALL, pairs)  56.8 us
    unnamed x58, local copies, waits for them, and re-layouts  14.5 us
    pallas_call x3, Pallas kernels, outputs(): pl.pallas_call(lambda *refs: outputs_kernel(sides, *refs), in_specs=[SMEM...  5.39 us
    pallas_call x1, Pallas kernels, gu_update(): pl.pallas_call(gu_adam_kernel, grid=(parts, 2), in_specs=[block, block, b...  5.26 us
    pallas_call x2, Pallas kernels, grads(): pl.pallas_call(lambda *refs: grads_kernel(own_rows, inverse_scale, *refs)...  4.93 us
    pallas_call x2, Pallas kernels, partial(): pl.pallas_call(lambda *refs: partial_kernel(mine, *refs), in_specs=[SMEM]...  4.73 us
  transfers between devices with their start and end apart: 27, of which 14 were waited for; matrix products, arithmetic and copies ran while one was open for 0% of the time, Pallas kernels for 10%

profile of v2, /device:TPU:22, one launch (start us, length us, event | category | flops | bytes accessed | tf_op | source)
XLA Modules:
  0.0 190.8 jit_solution(5373084871939248442)
XLA Ops:
  7.2 3.5 %quantize.1 = bf16[3,512,256]{2,1,0:T(8,128)(2,1)} custom-call(f32[2,512,256]{2,1,0:T(8,128)} %master.2, s32[2,128,256]{2,1,0:T(8,128)} %codes.2, s32[2,256]{1,0:T(2,128)} %expo.1, f32[256,512]{1,0:T(8,128)} %master.3, s32[64,512]{1,0:T(8,128)} %codes.3, s32[1,512]{1,0:T(1,128)} %bitcast.75), custom_call_target="tpu_custom_call" | custom-call | tf_op jit(solution)/shard_map/quantize/pallas_call | solution.py:392
  10.8 8.9 %collective-permute-start = (bf16[2,256,128]{2,1,0:T(8,128)(2,1)S(1)}, bf16[2,256,128]{2,1,0:T(8,128)(2,1)S(1)}, u32[]{:S(2)}, u32[]{:S(2)}) collective-permute-start(bf16[2,256,128]{2,1,0:T(8,128)(2,1)S(1)} %pad_maximum_fusion.3), channel_id=1, source_target_pairs={{0,0},{1,1},{2,2},{3,3},{4,32},{5,33},{6,34},{7,35},{8,8},{9,9},{1... | collective-permute-start | bytes 393224 | tf_op jit(solution)/shard_map/ppermute | solution.py:41
  19.7 4.7 %collective-permute-done = bf16[2,256,128]{2,1,0:T(8,128)(2,1)S(1)} collective-permute-done((bf16[2,256,128]{2,1,0:T(8,128)(2,1)S(1)}, bf16[2,256,128]{2,1,0:T(8,128)(2,1)S(1)}, u32[]{:S(2)}, u32[]{:S(2)}) %collective-permute-start) | collective-permute-done | bytes 131104 | tf_op jit(solution)/shard_map/ppermute | solution.py:41
  24.4 4.7 %collective-permute-start.3 = (bf16[2,256,128]{2,1,0:T(8,128)(2,1)S(1)}, bf16[2,256,128]{2,1,0:T(8,128)(2,1)S(1)}, u32[]{:S(2)}, u32[]{:S(2)}) collective-permute-start(bf16[2,256,128]{2,1,0:T(8,128)(2,1)S(1)} %collective-permute-done), channel_id=1, source_target_pairs={{0,24},{1,25},{2,26},{3,27},{4,28},{5,29},{6,30},{7,31},{8,0},{9,1... | collective-permute-start | bytes 393224 | tf_op jit(solution)/shard_map/ppermute | solution.py:41
  29.0 0.5 collective-permute-start.2
  29.6 2.0 %collective-permute-start.1 = (bf16[2,256,128]{2,1,0:T(8,128)(2,1)S(1)}, bf16[2,256,128]{2,1,0:T(8,128)(2,1)S(1)}, u32[]{:S(2)}, u32[]{:S(2)}) collective-permute-start(bf16[2,256,128]{2,1,0:T(8,128)(2,1)S(1)} %collective-permute-done), channel_id=1, source_target_pairs={{0,8},{1,9},{2,10},{3,11},{4,12},{5,13},{6,14},{7,15},{8,16},{9,17... | collective-permute-start | bytes 393224 | tf_op jit(solution)/shard_map/ppermute | solution.py:41
  31.6 1.3 collective-permute-done.3
  32.9 8.6 %collective-permute-done.2 = bf16[2,256,128]{2,1,0:T(8,128)(2,1)S(1)} collective-permute-done((bf16[2,256,128]{2,1,0:T(8,128)(2,1)S(1)}, bf16[2,256,128]{2,1,0:T(8,128)(2,1)S(1)}, u32[]{:S(2)}, u32[]{:S(2)}) %collective-permute-start.2) | collective-permute-done | bytes 131104 | tf_op jit(solution)/shard_map/ppermute | solution.py:41
  41.6 1.4 collective-permute-start.4
  43.0 0.7 collective-permute-start.5
  43.7 11.3 %collective-permute-done.4.refs_2_ = bf16[4,2,256,128]{3,2,1,0:T(8,128)(2,1)S(1)} collective-permute-done((bf16[4,2,256,128]{3,2,1,0:T(8,128)(2,1)S(1)}, bf16[4,2,256,128]{3,2,1,0:T(8,128)(2,1)S(1)}, u32[]{:S(2)}, u32[]{:S(2)}) %collective-permute-start.4) | collective-permute-done | bytes 524320 | tf_op jit(solution)/shard_map/ppermute | solution.py:41
  55.0 1.4 collective-permute-start.6
  56.4 0.6 collective-permute-start.10
  57.0 0.7 collective-permute-start.7
  57.8 4.2 %collective-permute-done.6.refs_4_ = bf16[2,2,256,128]{3,2,1,0:T(8,128)(2,1)S(1)} collective-permute-done((bf16[2,2,256,128]{3,2,1,0:T(8,128)(2,1)S(1)}, bf16[2,2,256,128]{3,2,1,0:T(8,128)(2,1)S(1)}, u32[]{:S(2)}, u32[]{:S(2)}) %collective-permute-start.6) | collective-permute-done | bytes 262176 | tf_op jit(solution)/shard_map/ppermute | solution.py:41
  62.0 3.5 %collective-permute-done.7.refs_5_ = bf16[2,2,256,128]{3,2,1,0:T(8,128)(2,1)} collective-permute-done((bf16[2,2,256,128]{3,2,1,0:T(8,128)(2,1)S(1)}, bf16[2,2,256,128]{3,2,1,0:T(8,128)(2,1)}, u32[]{:S(2)}, u32[]{:S(2)}) %collective-permute-start.7) | collective-permute-done | bytes 262176 | tf_op jit(solution)/shard_map/ppermute | solution.py:41
  65.4 0.1 stack.47.refs_0_.place
  65.6 1.7 collective-permute-done.12.refs_10_
  67.3 1.9 copy-done
  69.2 2.3 %partial_sent.1 = bf16[3,256,256]{2,1,0:T(8,128)(2,1)S(1)} custom-call(s32[5]{0:T(128)S(1)} %stack.47.refs_0_.place, bf16[4,2,256,128]{3,2,1,0:T(8,128)(2,1)S(1)} %pad_maximum_fusion.refs_1_, bf16[4,2,256,128]{3,2,1,0:T(8,128)(2,1)S(1)} %collective-permute-done.4.refs_2_, bf16[4,2,256,128]{3,2,1,0:T(8,128)(2,1)S(1)} %collective-permute-done.5.refs_3_, ...), custom_call_target="tpu_custom_call" | custom-call | tf_op jit(solution)/shard_map/partial_sent/pallas_call | solution.py:221
  71.5 4.8 %collective-permute-start.13 = (bf16[3,256,256]{2,1,0:T(8,128)(2,1)S(1)}, bf16[3,256,256]{2,1,0:T(8,128)(2,1)}, u32[]{:S(2)}, u32[]{:S(2)}) collective-permute-start(bf16[3,256,256]{2,1,0:T(8,128)(2,1)S(1)} %partial_sent.1), channel_id=1, source_target_pairs={{0,32},{1,33},{2,34},{3,35},{4,36},{5,37},{6,38},{7,39},{8,40},{9,... | collective-permute-start | bytes 1179656 | tf_op jit(solution)/shard_map/ppermute | solution.py:41
  76.4 2.4 %partial_own.1.own = f32[3,256,256]{2,1,0:T(8,128)S(1)} custom-call(s32[5]{0:T(128)S(1)} %stack.47.refs_0_.place, bf16[4,2,256,128]{3,2,1,0:T(8,128)(2,1)S(1)} %pad_maximum_fusion.refs_1_, bf16[4,2,256,128]{3,2,1,0:T(8,128)(2,1)S(1)} %collective-permute-done.4.refs_2_, bf16[4,2,256,128]{3,2,1,0:T(8,128)(2,1)S(1)} %collective-permute-done.5.refs_3_, ...), custom_call_target="tpu_custom_call" | custom-call | tf_op jit(solution)/shard_map/partial_own/pallas_call | solution.py:221
  78.8 0.9 copy-done.23
  79.6 9.2 %collective-permute-done.13.sent = bf16[3,256,256]{2,1,0:T(8,128)(2,1)} collective-permute-done((bf16[3,256,256]{2,1,0:T(8,128)(2,1)S(1)}, bf16[3,256,256]{2,1,0:T(8,128)(2,1)}, u32[]{:S(2)}, u32[]{:S(2)}) %collective-permute-start.13) | collective-permute-done | bytes 393248 | tf_op jit(solution)/shard_map/ppermute | solution.py:41
  88.9 2.2 %gated.1.refs_11_.refs_1_ = bf16[3,256,256]{2,1,0:T(8,128)(2,1)} custom-call(f32[3,256,256]{2,1,0:T(8,128)} %copy-done.23, bf16[3,256,256]{2,1,0:T(8,128)(2,1)} %collective-permute-done.13.sent), custom_call_target="tpu_custom_call" | custom-call | tf_op jit(solution)/shard_map/gated/pallas_call | solution.py:244
  91.0 4.5 %collective-permute-start.14 = (bf16[3,256,256]{2,1,0:T(8,128)(2,1)}, bf16[3,256,256]{2,1,0:T(8,128)(2,1)S(1)}, u32[]{:S(2)}, u32[]{:S(2)}) collective-permute-start(bf16[3,256,256]{2,1,0:T(8,128)(2,1)} %gated.1.refs_11_.refs_1_), channel_id=1, source_target_pairs={{0,32},{1,33},{2,34},{3,35},{4,36},{5,37},{6,38},{7,39},{8,40},{9,... | collective-permute-start | bytes 1179656 | tf_op jit(solution)/shard_map/ppermute | solution.py:41
  95.5 1.0 copy-done.3
  96.5 1.0 copy-done.6
  97.6 1.0 copy-done.9
  98.6 1.0 copy-done.12
  99.7 1.0 copy-done.15
  100.7 1.0 copy-done.18
  101.8 1.0 copy-done.22
  102.8 2.4 %own_grads.1.refs_12_ = bf16[4,3,512,256]{3,2,1,0:T(8,128)(2,1)S(1)} custom-call(s32[5]{0:T(128)S(1)} %stack.47.refs_0_.place, bf16[4,2,256,128]{3,2,1,0:T(8,128)(2,1)S(1)} %copy-done.3, bf16[4,2,256,128]{3,2,1,0:T(8,128)(2,1)S(1)} %copy-done.6, bf16[4,2,256,128]{3,2,1,0:T(8,128)(2,1)S(1)} %copy-done.9, ...), custom_call_target="tpu_custom_call" | custom-call | tf_op jit(solution)/shard_map/own_grads/pallas_call | solution.py:338
  105.2 2.3 %outputs_sent_kept.1 = (bf16[2,4,2,256,128]{4,3,2,1,0:T(8,128)(2,1)S(1)}, bf16[2,4,2,256,128]{4,3,2,1,0:T(8,128)(2,1)S(1)}) custom-call(s32[5]{0:T(128)S(1)} %stack.47.refs_0_.place, bf16[3,256,256]{2,1,0:T(8,128)(2,1)S(1)} %copy-done.22, bf16[4,3,512,256]{3,2,1,0:T(8,128)(2,1)S(1)} %bitcast.62), custom_call_target="tpu_custom_call" | custom-call | tf_op jit(solution)/shard_map/outputs_sent_kept/pallas_call | solution.py:275
  107.6 1.0 copy-done.24
  108.5 1.0 copy-done.26
  109.5 2.6 %arrived_grads.1 = bf16[4,3,512,256]{3,2,1,0:T(8,128)(2,1)S(1)} custom-call(s32[5]{0:T(128)S(1)} %stack.47.refs_0_.place, bf16[4,2,256,128]{3,2,1,0:T(8,128)(2,1)S(1)} %copy-done.3, bf16[4,2,256,128]{3,2,1,0:T(8,128)(2,1)S(1)} %copy-done.7, bf16[4,2,256,128]{3,2,1,0:T(8,128)(2,1)S(1)} %copy-done.10, ...), custom_call_target="tpu_custom_call" | custom-call | tf_op jit(solution)/shard_map/arrived_grads/pallas_call | solution.py:338
  112.1 1.6 copy-done.4
  113.8 0.1 collective-permute-start.15
  113.9 0.9 copy-done.21
  114.7 1.5 outputs_sent.1
  116.3 0.3 collective-permute-start.16
  116.6 1.5 outputs_kept.1.arrived_kept
  118.1 1.1 collective-permute-done.16.arrived_got
  119.2 1.1 combine.1
  120.3 0.1 slice_bitcast_fusion.6
  120.4 3.7 %collective-permute-start.17 = (bf16[2,2,256,128]{3,2,1,0:T(8,128)(2,1)S(1)}, bf16[2,2,256,128]{3,2,1,0:T(8,128)(2,1)S(1)}, u32[]{:S(2)}, u32[]{:S(2)}) collective-permute-start(bf16[2,2,256,128]{3,2,1,0:T(8,128)(2,1)S(1)} %get-tuple-element.44), channel_id=1, source_target_pairs={{0,2},{1,3},{2,4},{3,5},{4,6},{5,7},{6,0},{7,1},{8,10},{9,11},{10,... | collective-permute-start | bytes 786440 | tf_op jit(solution)/shard_map/ppermute | solution.py:41
  124.1 5.9 %collective-permute-done.17 = bf16[2,2,256,128]{3,2,1,0:T(8,128)(2,1)S(1)} collective-permute-done((bf16[2,2,256,128]{3,2,1,0:T(8,128)(2,1)S(1)}, bf16[2,2,256,128]{3,2,1,0:T(8,128)(2,1)S(1)}, u32[]{:S(2)}, u32[]{:S(2)}) %collective-permute-start.17) | collective-permute-done | bytes 262176 | tf_op jit(solution)/shard_map/ppermute | solution.py:41
  130.0 2.2 %collective-permute-done.19 = bf16[2,2,256,128]{3,2,1,0:T(8,128)(2,1)S(1)} collective-permute-done((bf16[2,2,256,128]{3,2,1,0:T(8,128)(2,1)S(1)}, bf16[2,2,256,128]{3,2,1,0:T(8,128)(2,1)S(1)}, u32[]{:S(2)}, u32[]{:S(2)}) %collective-permute-start.19) | collective-permute-done | bytes 262176 | tf_op jit(solution)/shard_map/ppermute | solution.py:41
  132.2 0.1 fusion.2
  132.4 0.4 collective-permute-start.20
  132.8 1.8 collective-permute-start.18
  134.6 10.8 %collective-permute-done.20 = bf16[4,2,256,128]{3,2,1,0:T(8,128)(2,1)S(1)} collective-permute-done((bf16[4,2,256,128]{3,2,1,0:T(8,128)(2,1)S(1)}, bf16[4,2,256,128]{3,2,1,0:T(8,128)(2,1)S(1)}, u32[]{:S(2)}, u32[]{:S(2)}) %collective-permute-start.20) | collective-permute-done | bytes 524320 | tf_op jit(solution)/shard_map/ppermute | solution.py:41
  145.5 0.3 collective-permute-done.18
  145.8 0.2 fusion.7
  146.0 0.1 collective-permute-start.23
  146.1 8.3 %collective-permute-start.22 = (bf16[2,256,128]{2,1,0:T(8,128)(2,1)S(1)}, bf16[2,256,128]{2,1,0:T(8,128)(2,1)S(1)}, u32[]{:S(2)}, u32[]{:S(2)}) collective-permute-start(bf16[2,256,128]{2,1,0:T(8,128)(2,1)S(1)} %get-tuple-element.50), channel_id=1, source_target_pairs={{0,16},{1,17},{2,18},{3,19},{4,20},{5,21},{6,22},{7,23},{8,24},{9,... | collective-permute-start | bytes 393224 | tf_op jit(solution)/shard_map/ppermute | solution.py:41
  154.4 1.9 %collective-permute-start.21 = (bf16[2,256,128]{2,1,0:T(8,128)(2,1)S(1)}, bf16[2,256,128]{2,1,0:T(8,128)(2,1)S(1)}, u32[]{:S(2)}, u32[]{:S(2)}) collective-permute-start(bf16[2,256,128]{2,1,0:T(8,128)(2,1)S(1)} %get-tuple-element.48), channel_id=1, source_target_pairs={{0,8},{1,9},{2,10},{3,11},{4,12},{5,13},{6,14},{7,15},{8,16},{9,17... | collective-permute-start | bytes 393224 | tf_op jit(solution)/shard_map/ppermute | solution.py:41
  156.3 8.4 %collective-permute-done.22 = bf16[2,256,128]{2,1,0:T(8,128)(2,1)S(1)} collective-permute-done((bf16[2,256,128]{2,1,0:T(8,128)(2,1)S(1)}, bf16[2,256,128]{2,1,0:T(8,128)(2,1)S(1)}, u32[]{:S(2)}, u32[]{:S(2)}) %collective-permute-start.22) | collective-permute-done | bytes 131104 | tf_op jit(solution)/shard_map/ppermute | solution.py:41
  164.8 10.1 %collective-permute-start.24 = (bf16[2,256,128]{2,1,0:T(8,128)(2,1)S(1)}, bf16[2,256,128]{2,1,0:T(8,128)(2,1)S(1)}, u32[]{:S(2)}, u32[]{:S(2)}) collective-permute-start(bf16[2,256,128]{2,1,0:T(8,128)(2,1)S(1)} %fusion.6), channel_id=1, source_target_pairs={{0,0},{1,1},{2,2},{3,3},{4,32},{5,33},{6,34},{7,35},{8,8},{9,9},{1... | collective-permute-start | bytes 393224 | tf_op jit(solution)/shard_map/ppermute | solution.py:41
  174.9 5.3 %gu_adam.1 = (f32[2,512,256]{2,1,0:T(8,128)}, f32[2,512,256]{2,1,0:T(8,128)}, f32[2,512,256]{2,1,0:T(8,128)}, bf16[2,512,256]{2,1,0:T(8,128)(2,1)}) custom-call(bf16[3,512,256]{2,1,0:T(8,128)(2,1)} %bitcast.67, f32[2,512,256]{2,1,0:T(8,128)} %master.2, f32[2,512,256]{2,1,0:T(8,128)} %first.2, f32[2,512,256]{2,1,0:T(8,128)} %second.2, s32[2,128,256]{2,1,0:T(8,128)} %codes.2, ...), custom_call_target="tpu_custom_call" | custom-call | tf_op jit(solution)/shard_map/gu_adam/pallas_call | solution.py:146
  180.2 3.1 %down_adam.1 = (f32[256,512]{1,0:T(8,128)}, f32[256,512]{1,0:T(8,128)}, f32[256,512]{1,0:T(8,128)}, bf16[256,512]{1,0:T(8,128)(2,1)}) custom-call(bf16[3,512,256]{2,1,0:T(8,128)(2,1)} %bitcast.68, f32[256,512]{1,0:T(8,128)} %master.3, f32[256,512]{1,0:T(8,128)} %first.3, f32[256,512]{1,0:T(8,128)} %second.3, s32[64,512]{1,0:T(8,128)} %codes.3, s32[1,512]{1,0:T(1,128)} %bitcast.76), custom_call_target="tpu_custom_call" | custom-call | tf_op jit(solution)/shard_map/down_adam/pallas_call | solution.py:163
  183.3 0.7 slice_bitcast_fusion.11
  (75 shorter events, 0.6 us)
Async XLA Ops:
  7.2 3.6 %copy-start.27 = (bf16[256,128]{1,0:T(8,128)(2,1)S(1)}, bf16[256,128]{1,0:T(8,128)(2,1)}, u32[]{:S(2)}) copy-start(bf16[256,128]{1,0:T(8,128)(2,1)} %param.13) | copy-start | bytes 196612
  7.2 3.6 %copy-start.28 = (bf16[256,128]{1,0:T(8,128)(2,1)S(1)}, bf16[256,128]{1,0:T(8,128)(2,1)}, u32[]{:S(2)}) copy-start(bf16[256,128]{1,0:T(8,128)(2,1)} %param.12) | copy-start | bytes 196612
  7.2 60.1 %all-gather.2.cloned.1.call-start = ((), (), s32[]{:S(2)}) async-start(), calls=%async_computation.1 | async-start | bytes 3932160 | tf_op jit(solution)/shard_map/all_gather | solution.py:399
  10.7 164.2 %reduce-scatter.2.cloned.1.call-start = ((), (), s32[]{:S(2)}) async-start(), calls=%async_computation.2 | async-start | bytes 3932160 | tf_op jit(solution)/shard_map/reduce_scatter | solution.py:415
  10.8 13.5 %collective-permute-start = (bf16[2,256,128]{2,1,0:T(8,128)(2,1)S(1)}, bf16[2,256,128]{2,1,0:T(8,128)(2,1)S(1)}, u32[]{:S(2)}, u32[]{:S(2)}) collective-permute-start(bf16[2,256,128]{2,1,0:T(8,128)(2,1)S(1)} %pad_maximum_fusion.3), channel_id=1, source_target_pairs={{0,0},{1,1},{2,2},{3,3},{4,32},{5,33},{6,34},{7,35},{8,8},{9,9},{1... | collective-permute-start | bytes 393224 | tf_op jit(solution)/shard_map/ppermute | solution.py:41
  24.4 8.5 %collective-permute-start.3 = (bf16[2,256,128]{2,1,0:T(8,128)(2,1)S(1)}, bf16[2,256,128]{2,1,0:T(8,128)(2,1)S(1)}, u32[]{:S(2)}, u32[]{:S(2)}) collective-permute-start(bf16[2,256,128]{2,1,0:T(8,128)(2,1)S(1)} %collective-permute-done), channel_id=1, source_target_pairs={{0,24},{1,25},{2,26},{3,27},{4,28},{5,29},{6,30},{7,31},{8,0},{9,1... | collective-permute-start | bytes 393224 | tf_op jit(solution)/shard_map/ppermute | solution.py:41
  29.0 12.5 %collective-permute-start.2 = (bf16[2,256,128]{2,1,0:T(8,128)(2,1)S(1)}, bf16[2,256,128]{2,1,0:T(8,128)(2,1)S(1)}, u32[]{:S(2)}, u32[]{:S(2)}) collective-permute-start(bf16[2,256,128]{2,1,0:T(8,128)(2,1)S(1)} %collective-permute-done), channel_id=1, source_target_pairs={{0,16},{1,17},{2,18},{3,19},{4,20},{5,21},{6,22},{7,23},{8,24},{9,... | collective-permute-start | bytes 393224 | tf_op jit(solution)/shard_map/ppermute | solution.py:41
  29.6 12.0 %collective-permute-start.1 = (bf16[2,256,128]{2,1,0:T(8,128)(2,1)S(1)}, bf16[2,256,128]{2,1,0:T(8,128)(2,1)S(1)}, u32[]{:S(2)}, u32[]{:S(2)}) collective-permute-start(bf16[2,256,128]{2,1,0:T(8,128)(2,1)S(1)} %collective-permute-done), channel_id=1, source_target_pairs={{0,8},{1,9},{2,10},{3,11},{4,12},{5,13},{6,14},{7,15},{8,16},{9,17... | collective-permute-start | bytes 393224 | tf_op jit(solution)/shard_map/ppermute | solution.py:41
  41.6 34.7 %copy-start.2 = (bf16[4,2,256,128]{3,2,1,0:T(8,128)(2,1)}, bf16[4,2,256,128]{3,2,1,0:T(8,128)(2,1)S(1)}, u32[]{:S(2)}) copy-start(bf16[4,2,256,128]{3,2,1,0:T(8,128)(2,1)S(1)} %pad_maximum_fusion.refs_1_) | copy-start | bytes 1572868
  41.6 13.4 %collective-permute-start.4 = (bf16[4,2,256,128]{3,2,1,0:T(8,128)(2,1)S(1)}, bf16[4,2,256,128]{3,2,1,0:T(8,128)(2,1)S(1)}, u32[]{:S(2)}, u32[]{:S(2)}) collective-permute-start(bf16[4,2,256,128]{3,2,1,0:T(8,128)(2,1)S(1)} %pad_maximum_fusion.refs_1_), channel_id=1, source_target_pairs={{0,2},{1,3},{2,4},{3,5},{4,6},{5,7},{6,0},{7,1},{8,10},{9,11},{10,... | collective-permute-start | bytes 1572872 | tf_op jit(solution)/shard_map/ppermute | solution.py:41
  43.0 13.4 %collective-permute-start.5 = (bf16[4,2,256,128]{3,2,1,0:T(8,128)(2,1)S(1)}, bf16[4,2,256,128]{3,2,1,0:T(8,128)(2,1)S(1)}, u32[]{:S(2)}, u32[]{:S(2)}) collective-permute-start(bf16[4,2,256,128]{3,2,1,0:T(8,128)(2,1)S(1)} %pad_maximum_fusion.refs_1_), channel_id=1, source_target_pairs={{0,6},{1,7},{2,0},{3,1},{4,2},{5,3},{6,4},{7,5},{8,14},{9,15},{10,... | collective-permute-start | bytes 1572872 | tf_op jit(solution)/shard_map/ppermute | solution.py:41
  43.7 21.8 %collective-permute-start.8 = (bf16[4,2,256,128]{3,2,1,0:T(8,128)(2,1)S(1)}, bf16[4,2,256,128]{3,2,1,0:T(8,128)(2,1)S(1)}, u32[]{:S(2)}, u32[]{:S(2)}) collective-permute-start(bf16[4,2,256,128]{3,2,1,0:T(8,128)(2,1)S(1)} %pad_maximum_fusion.refs_1_), channel_id=1, source_target_pairs={{0,1},{1,0},{2,3},{3,2},{4,5},{5,4},{6,7},{7,6},{8,9},{9,8},{10,11... | collective-permute-start | bytes 1572872 | tf_op jit(solution)/shard_map/ppermute | solution.py:41
  55.0 21.3 %copy-start.5 = (bf16[4,2,256,128]{3,2,1,0:T(8,128)(2,1)}, bf16[4,2,256,128]{3,2,1,0:T(8,128)(2,1)S(1)}, u32[]{:S(2)}) copy-start(bf16[4,2,256,128]{3,2,1,0:T(8,128)(2,1)S(1)} %collective-permute-done.4.refs_2_) | copy-start | bytes 1572868
  55.0 6.9 %collective-permute-start.6 = (bf16[2,2,256,128]{3,2,1,0:T(8,128)(2,1)S(1)}, bf16[2,2,256,128]{3,2,1,0:T(8,128)(2,1)S(1)}, u32[]{:S(2)}, u32[]{:S(2)}) collective-permute-start(bf16[2,2,256,128]{3,2,1,0:T(8,128)(2,1)S(1)} %slice.65), channel_id=1, source_target_pairs={{0,2},{1,3},{2,4},{3,5},{4,6},{5,7},{6,0},{7,1},{8,10},{9,11},{10,... | collective-permute-start | bytes 786440 | tf_op jit(solution)/shard_map/ppermute | solution.py:41
  56.4 9.1 %collective-permute-start.9 = (bf16[4,2,256,128]{3,2,1,0:T(8,128)(2,1)S(1)}, bf16[4,2,256,128]{3,2,1,0:T(8,128)(2,1)S(1)}, u32[]{:S(2)}, u32[]{:S(2)}) collective-permute-start(bf16[4,2,256,128]{3,2,1,0:T(8,128)(2,1)S(1)} %collective-permute-done.4.refs_2_), channel_id=1, source_target_pairs={{0,1},{1,0},{2,3},{3,2},{4,5},{5,4},{6,7},{7,6},{8,9},{9,8},{10,11... | collective-permute-start | bytes 1572872 | tf_op jit(solution)/shard_map/ppermute | solution.py:41
  56.4 19.9 %copy-start.8 = (bf16[4,2,256,128]{3,2,1,0:T(8,128)(2,1)}, bf16[4,2,256,128]{3,2,1,0:T(8,128)(2,1)S(1)}, u32[]{:S(2)}) copy-start(bf16[4,2,256,128]{3,2,1,0:T(8,128)(2,1)S(1)} %collective-permute-done.5.refs_3_) | copy-start | bytes 1572868
  56.4 9.1 %collective-permute-start.10 = (bf16[4,2,256,128]{3,2,1,0:T(8,128)(2,1)S(1)}, bf16[4,2,256,128]{3,2,1,0:T(8,128)(2,1)S(1)}, u32[]{:S(2)}, u32[]{:S(2)}) collective-permute-start(bf16[4,2,256,128]{3,2,1,0:T(8,128)(2,1)S(1)} %collective-permute-done.5.refs_3_), channel_id=1, source_target_pairs={{0,1},{1,0},{2,3},{3,2},{4,5},{5,4},{6,7},{7,6},{8,9},{9,8},{10,11... | collective-permute-start | bytes 1572872 | tf_op jit(solution)/shard_map/ppermute | solution.py:41
  57.0 8.4 %collective-permute-start.7 = (bf16[2,2,256,128]{3,2,1,0:T(8,128)(2,1)S(1)}, bf16[2,2,256,128]{3,2,1,0:T(8,128)(2,1)}, u32[]{:S(2)}, u32[]{:S(2)}) collective-permute-start(bf16[2,2,256,128]{3,2,1,0:T(8,128)(2,1)S(1)} %slice.66), channel_id=1, source_target_pairs={{0,6},{1,7},{2,0},{3,1},{4,2},{5,3},{6,4},{7,5},{8,14},{9,15},{10,... | collective-permute-start | bytes 786440 | tf_op jit(solution)/shard_map/ppermute | solution.py:41
  62.0 3.6 %collective-permute-start.11 = (bf16[2,2,256,128]{3,2,1,0:T(8,128)(2,1)S(1)}, bf16[2,2,256,128]{3,2,1,0:T(8,128)(2,1)}, u32[]{:S(2)}, u32[]{:S(2)}) collective-permute-start(bf16[2,2,256,128]{3,2,1,0:T(8,128)(2,1)S(1)} %collective-permute-done.6.refs_4_), channel_id=1, source_target_pairs={{0,1},{1,0},{2,3},{3,2},{4,5},{5,4},{6,7},{7,6},{8,9},{9,8},{10,11... | collective-permute-start | bytes 786440 | tf_op jit(solution)/shard_map/ppermute | solution.py:41
  65.4 1.9 collective-permute-start.12
  65.5 10.8 %copy-start.11 = (bf16[4,2,256,128]{3,2,1,0:T(8,128)(2,1)}, bf16[4,2,256,128]{3,2,1,0:T(8,128)(2,1)S(1)}, u32[]{:S(2)}) copy-start(bf16[4,2,256,128]{3,2,1,0:T(8,128)(2,1)S(1)} %collective-permute-done.8.refs_6_) | copy-start | bytes 1572868
  65.5 10.8 %copy-start.14 = (bf16[4,2,256,128]{3,2,1,0:T(8,128)(2,1)}, bf16[4,2,256,128]{3,2,1,0:T(8,128)(2,1)S(1)}, u32[]{:S(2)}) copy-start(bf16[4,2,256,128]{3,2,1,0:T(8,128)(2,1)S(1)} %collective-permute-done.9.refs_7_) | copy-start | bytes 1572868
  65.6 10.8 %copy-start.17 = (bf16[4,2,256,128]{3,2,1,0:T(8,128)(2,1)}, bf16[4,2,256,128]{3,2,1,0:T(8,128)(2,1)S(1)}, u32[]{:S(2)}) copy-start(bf16[4,2,256,128]{3,2,1,0:T(8,128)(2,1)S(1)} %collective-permute-done.10.refs_8_) | copy-start | bytes 1572868
  67.3 1.9 copy-start
  71.5 17.3 %collective-permute-start.13 = (bf16[3,256,256]{2,1,0:T(8,128)(2,1)S(1)}, bf16[3,256,256]{2,1,0:T(8,128)(2,1)}, u32[]{:S(2)}, u32[]{:S(2)}) collective-permute-start(bf16[3,256,256]{2,1,0:T(8,128)(2,1)S(1)} %partial_sent.1), channel_id=1, source_target_pairs={{0,32},{1,33},{2,34},{3,35},{4,36},{5,37},{6,38},{7,39},{8,40},{9,... | collective-permute-start | bytes 1179656 | tf_op jit(solution)/shard_map/ppermute | solution.py:41
  78.8 0.9 copy-start.23
  91.0 14.1 %copy-start.1 = (bf16[6144,256]{1,0:T(8,128)(2,1)S(1)}, bf16[6144,256]{1,0:T(8,128)(2,1)}, u32[]{:S(2)}) copy-start(bf16[6144,256]{1,0:T(8,128)(2,1)} %all-gather.2.cloned.1.call-done) | copy-start | bytes 9437188
  91.0 17.5 %collective-permute-start.14 = (bf16[3,256,256]{2,1,0:T(8,128)(2,1)}, bf16[3,256,256]{2,1,0:T(8,128)(2,1)S(1)}, u32[]{:S(2)}, u32[]{:S(2)}) collective-permute-start(bf16[3,256,256]{2,1,0:T(8,128)(2,1)} %gated.1.refs_11_.refs_1_), channel_id=1, source_target_pairs={{0,32},{1,33},{2,34},{3,35},{4,36},{5,37},{6,38},{7,39},{8,40},{9,... | collective-permute-start | bytes 1179656 | tf_op jit(solution)/shard_map/ppermute | solution.py:41
  95.5 1.0 copy-start.3
  96.5 1.0 copy-start.6
  97.6 1.0 copy-start.9
  98.6 1.0 copy-start.12
  99.7 1.0 copy-start.15
  100.7 1.0 copy-start.18
  101.8 1.0 copy-start.22
  105.1 4.4 %copy-start.7 = (bf16[4,2,256,128]{3,2,1,0:T(8,128)(2,1)S(1)}, bf16[4,2,256,128]{3,2,1,0:T(8,128)(2,1)}, u32[]{:S(2)}) copy-start(bf16[4,2,256,128]{3,2,1,0:T(8,128)(2,1)} %copy-done.5) | copy-start | bytes 1572868
  105.1 4.3 %copy-start.10 = (bf16[4,2,256,128]{3,2,1,0:T(8,128)(2,1)S(1)}, bf16[4,2,256,128]{3,2,1,0:T(8,128)(2,1)}, u32[]{:S(2)}) copy-start(bf16[4,2,256,128]{3,2,1,0:T(8,128)(2,1)} %copy-done.8) | copy-start | bytes 1572868
  105.2 4.3 %copy-start.13 = (bf16[4,2,256,128]{3,2,1,0:T(8,128)(2,1)S(1)}, bf16[4,2,256,128]{3,2,1,0:T(8,128)(2,1)}, u32[]{:S(2)}) copy-start(bf16[4,2,256,128]{3,2,1,0:T(8,128)(2,1)} %copy-done.11) | copy-start | bytes 1572868
  105.2 4.3 %copy-start.16 = (bf16[4,2,256,128]{3,2,1,0:T(8,128)(2,1)S(1)}, bf16[4,2,256,128]{3,2,1,0:T(8,128)(2,1)}, u32[]{:S(2)}) copy-start(bf16[4,2,256,128]{3,2,1,0:T(8,128)(2,1)} %copy-done.14) | copy-start | bytes 1572868
  105.2 4.3 %copy-start.19 = (bf16[4,2,256,128]{3,2,1,0:T(8,128)(2,1)S(1)}, bf16[4,2,256,128]{3,2,1,0:T(8,128)(2,1)}, u32[]{:S(2)}) copy-start(bf16[4,2,256,128]{3,2,1,0:T(8,128)(2,1)} %copy-done.17) | copy-start | bytes 1572868
  107.5 1.0 copy-start.24
  108.5 1.0 copy-start.26
  109.5 2.6 %copy-start.20 = (bf16[3,256,256]{2,1,0:T(8,128)(2,1)}, bf16[3,256,256]{2,1,0:T(8,128)(2,1)S(1)}, u32[]{:S(2)}) copy-start(bf16[3,256,256]{2,1,0:T(8,128)(2,1)S(1)} %collective-permute-done.14.refs_1_.refs_11_) | copy-start | bytes 1179652
  112.1 1.6 copy-start.4
  113.7 1.0 copy-start.21
  113.8 4.4 %collective-permute-start.15 = (bf16[2,4,2,256,128]{4,3,2,1,0:T(8,128)(2,1)}, bf16[2,4,2,256,128]{4,3,2,1,0:T(8,128)(2,1)S(1)}, u32[]{:S(2)}, u32[]{:S(2)}) collective-permute-start(bf16[2,4,2,256,128]{4,3,2,1,0:T(8,128)(2,1)} %copy-done.26), channel_id=1, source_target_pairs={{0,1},{1,0},{2,3},{3,2},{4,5},{5,4},{6,7},{7,6},{8,9},{9,8},{10,11... | collective-permute-start | bytes 3145736 | tf_op jit(solution)/shard_map/ppermute | solution.py:41
  116.3 3.0 %copy-start.25 = (bf16[2,4,2,256,128]{4,3,2,1,0:T(8,128)(2,1)S(1)}, bf16[2,4,2,256,128]{4,3,2,1,0:T(8,128)(2,1)}, u32[]{:S(2)}) copy-start(bf16[2,4,2,256,128]{4,3,2,1,0:T(8,128)(2,1)} %copy-done.24) | copy-start | bytes 3145732
  116.3 3.0 %collective-permute-start.16 = (bf16[2,4,2,256,128]{4,3,2,1,0:T(8,128)(2,1)S(1)}, bf16[2,4,2,256,128]{4,3,2,1,0:T(8,128)(2,1)S(1)}, u32[]{:S(2)}, u32[]{:S(2)}) collective-permute-start(bf16[2,4,2,256,128]{4,3,2,1,0:T(8,128)(2,1)S(1)} %outputs_sent.1), channel_id=1, source_target_pairs={{0,1},{1,0},{2,3},{3,2},{4,5},{5,4},{6,7},{7,6},{8,9},{9,8},{10,11... | collective-permute-start | bytes 3145736 | tf_op jit(solution)/shard_map/ppermute | solution.py:41
  120.4 9.6 %collective-permute-start.17 = (bf16[2,2,256,128]{3,2,1,0:T(8,128)(2,1)S(1)}, bf16[2,2,256,128]{3,2,1,0:T(8,128)(2,1)S(1)}, u32[]{:S(2)}, u32[]{:S(2)}) collective-permute-start(bf16[2,2,256,128]{3,2,1,0:T(8,128)(2,1)S(1)} %get-tuple-element.44), channel_id=1, source_target_pairs={{0,2},{1,3},{2,4},{3,5},{4,6},{5,7},{6,0},{7,1},{8,10},{9,11},{10,... | collective-permute-start | bytes 786440 | tf_op jit(solution)/shard_map/ppermute | solution.py:41
  124.1 8.1 %collective-permute-start.19 = (bf16[2,2,256,128]{3,2,1,0:T(8,128)(2,1)S(1)}, bf16[2,2,256,128]{3,2,1,0:T(8,128)(2,1)S(1)}, u32[]{:S(2)}, u32[]{:S(2)}) collective-permute-start(bf16[2,2,256,128]{3,2,1,0:T(8,128)(2,1)S(1)} %get-tuple-element.45), channel_id=1, source_target_pairs={{0,6},{1,7},{2,0},{3,1},{4,2},{5,3},{6,4},{7,5},{8,14},{9,15},{10,... | collective-permute-start | bytes 786440 | tf_op jit(solution)/shard_map/ppermute | solution.py:41
  132.4 13.1 %collective-permute-start.20 = (bf16[4,2,256,128]{3,2,1,0:T(8,128)(2,1)S(1)}, bf16[4,2,256,128]{3,2,1,0:T(8,128)(2,1)S(1)}, u32[]{:S(2)}, u32[]{:S(2)}) collective-permute-start(bf16[4,2,256,128]{3,2,1,0:T(8,128)(2,1)S(1)} %pad_maximum_fusion.2), channel_id=1, source_target_pairs={{0,6},{1,7},{2,0},{3,1},{4,2},{5,3},{6,4},{7,5},{8,14},{9,15},{10,... | collective-permute-start | bytes 1572872 | tf_op jit(solution)/shard_map/ppermute | solution.py:41
  132.8 12.9 %collective-permute-start.18 = (bf16[4,2,256,128]{3,2,1,0:T(8,128)(2,1)S(1)}, bf16[4,2,256,128]{3,2,1,0:T(8,128)(2,1)S(1)}, u32[]{:S(2)}, u32[]{:S(2)}) collective-permute-start(bf16[4,2,256,128]{3,2,1,0:T(8,128)(2,1)S(1)} %pad_maximum_fusion.1), channel_id=1, source_target_pairs={{0,2},{1,3},{2,4},{3,5},{4,6},{5,7},{6,0},{7,1},{8,10},{9,11},{10,... | collective-permute-start | bytes 1572872 | tf_op jit(solution)/shard_map/ppermute | solution.py:41
  146.0 10.3 %collective-permute-start.23 = (bf16[2,256,128]{2,1,0:T(8,128)(2,1)S(1)}, bf16[2,256,128]{2,1,0:T(8,128)(2,1)S(1)}, u32[]{:S(2)}, u32[]{:S(2)}) collective-permute-start(bf16[2,256,128]{2,1,0:T(8,128)(2,1)S(1)} %get-tuple-element.49), channel_id=1, source_target_pairs={{0,24},{1,25},{2,26},{3,27},{4,28},{5,29},{6,30},{7,31},{8,0},{9,1... | collective-permute-start | bytes 393224 | tf_op jit(solution)/shard_map/ppermute | solution.py:41
  146.1 18.6 %collective-permute-start.22 = (bf16[2,256,128]{2,1,0:T(8,128)(2,1)S(1)}, bf16[2,256,128]{2,1,0:T(8,128)(2,1)S(1)}, u32[]{:S(2)}, u32[]{:S(2)}) collective-permute-start(bf16[2,256,128]{2,1,0:T(8,128)(2,1)S(1)} %get-tuple-element.50), channel_id=1, source_target_pairs={{0,16},{1,17},{2,18},{3,19},{4,20},{5,21},{6,22},{7,23},{8,24},{9,... | collective-permute-start | bytes 393224 | tf_op jit(solution)/shard_map/ppermute | solution.py:41
  154.4 10.4 %collective-permute-start.21 = (bf16[2,256,128]{2,1,0:T(8,128)(2,1)S(1)}, bf16[2,256,128]{2,1,0:T(8,128)(2,1)S(1)}, u32[]{:S(2)}, u32[]{:S(2)}) collective-permute-start(bf16[2,256,128]{2,1,0:T(8,128)(2,1)S(1)} %get-tuple-element.48), channel_id=1, source_target_pairs={{0,8},{1,9},{2,10},{3,11},{4,12},{5,13},{6,14},{7,15},{8,16},{9,17... | collective-permute-start | bytes 393224 | tf_op jit(solution)/shard_map/ppermute | solution.py:41
  164.8 18.5 %collective-permute-start.24 = (bf16[2,256,128]{2,1,0:T(8,128)(2,1)S(1)}, bf16[2,256,128]{2,1,0:T(8,128)(2,1)S(1)}, u32[]{:S(2)}, u32[]{:S(2)}) collective-permute-start(bf16[2,256,128]{2,1,0:T(8,128)(2,1)S(1)} %fusion.6), channel_id=1, source_target_pairs={{0,0},{1,1},{2,2},{3,3},{4,32},{5,33},{6,34},{7,35},{8,8},{9,9},{1... | collective-permute-start | bytes 393224 | tf_op jit(solution)/shard_map/ppermute | solution.py:41
Sparse Core Ops, SparseCore 0:
  10.9 43.0 all-gather.1
  113.9 44.7 reduce-scatter.1

commit v3 on v2

--- a/solution.py
+++ b/solution.py
@@ -61,8 +61,16 @@
     return (x, hi, lo, y, 1 - core)
 
 
-def swap_hi_y(x, hi, lo, y, core):
-    return (x, y >> 1, lo, hi * 2 + (y & 1), core)
+def to_half(x, hi, lo, y, core):
+    if hi != y >> 1:
+        return (x, 1 - hi, lo, y, core)
+    return (x, hi, lo, y ^ 2, core)
+
+
+def from_half(x, hi, lo, y, core):
+    if hi != y >> 1:
+        return (x, hi, lo, y ^ 2, core)
+    return (x, 1 - hi, lo, y, core)
 
 
 def power_of_two(expo, sign):
@@ -138,14 +146,14 @@
 
 def gu_update(grads, master, first, second, codes, expo):
     parts, rows, cols = master.shape
-    size = rows // 2
+    size = rows
     block = pl.BlockSpec((1, size, cols), lambda i, j: (i, j, 0))
     narrow = pl.BlockSpec((1, size // 4, cols), lambda i, j: (i, j, 0))
     whole = pl.BlockSpec((parts, cols), lambda i, j: (0, 0))
     like = jax.ShapeDtypeStruct(master.shape, F32)
     return pl.pallas_call(
         gu_adam_kernel,
-        grid=(parts, 2),
+        grid=(parts, 1),
         in_specs=[block, block, block, block, narrow, whole],
         out_specs=[block] * 4,
         out_shape=[like, like, like, jax.ShapeDtypeStruct(master.shape, BF16)],
@@ -200,7 +208,7 @@
     own, other, weights, out = refs[:5], refs[5:10], refs[10], refs[11]
     acc = refs[12]
     hi, lo, y, core = place[1], place[2], place[3], place[4]
-    target = hi if mine else 1 - hi
+    target = 1 - hi if mine else hi
     acc[...] = jnp.zeros_like(acc)
     for ring, offset in enumerate(Y_OFFSETS):
         from_y = (y + offset) & 3
@@ -288,11 +296,11 @@
         to_y = (y + step) & 3
         low = to_y & 1
 
-        @pl.when((to_y >> 1) == hi)
+        @pl.when((to_y >> 1) != hi)
         def _():
             out[step] = (own_kept[low].astype(F32) + own_got[low].astype(F32)).astype(BF16)
 
-        @pl.when((to_y >> 1) != hi)
+        @pl.when((to_y >> 1) == hi)
         def _():
             out[step] = (arrived_kept[low].astype(F32) + arrived_got[low].astype(F32)).astype(BF16)
 
@@ -311,7 +319,7 @@
 def grads_kernel(own_rows, inverse_scale, place, *refs):
     own, other, rows, out = refs[:5], refs[5:10], refs[10], refs[-1]
     hi, lo, y, core = place[1], place[2], place[3], place[4]
-    target = hi if own_rows else 1 - hi
+    target = 1 - hi if own_rows else hi
     for ring, offset in enumerate(Y_OFFSETS):
         from_y = (y + offset) & 3
 
@@ -345,15 +353,16 @@
     )(place, *pieces, rows, *before)
 
 
-def gather_pieces(tokens, cotangent):
-    start = move(jnp.stack([tokens, cotangent]), swap_hi_y)
+def gather_pieces(tokens, cotangent, weights):
+    start = move(jnp.stack([tokens, cotangent]), to_half)
     line = jnp.stack([start] + [move(start, along_lo(step)) for step in (1, 2, 3)])
     before = move(line, along_y(1))
     after = move(line, along_y(-1))
     far_low = move(before[:2], along_y(1))
     far_high = move(after[2:], along_y(-1))
+    far_high, weights = lax.optimization_barrier((far_high, weights))
     own = (line, before, after, far_low, far_high)
-    return own + tuple(move(piece, other_core) for piece in own)
+    return own + tuple(move(piece, other_core) for piece in own), weights
 
 
 def scatter_outputs(total):
@@ -399,7 +408,7 @@
     weights = lax.all_gather(
         quant.reshape(1536, 256), "dp", axis=0, tiled=True, axis_index_groups=X_GROUPS
     ).reshape(4, 3, 512, 256)
-    pieces = gather_pieces(tokens, cotangent)
+    pieces, weights = gather_pieces(tokens, cotangent, weights)
     sent = partial(False, place, pieces, weights)
     arrived = move(sent, other_hi)
     kept = partial(True, place, pieces, weights)
@@ -425,7 +434,7 @@
     down_new, down_first_new, down_second_new, down_copy = down_update(
         grad, down_master, down_first, down_second, down_codes, down_expo
     )
-    both = after(move(both, swap_hi_y), gu_copy, down_copy)
+    both = after(move(both, from_half), gu_copy, down_copy)
     return (
         both[0],
         both[1],

time: 192 us -> 182 us (0.948)
  the two profiles are of different devices: /device:TPU:22 before, /device:TPU:2 now
where the time goes in v3:
time: 182 us; the launch traced here: 181 us
  waiting for transfers between devices  75.7 us (42%)
  starting transfers between devices  45.7 us (25%)
  Pallas kernels  29.8 us (16%)
  local copies, waits for them, and re-layouts  15.2 us (8%)
  between operations  14.4 us (8%)
    ppermute x25, waiting for transfers between devices, move(): return lax.ppermute(value, ALL, pairs)  75.6 us
    ppermute x25, starting transfers between devices, move(): return lax.ppermute(value, ALL, pairs)  45.6 us
    unnamed x58, local copies, waits for them, and re-layouts  14.3 us
    pallas_call x3, Pallas kernels, outputs(): pl.pallas_call(lambda *refs: outputs_kernel(sides, *refs), in_specs=[SMEM...  5.39 us
    pallas_call x2, Pallas kernels, grads(): pl.pallas_call(lambda *refs: grads_kernel(own_rows, inverse_scale, *refs)...  4.93 us
    pallas_call x2, Pallas kernels, partial(): pl.pallas_call(lambda *refs: partial_kernel(mine, *refs), in_specs=[SMEM]...  4.9 us
    pallas_call x1, Pallas kernels, gu_update(): pl.pallas_call(gu_adam_kernel, grid=(parts, 1), in_specs=[block, block, b...  4.68 us
  transfers between devices with their start and end apart: 27, of which 16 were waited for; matrix products, arithmetic and copies ran while one was open for 0% of the time, Pallas kernels for 11%

profile of v3, /device:TPU:2, one launch (start us, length us, event | category | flops | bytes accessed | tf_op | source)
XLA Modules:
  0.0 181.3 jit_solution(3806919144736752810)
XLA Ops:
  7.2 3.5 %quantize.1 = bf16[3,512,256]{2,1,0:T(8,128)(2,1)} custom-call(f32[2,512,256]{2,1,0:T(8,128)} %master.2, s32[2,128,256]{2,1,0:T(8,128)} %codes.2, s32[2,256]{1,0:T(2,128)} %expo.1, f32[256,512]{1,0:T(8,128)} %master.3, s32[64,512]{1,0:T(8,128)} %codes.3, s32[1,512]{1,0:T(1,128)} %bitcast.75), custom_call_target="tpu_custom_call" | custom-call | tf_op jit(solution)/shard_map/quantize/pallas_call | solution.py:401
  10.8 3.3 %collective-permute-start = (bf16[2,256,128]{2,1,0:T(8,128)(2,1)S(1)}, bf16[2,256,128]{2,1,0:T(8,128)(2,1)S(1)}, u32[]{:S(2)}, u32[]{:S(2)}) collective-permute-start(bf16[2,256,128]{2,1,0:T(8,128)(2,1)S(1)} %pad_maximum_fusion.3), channel_id=1, source_target_pairs={{0,4},{1,5},{2,6},{3,7},{4,36},{5,37},{6,38},{7,39},{8,12},{9,13},... | collective-permute-start | bytes 393224 | tf_op jit(solution)/shard_map/ppermute | solution.py:41
  14.1 7.6 %collective-permute-done = bf16[2,256,128]{2,1,0:T(8,128)(2,1)S(1)} collective-permute-done((bf16[2,256,128]{2,1,0:T(8,128)(2,1)S(1)}, bf16[2,256,128]{2,1,0:T(8,128)(2,1)S(1)}, u32[]{:S(2)}, u32[]{:S(2)}) %collective-permute-start) | collective-permute-done | bytes 131104 | tf_op jit(solution)/shard_map/ppermute | solution.py:41
  21.7 3.1 %collective-permute-start.3 = (bf16[2,256,128]{2,1,0:T(8,128)(2,1)S(1)}, bf16[2,256,128]{2,1,0:T(8,128)(2,1)S(1)}, u32[]{:S(2)}, u32[]{:S(2)}) collective-permute-start(bf16[2,256,128]{2,1,0:T(8,128)(2,1)S(1)} %collective-permute-done), channel_id=1, source_target_pairs={{0,24},{1,25},{2,26},{3,27},{4,28},{5,29},{6,30},{7,31},{8,0},{9,1... | collective-permute-start | bytes 393224 | tf_op jit(solution)/shard_map/ppermute | solution.py:41
  24.8 2.1 %collective-permute-start.2 = (bf16[2,256,128]{2,1,0:T(8,128)(2,1)S(1)}, bf16[2,256,128]{2,1,0:T(8,128)(2,1)S(1)}, u32[]{:S(2)}, u32[]{:S(2)}) collective-permute-start(bf16[2,256,128]{2,1,0:T(8,128)(2,1)S(1)} %collective-permute-done), channel_id=1, source_target_pairs={{0,16},{1,17},{2,18},{3,19},{4,20},{5,21},{6,22},{7,23},{8,24},{9,... | collective-permute-start | bytes 393224 | tf_op jit(solution)/shard_map/ppermute | solution.py:41
  26.9 1.3 collective-permute-start.1
  28.2 1.2 collective-permute-done.3
  29.4 8.2 %collective-permute-done.2 = bf16[2,256,128]{2,1,0:T(8,128)(2,1)S(1)} collective-permute-done((bf16[2,256,128]{2,1,0:T(8,128)(2,1)S(1)}, bf16[2,256,128]{2,1,0:T(8,128)(2,1)S(1)}, u32[]{:S(2)}, u32[]{:S(2)}) %collective-permute-start.2) | collective-permute-done | bytes 131104 | tf_op jit(solution)/shard_map/ppermute | solution.py:41
  37.7 1.7 collective-permute-start.4
  39.3 1.7 collective-permute-start.5
  41.0 8.8 %collective-permute-done.4.refs_2_ = bf16[4,2,256,128]{3,2,1,0:T(8,128)(2,1)S(1)} collective-permute-done((bf16[4,2,256,128]{3,2,1,0:T(8,128)(2,1)S(1)}, bf16[4,2,256,128]{3,2,1,0:T(8,128)(2,1)S(1)}, u32[]{:S(2)}, u32[]{:S(2)}) %collective-permute-start.4) | collective-permute-done | bytes 524320 | tf_op jit(solution)/shard_map/ppermute | solution.py:41
  49.8 1.5 collective-permute-start.6
  51.3 1.8 %collective-permute-start.7 = (bf16[2,2,256,128]{3,2,1,0:T(8,128)(2,1)S(1)}, bf16[2,2,256,128]{3,2,1,0:T(8,128)(2,1)}, u32[]{:S(2)}, u32[]{:S(2)}) collective-permute-start(bf16[2,2,256,128]{3,2,1,0:T(8,128)(2,1)S(1)} %slice.66), channel_id=1, source_target_pairs={{0,6},{1,7},{2,0},{3,1},{4,2},{5,3},{6,4},{7,5},{8,14},{9,15},{10,... | collective-permute-start | bytes 786440 | tf_op jit(solution)/shard_map/ppermute | solution.py:41
  53.2 0.5 collective-permute-start.9
  53.7 3.7 %collective-permute-done.6.refs_4_ = bf16[2,2,256,128]{3,2,1,0:T(8,128)(2,1)S(1)} collective-permute-done((bf16[2,2,256,128]{3,2,1,0:T(8,128)(2,1)S(1)}, bf16[2,2,256,128]{3,2,1,0:T(8,128)(2,1)S(1)}, u32[]{:S(2)}, u32[]{:S(2)}) %collective-permute-start.6) | collective-permute-done | bytes 262176 | tf_op jit(solution)/shard_map/ppermute | solution.py:41
  57.4 0.5 collective-permute-done.7.refs_5_
  58.1 1.0 collective-permute-done.11.refs_9_
  59.1 0.7 collective-permute-done.12.refs_10_
  59.8 1.9 %copy-done = bf16[6144,256]{1,0:T(8,128)(2,1)S(1)} copy-done((bf16[6144,256]{1,0:T(8,128)(2,1)S(1)}, bf16[6144,256]{1,0:T(8,128)(2,1)}, u32[]{:S(2)}) %copy-start) | copy-done | bytes 3145752
  61.7 2.5 %partial_sent.1 = bf16[3,256,256]{2,1,0:T(8,128)(2,1)S(1)} custom-call(s32[5]{0:T(128)S(1)} %stack.47.refs_0_.place, bf16[4,2,256,128]{3,2,1,0:T(8,128)(2,1)S(1)} %pad_maximum_fusion.refs_1_, bf16[4,2,256,128]{3,2,1,0:T(8,128)(2,1)S(1)} %collective-permute-done.4.refs_2_, bf16[4,2,256,128]{3,2,1,0:T(8,128)(2,1)S(1)} %collective-permute-done.5.refs_3_, ...), custom_call_target="tpu_custom_call" | custom-call | tf_op jit(solution)/shard_map/partial_sent/pallas_call | solution.py:229
  64.2 5.9 %collective-permute-start.13 = (bf16[3,256,256]{2,1,0:T(8,128)(2,1)S(1)}, bf16[3,256,256]{2,1,0:T(8,128)(2,1)}, u32[]{:S(2)}, u32[]{:S(2)}) collective-permute-start(bf16[3,256,256]{2,1,0:T(8,128)(2,1)S(1)} %partial_sent.1), channel_id=1, source_target_pairs={{0,32},{1,33},{2,34},{3,35},{4,36},{5,37},{6,38},{7,39},{8,40},{9,... | collective-permute-start | bytes 1179656 | tf_op jit(solution)/shard_map/ppermute | solution.py:41
  70.2 2.4 %partial_own.1.own = f32[3,256,256]{2,1,0:T(8,128)S(1)} custom-call(s32[5]{0:T(128)S(1)} %stack.47.refs_0_.place, bf16[4,2,256,128]{3,2,1,0:T(8,128)(2,1)S(1)} %pad_maximum_fusion.refs_1_, bf16[4,2,256,128]{3,2,1,0:T(8,128)(2,1)S(1)} %collective-permute-done.4.refs_2_, bf16[4,2,256,128]{3,2,1,0:T(8,128)(2,1)S(1)} %collective-permute-done.5.refs_3_, ...), custom_call_target="tpu_custom_call" | custom-call | tf_op jit(solution)/shard_map/partial_own/pallas_call | solution.py:229
  72.6 0.9 copy-done.23
  73.4 13.9 %collective-permute-done.13.sent = bf16[3,256,256]{2,1,0:T(8,128)(2,1)} collective-permute-done((bf16[3,256,256]{2,1,0:T(8,128)(2,1)S(1)}, bf16[3,256,256]{2,1,0:T(8,128)(2,1)}, u32[]{:S(2)}, u32[]{:S(2)}) %collective-permute-start.13) | collective-permute-done | bytes 393248 | tf_op jit(solution)/shard_map/ppermute | solution.py:41
  87.3 2.2 %gated.1.refs_11_.refs_1_ = bf16[3,256,256]{2,1,0:T(8,128)(2,1)} custom-call(f32[3,256,256]{2,1,0:T(8,128)} %copy-done.23, bf16[3,256,256]{2,1,0:T(8,128)(2,1)} %collective-permute-done.13.sent), custom_call_target="tpu_custom_call" | custom-call | tf_op jit(solution)/shard_map/gated/pallas_call | solution.py:252
  89.5 6.5 %collective-permute-start.14 = (bf16[3,256,256]{2,1,0:T(8,128)(2,1)}, bf16[3,256,256]{2,1,0:T(8,128)(2,1)S(1)}, u32[]{:S(2)}, u32[]{:S(2)}) collective-permute-start(bf16[3,256,256]{2,1,0:T(8,128)(2,1)} %gated.1.refs_11_.refs_1_), channel_id=1, source_target_pairs={{0,32},{1,33},{2,34},{3,35},{4,36},{5,37},{6,38},{7,39},{8,40},{9,... | collective-permute-start | bytes 1179656 | tf_op jit(solution)/shard_map/ppermute | solution.py:41
  96.0 1.0 copy-done.3
  97.0 1.0 copy-done.6
  98.1 1.0 copy-done.9
  99.1 1.0 copy-done.12
  100.2 1.0 copy-done.15
  101.2 1.0 copy-done.18
  102.2 1.0 copy-done.22
  103.2 2.4 %own_grads.1.refs_12_ = bf16[4,3,512,256]{3,2,1,0:T(8,128)(2,1)S(1)} custom-call(s32[5]{0:T(128)S(1)} %stack.47.refs_0_.place, bf16[4,2,256,128]{3,2,1,0:T(8,128)(2,1)S(1)} %copy-done.3, bf16[4,2,256,128]{3,2,1,0:T(8,128)(2,1)S(1)} %copy-done.6, bf16[4,2,256,128]{3,2,1,0:T(8,128)(2,1)S(1)} %copy-done.9, ...), custom_call_target="tpu_custom_call" | custom-call | tf_op jit(solution)/shard_map/own_grads/pallas_call | solution.py:346
  105.7 2.3 %outputs_sent_kept.1 = (bf16[2,4,2,256,128]{4,3,2,1,0:T(8,128)(2,1)S(1)}, bf16[2,4,2,256,128]{4,3,2,1,0:T(8,128)(2,1)S(1)}) custom-call(s32[5]{0:T(128)S(1)} %stack.47.refs_0_.place, bf16[3,256,256]{2,1,0:T(8,128)(2,1)S(1)} %copy-done.22, bf16[4,3,512,256]{3,2,1,0:T(8,128)(2,1)S(1)} %bitcast.62), custom_call_target="tpu_custom_call" | custom-call | tf_op jit(solution)/shard_map/outputs_sent_kept/pallas_call | solution.py:283
  108.0 1.0 copy-done.24
  109.0 0.2 collective-permute-done.14.refs_1_.refs_11_
  109.2 0.7 copy-done.26
  110.0 2.6 %arrived_grads.1 = bf16[4,3,512,256]{3,2,1,0:T(8,128)(2,1)S(1)} custom-call(s32[5]{0:T(128)S(1)} %stack.47.refs_0_.place, bf16[4,2,256,128]{3,2,1,0:T(8,128)(2,1)S(1)} %copy-done.3, bf16[4,2,256,128]{3,2,1,0:T(8,128)(2,1)S(1)} %copy-done.7, bf16[4,2,256,128]{3,2,1,0:T(8,128)(2,1)S(1)} %copy-done.10, ...), custom_call_target="tpu_custom_call" | custom-call | tf_op jit(solution)/shard_map/arrived_grads/pallas_call | solution.py:346
  112.6 1.6 copy-done.4
  114.2 0.1 collective-permute-start.15
  114.3 0.9 copy-done.21
  115.2 1.5 outputs_sent.1
  116.7 0.3 collective-permute-start.16
  117.1 1.5 outputs_kept.1.arrived_kept
  118.6 1.1 collective-permute-done.16.arrived_got
  119.7 1.1 combine.1
  120.8 0.1 slice_bitcast_fusion.6
  120.9 1.7 collective-permute-start.17
  122.6 1.8 %collective-permute-start.19 = (bf16[2,2,256,128]{3,2,1,0:T(8,128)(2,1)S(1)}, bf16[2,2,256,128]{3,2,1,0:T(8,128)(2,1)S(1)}, u32[]{:S(2)}, u32[]{:S(2)}) collective-permute-start(bf16[2,2,256,128]{3,2,1,0:T(8,128)(2,1)S(1)} %get-tuple-element.49), channel_id=1, source_target_pairs={{0,6},{1,7},{2,0},{3,1},{4,2},{5,3},{6,4},{7,5},{8,14},{9,15},{10,... | collective-permute-start | bytes 786440 | tf_op jit(solution)/shard_map/ppermute | solution.py:41
  124.4 6.5 %collective-permute-done.17 = bf16[2,2,256,128]{3,2,1,0:T(8,128)(2,1)S(1)} collective-permute-done((bf16[2,2,256,128]{3,2,1,0:T(8,128)(2,1)S(1)}, bf16[2,2,256,128]{3,2,1,0:T(8,128)(2,1)S(1)}, u32[]{:S(2)}, u32[]{:S(2)}) %collective-permute-start.17) | collective-permute-done | bytes 262176 | tf_op jit(solution)/shard_map/ppermute | solution.py:41
  130.9 0.1 fusion.2
  131.1 3.1 %collective-permute-start.20 = (bf16[4,2,256,128]{3,2,1,0:T(8,128)(2,1)S(1)}, bf16[4,2,256,128]{3,2,1,0:T(8,128)(2,1)S(1)}, u32[]{:S(2)}, u32[]{:S(2)}) collective-permute-start(bf16[4,2,256,128]{3,2,1,0:T(8,128)(2,1)S(1)} %pad_maximum_fusion.2), channel_id=1, source_target_pairs={{0,6},{1,7},{2,0},{3,1},{4,2},{5,3},{6,4},{7,5},{8,14},{9,15},{10,... | collective-permute-start | bytes 1572872 | tf_op jit(solution)/shard_map/ppermute | solution.py:41
  134.4 10.5 %collective-permute-done.20 = bf16[4,2,256,128]{3,2,1,0:T(8,128)(2,1)S(1)} collective-permute-done((bf16[4,2,256,128]{3,2,1,0:T(8,128)(2,1)S(1)}, bf16[4,2,256,128]{3,2,1,0:T(8,128)(2,1)S(1)}, u32[]{:S(2)}, u32[]{:S(2)}) %collective-permute-start.20) | collective-permute-done | bytes 524320 | tf_op jit(solution)/shard_map/ppermute | solution.py:41
  144.9 3.5 %collective-permute-done.18 = bf16[4,2,256,128]{3,2,1,0:T(8,128)(2,1)S(1)} collective-permute-done((bf16[4,2,256,128]{3,2,1,0:T(8,128)(2,1)S(1)}, bf16[4,2,256,128]{3,2,1,0:T(8,128)(2,1)S(1)}, u32[]{:S(2)}, u32[]{:S(2)}) %collective-permute-start.18) | collective-permute-done | bytes 524320 | tf_op jit(solution)/shard_map/ppermute | solution.py:41
  148.4 0.2 fusion.7
  148.8 2.2 %collective-permute-start.22 = (bf16[2,256,128]{2,1,0:T(8,128)(2,1)S(1)}, bf16[2,256,128]{2,1,0:T(8,128)(2,1)S(1)}, u32[]{:S(2)}, u32[]{:S(2)}) collective-permute-start(bf16[2,256,128]{2,1,0:T(8,128)(2,1)S(1)} %get-tuple-element.54), channel_id=1, source_target_pairs={{0,16},{1,17},{2,18},{3,19},{4,20},{5,21},{6,22},{7,23},{8,24},{9,... | collective-permute-start | bytes 393224 | tf_op jit(solution)/shard_map/ppermute | solution.py:41
  151.0 1.9 %collective-permute-start.21 = (bf16[2,256,128]{2,1,0:T(8,128)(2,1)S(1)}, bf16[2,256,128]{2,1,0:T(8,128)(2,1)S(1)}, u32[]{:S(2)}, u32[]{:S(2)}) collective-permute-start(bf16[2,256,128]{2,1,0:T(8,128)(2,1)S(1)} %get-tuple-element.52), channel_id=1, source_target_pairs={{0,8},{1,9},{2,10},{3,11},{4,12},{5,13},{6,14},{7,15},{8,16},{9,17... | collective-permute-start | bytes 393224 | tf_op jit(solution)/shard_map/ppermute | solution.py:41
  152.9 1.0 collective-permute-done.23
  154.0 7.2 %collective-permute-done.22 = bf16[2,256,128]{2,1,0:T(8,128)(2,1)S(1)} collective-permute-done((bf16[2,256,128]{2,1,0:T(8,128)(2,1)S(1)}, bf16[2,256,128]{2,1,0:T(8,128)(2,1)S(1)}, u32[]{:S(2)}, u32[]{:S(2)}) %collective-permute-start.22) | collective-permute-done | bytes 131104 | tf_op jit(solution)/shard_map/ppermute | solution.py:41
  161.2 4.8 %collective-permute-start.24 = (bf16[2,256,128]{2,1,0:T(8,128)(2,1)S(1)}, bf16[2,256,128]{2,1,0:T(8,128)(2,1)S(1)}, u32[]{:S(2)}, u32[]{:S(2)}) collective-permute-start(bf16[2,256,128]{2,1,0:T(8,128)(2,1)S(1)} %fusion.6), channel_id=1, source_target_pairs={{0,32},{1,33},{2,34},{3,35},{4,0},{5,1},{6,2},{7,3},{8,40},{9,41},... | collective-permute-start | bytes 393224 | tf_op jit(solution)/shard_map/ppermute | solution.py:41
  166.0 4.7 %gu_adam.1 = (f32[2,512,256]{2,1,0:T(8,128)}, f32[2,512,256]{2,1,0:T(8,128)}, f32[2,512,256]{2,1,0:T(8,128)}, bf16[2,512,256]{2,1,0:T(8,128)(2,1)}) custom-call(bf16[3,512,256]{2,1,0:T(8,128)(2,1)} %bitcast.67, f32[2,512,256]{2,1,0:T(8,128)} %master.2, f32[2,512,256]{2,1,0:T(8,128)} %first.2, f32[2,512,256]{2,1,0:T(8,128)} %second.2, s32[2,128,256]{2,1,0:T(8,128)} %codes.2, ...), custom_call_target="tpu_custom_call" | custom-call | tf_op jit(solution)/shard_map/gu_adam/pallas_call | solution.py:154
  170.7 3.1 %down_adam.1 = (f32[256,512]{1,0:T(8,128)}, f32[256,512]{1,0:T(8,128)}, f32[256,512]{1,0:T(8,128)}, bf16[256,512]{1,0:T(8,128)(2,1)}) custom-call(bf16[3,512,256]{2,1,0:T(8,128)(2,1)} %bitcast.68, f32[256,512]{1,0:T(8,128)} %master.3, f32[256,512]{1,0:T(8,128)} %first.3, f32[256,512]{1,0:T(8,128)} %second.3, s32[64,512]{1,0:T(8,128)} %codes.3, s32[1,512]{1,0:T(1,128)} %bitcast.76), custom_call_target="tpu_custom_call" | custom-call | tf_op jit(solution)/shard_map/down_adam/pallas_call | solution.py:171
  173.8 0.7 slice_bitcast_fusion.11
  (75 shorter events, 0.9 us)
Async XLA Ops:
  7.2 3.6 %copy-start.27 = (bf16[256,128]{1,0:T(8,128)(2,1)S(1)}, bf16[256,128]{1,0:T(8,128)(2,1)}, u32[]{:S(2)}) copy-start(bf16[256,128]{1,0:T(8,128)(2,1)} %param.13) | copy-start | bytes 196612
  7.2 3.6 %copy-start.28 = (bf16[256,128]{1,0:T(8,128)(2,1)S(1)}, bf16[256,128]{1,0:T(8,128)(2,1)}, u32[]{:S(2)}) copy-start(bf16[256,128]{1,0:T(8,128)(2,1)} %param.12) | copy-start | bytes 196612
  7.2 50.7 %all-gather.2.cloned.1.call-start = ((), (), s32[]{:S(2)}) async-start(), calls=%async_computation.1 | async-start | bytes 3932160 | tf_op jit(solution)/shard_map/all_gather | solution.py:408
  10.7 155.2 %reduce-scatter.2.cloned.1.call-start = ((), (), s32[]{:S(2)}) async-start(), calls=%async_computation.2 | async-start | bytes 3932160 | tf_op jit(solution)/shard_map/reduce_scatter | solution.py:424
  10.8 10.9 %collective-permute-start = (bf16[2,256,128]{2,1,0:T(8,128)(2,1)S(1)}, bf16[2,256,128]{2,1,0:T(8,128)(2,1)S(1)}, u32[]{:S(2)}, u32[]{:S(2)}) collective-permute-start(bf16[2,256,128]{2,1,0:T(8,128)(2,1)S(1)} %pad_maximum_fusion.3), channel_id=1, source_target_pairs={{0,4},{1,5},{2,6},{3,7},{4,36},{5,37},{6,38},{7,39},{8,12},{9,13},... | collective-permute-start | bytes 393224 | tf_op jit(solution)/shard_map/ppermute | solution.py:41
  21.7 7.7 %collective-permute-start.3 = (bf16[2,256,128]{2,1,0:T(8,128)(2,1)S(1)}, bf16[2,256,128]{2,1,0:T(8,128)(2,1)S(1)}, u32[]{:S(2)}, u32[]{:S(2)}) collective-permute-start(bf16[2,256,128]{2,1,0:T(8,128)(2,1)S(1)} %collective-permute-done), channel_id=1, source_target_pairs={{0,24},{1,25},{2,26},{3,27},{4,28},{5,29},{6,30},{7,31},{8,0},{9,1... | collective-permute-start | bytes 393224 | tf_op jit(solution)/shard_map/ppermute | solution.py:41
  24.8 12.8 %collective-permute-start.2 = (bf16[2,256,128]{2,1,0:T(8,128)(2,1)S(1)}, bf16[2,256,128]{2,1,0:T(8,128)(2,1)S(1)}, u32[]{:S(2)}, u32[]{:S(2)}) collective-permute-start(bf16[2,256,128]{2,1,0:T(8,128)(2,1)S(1)} %collective-permute-done), channel_id=1, source_target_pairs={{0,16},{1,17},{2,18},{3,19},{4,20},{5,21},{6,22},{7,23},{8,24},{9,... | collective-permute-start | bytes 393224 | tf_op jit(solution)/shard_map/ppermute | solution.py:41
  26.9 10.7 %collective-permute-start.1 = (bf16[2,256,128]{2,1,0:T(8,128)(2,1)S(1)}, bf16[2,256,128]{2,1,0:T(8,128)(2,1)S(1)}, u32[]{:S(2)}, u32[]{:S(2)}) collective-permute-start(bf16[2,256,128]{2,1,0:T(8,128)(2,1)S(1)} %collective-permute-done), channel_id=1, source_target_pairs={{0,8},{1,9},{2,10},{3,11},{4,12},{5,13},{6,14},{7,15},{8,16},{9,17... | collective-permute-start | bytes 393224 | tf_op jit(solution)/shard_map/ppermute | solution.py:41
  37.7 32.5 %copy-start.2 = (bf16[4,2,256,128]{3,2,1,0:T(8,128)(2,1)}, bf16[4,2,256,128]{3,2,1,0:T(8,128)(2,1)S(1)}, u32[]{:S(2)}) copy-start(bf16[4,2,256,128]{3,2,1,0:T(8,128)(2,1)S(1)} %pad_maximum_fusion.refs_1_) | copy-start | bytes 1572868
  37.7 12.1 %collective-permute-start.4 = (bf16[4,2,256,128]{3,2,1,0:T(8,128)(2,1)S(1)}, bf16[4,2,256,128]{3,2,1,0:T(8,128)(2,1)S(1)}, u32[]{:S(2)}, u32[]{:S(2)}) collective-permute-start(bf16[4,2,256,128]{3,2,1,0:T(8,128)(2,1)S(1)} %pad_maximum_fusion.refs_1_), channel_id=1, source_target_pairs={{0,2},{1,3},{2,4},{3,5},{4,6},{5,7},{6,0},{7,1},{8,10},{9,11},{10,... | collective-permute-start | bytes 1572872 | tf_op jit(solution)/shard_map/ppermute | solution.py:41
  39.3 12.0 %collective-permute-start.5 = (bf16[4,2,256,128]{3,2,1,0:T(8,128)(2,1)S(1)}, bf16[4,2,256,128]{3,2,1,0:T(8,128)(2,1)S(1)}, u32[]{:S(2)}, u32[]{:S(2)}) collective-permute-start(bf16[4,2,256,128]{3,2,1,0:T(8,128)(2,1)S(1)} %pad_maximum_fusion.refs_1_), channel_id=1, source_target_pairs={{0,6},{1,7},{2,0},{3,1},{4,2},{5,3},{6,4},{7,5},{8,14},{9,15},{10,... | collective-permute-start | bytes 1572872 | tf_op jit(solution)/shard_map/ppermute | solution.py:41
  49.7 20.4 %copy-start.5 = (bf16[4,2,256,128]{3,2,1,0:T(8,128)(2,1)}, bf16[4,2,256,128]{3,2,1,0:T(8,128)(2,1)S(1)}, u32[]{:S(2)}) copy-start(bf16[4,2,256,128]{3,2,1,0:T(8,128)(2,1)S(1)} %collective-permute-done.4.refs_2_) | copy-start | bytes 1572868
  49.8 7.7 %collective-permute-start.6 = (bf16[2,2,256,128]{3,2,1,0:T(8,128)(2,1)S(1)}, bf16[2,2,256,128]{3,2,1,0:T(8,128)(2,1)S(1)}, u32[]{:S(2)}, u32[]{:S(2)}) collective-permute-start(bf16[2,2,256,128]{3,2,1,0:T(8,128)(2,1)S(1)} %slice.65), channel_id=1, source_target_pairs={{0,2},{1,3},{2,4},{3,5},{4,6},{5,7},{6,0},{7,1},{8,10},{9,11},{10,... | collective-permute-start | bytes 786440 | tf_op jit(solution)/shard_map/ppermute | solution.py:41
  51.3 18.8 %copy-start.8 = (bf16[4,2,256,128]{3,2,1,0:T(8,128)(2,1)}, bf16[4,2,256,128]{3,2,1,0:T(8,128)(2,1)S(1)}, u32[]{:S(2)}) copy-start(bf16[4,2,256,128]{3,2,1,0:T(8,128)(2,1)S(1)} %collective-permute-done.5.refs_3_) | copy-start | bytes 1572868
  51.3 6.6 %collective-permute-start.7 = (bf16[2,2,256,128]{3,2,1,0:T(8,128)(2,1)S(1)}, bf16[2,2,256,128]{3,2,1,0:T(8,128)(2,1)}, u32[]{:S(2)}, u32[]{:S(2)}) collective-permute-start(bf16[2,2,256,128]{3,2,1,0:T(8,128)(2,1)S(1)} %slice.66), channel_id=1, source_target_pairs={{0,6},{1,7},{2,0},{3,1},{4,2},{5,3},{6,4},{7,5},{8,14},{9,15},{10,... | collective-permute-start | bytes 786440 | tf_op jit(solution)/shard_map/ppermute | solution.py:41
  53.2 4.8 %collective-permute-start.8 = (bf16[4,2,256,128]{3,2,1,0:T(8,128)(2,1)S(1)}, bf16[4,2,256,128]{3,2,1,0:T(8,128)(2,1)S(1)}, u32[]{:S(2)}, u32[]{:S(2)}) collective-permute-start(bf16[4,2,256,128]{3,2,1,0:T(8,128)(2,1)S(1)} %pad_maximum_fusion.refs_1_), channel_id=1, source_target_pairs={{0,1},{1,0},{2,3},{3,2},{4,5},{5,4},{6,7},{7,6},{8,9},{9,8},{10,11... | collective-permute-start | bytes 1572872 | tf_op jit(solution)/shard_map/ppermute | solution.py:41
  53.2 4.8 %collective-permute-start.9 = (bf16[4,2,256,128]{3,2,1,0:T(8,128)(2,1)S(1)}, bf16[4,2,256,128]{3,2,1,0:T(8,128)(2,1)S(1)}, u32[]{:S(2)}, u32[]{:S(2)}) collective-permute-start(bf16[4,2,256,128]{3,2,1,0:T(8,128)(2,1)S(1)} %collective-permute-done.4.refs_2_), channel_id=1, source_target_pairs={{0,1},{1,0},{2,3},{3,2},{4,5},{5,4},{6,7},{7,6},{8,9},{9,8},{10,11... | collective-permute-start | bytes 1572872 | tf_op jit(solution)/shard_map/ppermute | solution.py:41
  53.7 4.4 %collective-permute-start.10 = (bf16[4,2,256,128]{3,2,1,0:T(8,128)(2,1)S(1)}, bf16[4,2,256,128]{3,2,1,0:T(8,128)(2,1)S(1)}, u32[]{:S(2)}, u32[]{:S(2)}) collective-permute-start(bf16[4,2,256,128]{3,2,1,0:T(8,128)(2,1)S(1)} %collective-permute-done.5.refs_3_), channel_id=1, source_target_pairs={{0,1},{1,0},{2,3},{3,2},{4,5},{5,4},{6,7},{7,6},{8,9},{9,8},{10,11... | collective-permute-start | bytes 1572872 | tf_op jit(solution)/shard_map/ppermute | solution.py:41
  57.4 1.7 collective-permute-start.11
  57.9 1.9 %collective-permute-start.12 = (bf16[2,2,256,128]{3,2,1,0:T(8,128)(2,1)}, bf16[2,2,256,128]{3,2,1,0:T(8,128)(2,1)}, u32[]{:S(2)}, u32[]{:S(2)}) collective-permute-start(bf16[2,2,256,128]{3,2,1,0:T(8,128)(2,1)} %collective-permute-done.7.refs_5_), channel_id=1, source_target_pairs={{0,1},{1,0},{2,3},{3,2},{4,5},{5,4},{6,7},{7,6},{8,9},{9,8},{10,11... | collective-permute-start | bytes 786440 | tf_op jit(solution)/shard_map/ppermute | solution.py:41
  58.0 12.1 %copy-start.11 = (bf16[4,2,256,128]{3,2,1,0:T(8,128)(2,1)}, bf16[4,2,256,128]{3,2,1,0:T(8,128)(2,1)S(1)}, u32[]{:S(2)}) copy-start(bf16[4,2,256,128]{3,2,1,0:T(8,128)(2,1)S(1)} %collective-permute-done.8.refs_6_) | copy-start | bytes 1572868
  58.0 12.1 %copy-start.14 = (bf16[4,2,256,128]{3,2,1,0:T(8,128)(2,1)}, bf16[4,2,256,128]{3,2,1,0:T(8,128)(2,1)S(1)}, u32[]{:S(2)}) copy-start(bf16[4,2,256,128]{3,2,1,0:T(8,128)(2,1)S(1)} %collective-permute-done.9.refs_7_) | copy-start | bytes 1572868
  58.1 12.1 %copy-start.17 = (bf16[4,2,256,128]{3,2,1,0:T(8,128)(2,1)}, bf16[4,2,256,128]{3,2,1,0:T(8,128)(2,1)S(1)}, u32[]{:S(2)}) copy-start(bf16[4,2,256,128]{3,2,1,0:T(8,128)(2,1)S(1)} %collective-permute-done.10.refs_8_) | copy-start | bytes 1572868
  59.8 1.9 %copy-start = (bf16[6144,256]{1,0:T(8,128)(2,1)S(1)}, bf16[6144,256]{1,0:T(8,128)(2,1)}, u32[]{:S(2)}) copy-start(bf16[6144,256]{1,0:T(8,128)(2,1)} %all-gather.2.cloned.1.call-done) | copy-start | bytes 9437188
  64.2 23.1 %collective-permute-start.13 = (bf16[3,256,256]{2,1,0:T(8,128)(2,1)S(1)}, bf16[3,256,256]{2,1,0:T(8,128)(2,1)}, u32[]{:S(2)}, u32[]{:S(2)}) collective-permute-start(bf16[3,256,256]{2,1,0:T(8,128)(2,1)S(1)} %partial_sent.1), channel_id=1, source_target_pairs={{0,32},{1,33},{2,34},{3,35},{4,36},{5,37},{6,38},{7,39},{8,40},{9,... | collective-permute-start | bytes 1179656 | tf_op jit(solution)/shard_map/ppermute | solution.py:41
  72.6 0.9 copy-start.23
  89.5 16.1 %copy-start.1 = (bf16[6144,256]{1,0:T(8,128)(2,1)S(1)}, bf16[6144,256]{1,0:T(8,128)(2,1)}, u32[]{:S(2)}) copy-start(bf16[6144,256]{1,0:T(8,128)(2,1)} %all-gather.2.cloned.1.call-done) | copy-start | bytes 9437188
  89.5 19.8 %collective-permute-start.14 = (bf16[3,256,256]{2,1,0:T(8,128)(2,1)}, bf16[3,256,256]{2,1,0:T(8,128)(2,1)S(1)}, u32[]{:S(2)}, u32[]{:S(2)}) collective-permute-start(bf16[3,256,256]{2,1,0:T(8,128)(2,1)} %gated.1.refs_11_.refs_1_), channel_id=1, source_target_pairs={{0,32},{1,33},{2,34},{3,35},{4,36},{5,37},{6,38},{7,39},{8,40},{9,... | collective-permute-start | bytes 1179656 | tf_op jit(solution)/shard_map/ppermute | solution.py:41
  96.0 1.0 copy-start.3
  97.0 1.0 copy-start.6
  98.1 1.0 copy-start.9
  99.1 1.0 copy-start.12
  100.1 1.0 copy-start.15
  101.2 1.0 copy-start.18
  102.2 1.0 copy-start.22
  105.6 4.4 %copy-start.7 = (bf16[4,2,256,128]{3,2,1,0:T(8,128)(2,1)S(1)}, bf16[4,2,256,128]{3,2,1,0:T(8,128)(2,1)}, u32[]{:S(2)}) copy-start(bf16[4,2,256,128]{3,2,1,0:T(8,128)(2,1)} %copy-done.5) | copy-start | bytes 1572868
  105.6 4.3 %copy-start.10 = (bf16[4,2,256,128]{3,2,1,0:T(8,128)(2,1)S(1)}, bf16[4,2,256,128]{3,2,1,0:T(8,128)(2,1)}, u32[]{:S(2)}) copy-start(bf16[4,2,256,128]{3,2,1,0:T(8,128)(2,1)} %copy-done.8) | copy-start | bytes 1572868
  105.6 4.3 %copy-start.13 = (bf16[4,2,256,128]{3,2,1,0:T(8,128)(2,1)S(1)}, bf16[4,2,256,128]{3,2,1,0:T(8,128)(2,1)}, u32[]{:S(2)}) copy-start(bf16[4,2,256,128]{3,2,1,0:T(8,128)(2,1)} %copy-done.11) | copy-start | bytes 1572868
  105.6 4.3 %copy-start.16 = (bf16[4,2,256,128]{3,2,1,0:T(8,128)(2,1)S(1)}, bf16[4,2,256,128]{3,2,1,0:T(8,128)(2,1)}, u32[]{:S(2)}) copy-start(bf16[4,2,256,128]{3,2,1,0:T(8,128)(2,1)} %copy-done.14) | copy-start | bytes 1572868
  105.7 4.3 %copy-start.19 = (bf16[4,2,256,128]{3,2,1,0:T(8,128)(2,1)S(1)}, bf16[4,2,256,128]{3,2,1,0:T(8,128)(2,1)}, u32[]{:S(2)}) copy-start(bf16[4,2,256,128]{3,2,1,0:T(8,128)(2,1)} %copy-done.17) | copy-start | bytes 1572868
  108.0 1.0 copy-start.24
  109.0 1.0 copy-start.26
  110.0 2.6 %copy-start.20 = (bf16[3,256,256]{2,1,0:T(8,128)(2,1)}, bf16[3,256,256]{2,1,0:T(8,128)(2,1)S(1)}, u32[]{:S(2)}) copy-start(bf16[3,256,256]{2,1,0:T(8,128)(2,1)S(1)} %collective-permute-done.14.refs_1_.refs_11_) | copy-start | bytes 1179652
  112.6 1.6 copy-start.4
  114.2 1.0 copy-start.21
  114.2 4.4 %collective-permute-start.15 = (bf16[2,4,2,256,128]{4,3,2,1,0:T(8,128)(2,1)}, bf16[2,4,2,256,128]{4,3,2,1,0:T(8,128)(2,1)S(1)}, u32[]{:S(2)}, u32[]{:S(2)}) collective-permute-start(bf16[2,4,2,256,128]{4,3,2,1,0:T(8,128)(2,1)} %copy-done.26), channel_id=1, source_target_pairs={{0,1},{1,0},{2,3},{3,2},{4,5},{5,4},{6,7},{7,6},{8,9},{9,8},{10,11... | collective-permute-start | bytes 3145736 | tf_op jit(solution)/shard_map/ppermute | solution.py:41
  116.7 3.0 %copy-start.25 = (bf16[2,4,2,256,128]{4,3,2,1,0:T(8,128)(2,1)S(1)}, bf16[2,4,2,256,128]{4,3,2,1,0:T(8,128)(2,1)}, u32[]{:S(2)}) copy-start(bf16[2,4,2,256,128]{4,3,2,1,0:T(8,128)(2,1)} %copy-done.24) | copy-start | bytes 3145732
  116.7 3.0 %collective-permute-start.16 = (bf16[2,4,2,256,128]{4,3,2,1,0:T(8,128)(2,1)S(1)}, bf16[2,4,2,256,128]{4,3,2,1,0:T(8,128)(2,1)S(1)}, u32[]{:S(2)}, u32[]{:S(2)}) collective-permute-start(bf16[2,4,2,256,128]{4,3,2,1,0:T(8,128)(2,1)S(1)} %outputs_sent.1), channel_id=1, source_target_pairs={{0,1},{1,0},{2,3},{3,2},{4,5},{5,4},{6,7},{7,6},{8,9},{9,8},{10,11... | collective-permute-start | bytes 3145736 | tf_op jit(solution)/shard_map/ppermute | solution.py:41
  120.9 10.0 %collective-permute-start.17 = (bf16[2,2,256,128]{3,2,1,0:T(8,128)(2,1)S(1)}, bf16[2,2,256,128]{3,2,1,0:T(8,128)(2,1)S(1)}, u32[]{:S(2)}, u32[]{:S(2)}) collective-permute-start(bf16[2,2,256,128]{3,2,1,0:T(8,128)(2,1)S(1)} %get-tuple-element.48), channel_id=1, source_target_pairs={{0,2},{1,3},{2,4},{3,5},{4,6},{5,7},{6,0},{7,1},{8,10},{9,11},{10,... | collective-permute-start | bytes 786440 | tf_op jit(solution)/shard_map/ppermute | solution.py:41
  122.6 8.3 %collective-permute-start.19 = (bf16[2,2,256,128]{3,2,1,0:T(8,128)(2,1)S(1)}, bf16[2,2,256,128]{3,2,1,0:T(8,128)(2,1)S(1)}, u32[]{:S(2)}, u32[]{:S(2)}) collective-permute-start(bf16[2,2,256,128]{3,2,1,0:T(8,128)(2,1)S(1)} %get-tuple-element.49), channel_id=1, source_target_pairs={{0,6},{1,7},{2,0},{3,1},{4,2},{5,3},{6,4},{7,5},{8,14},{9,15},{10,... | collective-permute-start | bytes 786440 | tf_op jit(solution)/shard_map/ppermute | solution.py:41
  131.1 13.8 %collective-permute-start.20 = (bf16[4,2,256,128]{3,2,1,0:T(8,128)(2,1)S(1)}, bf16[4,2,256,128]{3,2,1,0:T(8,128)(2,1)S(1)}, u32[]{:S(2)}, u32[]{:S(2)}) collective-permute-start(bf16[4,2,256,128]{3,2,1,0:T(8,128)(2,1)S(1)} %pad_maximum_fusion.2), channel_id=1, source_target_pairs={{0,6},{1,7},{2,0},{3,1},{4,2},{5,3},{6,4},{7,5},{8,14},{9,15},{10,... | collective-permute-start | bytes 1572872 | tf_op jit(solution)/shard_map/ppermute | solution.py:41
  134.3 14.1 %collective-permute-start.18 = (bf16[4,2,256,128]{3,2,1,0:T(8,128)(2,1)S(1)}, bf16[4,2,256,128]{3,2,1,0:T(8,128)(2,1)S(1)}, u32[]{:S(2)}, u32[]{:S(2)}) collective-permute-start(bf16[4,2,256,128]{3,2,1,0:T(8,128)(2,1)S(1)} %pad_maximum_fusion.1), channel_id=1, source_target_pairs={{0,2},{1,3},{2,4},{3,5},{4,6},{5,7},{6,0},{7,1},{8,10},{9,11},{10,... | collective-permute-start | bytes 1572872 | tf_op jit(solution)/shard_map/ppermute | solution.py:41
  148.7 5.3 %collective-permute-start.23 = (bf16[2,256,128]{2,1,0:T(8,128)(2,1)S(1)}, bf16[2,256,128]{2,1,0:T(8,128)(2,1)S(1)}, u32[]{:S(2)}, u32[]{:S(2)}) collective-permute-start(bf16[2,256,128]{2,1,0:T(8,128)(2,1)S(1)} %get-tuple-element.53), channel_id=1, source_target_pairs={{0,24},{1,25},{2,26},{3,27},{4,28},{5,29},{6,30},{7,31},{8,0},{9,1... | collective-permute-start | bytes 393224 | tf_op jit(solution)/shard_map/ppermute | solution.py:41
  148.8 12.3 %collective-permute-start.22 = (bf16[2,256,128]{2,1,0:T(8,128)(2,1)S(1)}, bf16[2,256,128]{2,1,0:T(8,128)(2,1)S(1)}, u32[]{:S(2)}, u32[]{:S(2)}) collective-permute-start(bf16[2,256,128]{2,1,0:T(8,128)(2,1)S(1)} %get-tuple-element.54), channel_id=1, source_target_pairs={{0,16},{1,17},{2,18},{3,19},{4,20},{5,21},{6,22},{7,23},{8,24},{9,... | collective-permute-start | bytes 393224 | tf_op jit(solution)/shard_map/ppermute | solution.py:41
  151.0 10.1 %collective-permute-start.21 = (bf16[2,256,128]{2,1,0:T(8,128)(2,1)S(1)}, bf16[2,256,128]{2,1,0:T(8,128)(2,1)S(1)}, u32[]{:S(2)}, u32[]{:S(2)}) collective-permute-start(bf16[2,256,128]{2,1,0:T(8,128)(2,1)S(1)} %get-tuple-element.52), channel_id=1, source_target_pairs={{0,8},{1,9},{2,10},{3,11},{4,12},{5,13},{6,14},{7,15},{8,16},{9,17... | collective-permute-start | bytes 393224 | tf_op jit(solution)/shard_map/ppermute | solution.py:41
  161.2 12.6 %collective-permute-start.24 = (bf16[2,256,128]{2,1,0:T(8,128)(2,1)S(1)}, bf16[2,256,128]{2,1,0:T(8,128)(2,1)S(1)}, u32[]{:S(2)}, u32[]{:S(2)}) collective-permute-start(bf16[2,256,128]{2,1,0:T(8,128)(2,1)S(1)} %fusion.6), channel_id=1, source_target_pairs={{0,32},{1,33},{2,34},{3,35},{4,0},{5,1},{6,2},{7,3},{8,40},{9,41},... | collective-permute-start | bytes 393224 | tf_op jit(solution)/shard_map/ppermute | solution.py:41
Sparse Core Ops, SparseCore 0:
  10.9 44.2 all-gather.1
  114.3 40.9 reduce-scatter.1

commit v4 on v3

--- a/solution.py
+++ b/solution.py
@@ -87,17 +87,16 @@
         (lax.broadcasted_iota(jnp.int32, (rows, groups), 0) >> 2)
         == lax.broadcasted_iota(jnp.int32, (rows, groups), 1)
     ).astype(F32).astype(BF16)
-    code = jnp.dot(spread, codes.astype(F32).astype(BF16), preferred_element_type=F32)
-    place = (lax.broadcasted_iota(jnp.int32, code.shape, 0) & 3).astype(F32)
-    first = jnp.where(code < 2.5, 0.0, jnp.where(code < 4.5, 1.0, 2.0))
-    second = jnp.where(
-        code == 0.0, 1.0, jnp.where((code == 1.0) | (code == 3.0), 2.0, 3.0)
-    )
-    return ((place == first) | (place == second)).astype(F32)
+    mask = jnp.full(codes.shape, 12.0, F32)
+    for code, bits in enumerate((3.0, 5.0, 9.0, 6.0, 10.0)):
+        mask = jnp.where(codes == code, bits, mask)
+    mask = jnp.dot(spread, mask.astype(BF16), preferred_element_type=F32).astype(jnp.int32)
+    place = lax.broadcasted_iota(jnp.int32, mask.shape, 0) & 3
+    return ((mask >> place) & 1) == 1
 
 
 def quantize(master, keeper, scale, inverse):
-    inner = jnp.clip(master * inverse, -1.0, 1.0) * keeper
+    inner = jnp.where(keeper, jnp.clip(master * inverse, -1.0, 1.0), 0.0)
     return inner.astype(BF16) * scale.astype(BF16)
 
 
@@ -111,16 +110,17 @@
             power_of_two(expo, -1),
         )
     expo = dn_expo[...]
-    down = jnp.clip(dn_ref[...] * power_of_two(expo, -1), -1.0, 1.0) * expand_codes(dn_codes[...])
-    down = down.astype(BF16) * power_of_two(expo, 1).astype(BF16)
-    out_ref[2] = down.astype(F32).T.astype(BF16)
+    down = quantize(
+        dn_ref[...], expand_codes(dn_codes[...]), power_of_two(expo, 1), power_of_two(expo, -1)
+    )
+    out_ref[2, :256] = down[:, :256]
+    out_ref[2, 256:] = down[:, 256:]
 
 
 def adam(master, first, second, grad, codes, expo):
     keeper = expand_codes(codes)
     inverse = power_of_two(expo, -1)
-    inside = (jnp.abs(master * inverse) <= 1.0).astype(F32)
-    grad = grad * keeper * inside
+    grad = jnp.where(keeper & (jnp.abs(master * inverse) <= 1.0), grad, 0.0)
     first = BETA_ONE * first + (1.0 - BETA_ONE) * grad
     second = BETA_TWO * second + (1.0 - BETA_TWO) * grad * grad
     step = (LEARN_RATE / CORRECT_ONE) * first
@@ -139,7 +139,12 @@
 
 def down_adam_kernel(grad, master, first, second, codes, expo, new, new_first, new_second, copy):
     result = adam(
-        master[...], first[...], second[...], grad[0].astype(F32).T, codes[...], expo[...]
+        master[...],
+        first[...],
+        second[...],
+        jnp.concatenate([grad[0, :256], grad[0, 256:]], axis=1).astype(F32),
+        codes[...],
+        expo[...],
     )
     new[...], new_first[...], new_second[...], copy[...] = result
 
@@ -163,16 +168,16 @@
 
 def down_update(grads, master, first, second, codes, expo):
     rows, cols = master.shape
-    size = rows // 2
+    size = rows
     block = pl.BlockSpec((size, cols), lambda i: (i, 0))
     narrow = pl.BlockSpec((size // 4, cols), lambda i: (i, 0))
     whole = pl.BlockSpec((1, cols), lambda i: (0, 0))
     like = jax.ShapeDtypeStruct(master.shape, F32)
     return pl.pallas_call(
         down_adam_kernel,
-        grid=(2,),
+        grid=(1,),
         in_specs=[
-            pl.BlockSpec((1, cols, size), lambda i: (2, 0, i)),
+            pl.BlockSpec((1, cols, size), lambda i: (2, 0, 0)),
             block,
             block,
             block,
@@ -195,6 +200,10 @@
     )
 
 
+def down_columns(low, core):
+    return pl.ds(pl.multiple_of(low * 256, 256), 256), pl.ds(pl.multiple_of(core * 128, 128), 128)
+
+
 def weight_rows(weights, block, which, low, core):
     start = pl.multiple_of(low * 256 + core * 128, 128)
     second = pl.multiple_of(low * 256 + (1 - core) * 128, 128)
@@ -217,10 +226,17 @@
         def _():
             for lo_step in range(4):
                 block = (lo - lo_step) & 3
-                for which in range(3):
-                    left = piece_rows((own, other), ring, lo_step, which // 2)
+                for which in range(2):
+                    left = piece_rows((own, other), ring, lo_step, 0)
                     right = weight_rows(weights, block, which, from_y & 1, core)
                     acc[which] += jnp.dot(left, right, preferred_element_type=F32)
+                left = piece_rows((own, other), ring, lo_step, 1)
+                rows, first = down_columns(from_y & 1, core)
+                _, second = down_columns(from_y & 1, 1 - core)
+                right = jnp.concatenate(
+                    [weights[block, 2, rows, first], weights[block, 2, rows, second]], axis=1
+                )
+                acc[2] += cross(left, right, 1, 1)
 
     out[...] = acc[...].astype(out.dtype)
 
@@ -272,8 +288,9 @@
             start = pl.multiple_of(low * 256 + to_core * 128, 128)
             for lo_step in range(4):
                 block = (lo + lo_step) & 3
-                parts = [weights[block, which, pl.ds(start, 128), :] for which in range(3)]
-                out[low, lo_step, 0] = cross(rows[2], parts[2], 1, 1).astype(out.dtype)
+                parts = [weights[block, which, pl.ds(start, 128), :] for which in range(2)]
+                down = weights[(block, 2) + down_columns(low, to_core)]
+                out[low, lo_step, 0] = cross(rows[2], down, 1, 0).astype(out.dtype)
                 out[low, lo_step, 1] = (
                     cross(rows[0], parts[0], 1, 1) + cross(rows[1], parts[1], 1, 1)
                 ).astype(out.dtype)
@@ -318,6 +335,12 @@
 
 def grads_kernel(own_rows, inverse_scale, place, *refs):
     own, other, rows, out = refs[:5], refs[5:10], refs[10], refs[-1]
+
+    def put(at, value):
+        if not own_rows:
+            value += refs[11][at].astype(F32)
+        out[at] = value.astype(BF16)
+
     hi, lo, y, core = place[1], place[2], place[3], place[4]
     target = 1 - hi if own_rows else hi
     for ring, offset in enumerate(Y_OFFSETS):
@@ -330,16 +353,15 @@
             second = pl.ds(pl.multiple_of(low * 256 + (1 - core) * 128, 128), 128)
             for lo_step in range(4):
                 block = (lo - lo_step) & 3
-                for which in range(3):
-                    left = piece_rows((own, other), ring, lo_step, which // 2)
+                left = piece_rows((own, other), ring, lo_step, 0)
+                for which in range(2):
                     term = cross(left, rows[which], 0, 0) * inverse_scale
-                    upper, lower = term[:128], term[128:]
-                    if not own_rows:
-                        before = refs[11]
-                        upper += before[block, which, first, :].astype(F32)
-                        lower += before[block, which, second, :].astype(F32)
-                    out[block, which, first, :] = upper.astype(BF16)
-                    out[block, which, second, :] = lower.astype(BF16)
+                    put((block, which, first, slice(None)), term[:128])
+                    put((block, which, second, slice(None)), term[128:])
+                left = piece_rows((own, other), ring, lo_step, 1)
+                term = cross(rows[2], left, 0, 0) * inverse_scale
+                put((block, 2) + down_columns(low, core), term[:, :128])
+                put((block, 2) + down_columns(low, 1 - core), term[:, 128:])
 
 
 def grads(own_rows, inverse_scale, place, pieces, rows, *before):

time: 182 us -> 182 us (level)
  no operation moved by 1% of the time
where the time goes in v4:
time: 182 us; the launch traced here: 181 us
  waiting for transfers between devices  75.6 us (42%)
  starting transfers between devices  45.8 us (25%)
  Pallas kernels  29.6 us (16%)
  local copies, waits for them, and re-layouts  15.2 us (8%)
  between operations  14.4 us (8%)
    ppermute x25, waiting for transfers between devices, move(): return lax.ppermute(value, ALL, pairs)  75.6 us
    ppermute x25, starting transfers between devices, move(): return lax.ppermute(value, ALL, pairs)  45.7 us
    unnamed x58, local copies, waits for them, and re-layouts  14.3 us
    pallas_call x3, Pallas kernels, outputs(): pl.pallas_call(lambda *refs: outputs_kernel(sides, *refs), in_specs=[SMEM...  5.36 us
    pallas_call x2, Pallas kernels, grads(): pl.pallas_call(lambda *refs: grads_kernel(own_rows, inverse_scale, *refs)...  5.19 us
    pallas_call x2, Pallas kernels, partial(): pl.pallas_call(lambda *refs: partial_kernel(mine, *refs), in_specs=[SMEM]...  4.75 us
    pallas_call x1, Pallas kernels, gu_update(): pl.pallas_call(gu_adam_kernel, grid=(parts, 1), in_specs=[block, block, b...  4.53 us
  transfers between devices with their start and end apart: 27, of which 16 were waited for; matrix products, arithmetic and copies ran while one was open for 0% of the time, Pallas kernels for 11%

profile of v4, /device:TPU:2, one launch (start us, length us, event | category | flops | bytes accessed | tf_op | source)
XLA Modules:
  0.0 181.3 jit_solution(14991196077497597214)
XLA Ops:
  7.2 3.1 %quantize.1 = bf16[3,512,256]{2,1,0:T(8,128)(2,1)} custom-call(f32[2,512,256]{2,1,0:T(8,128)} %master.2, s32[2,128,256]{2,1,0:T(8,128)} %codes.2, s32[2,256]{1,0:T(2,128)} %expo.1, f32[256,512]{1,0:T(8,128)} %master.3, s32[64,512]{1,0:T(8,128)} %codes.3, s32[1,512]{1,0:T(1,128)} %bitcast.75), custom_call_target="tpu_custom_call" | custom-call | tf_op jit(solution)/shard_map/quantize/pallas_call | solution.py:423
  10.4 3.3 %collective-permute-start = (bf16[2,256,128]{2,1,0:T(8,128)(2,1)S(1)}, bf16[2,256,128]{2,1,0:T(8,128)(2,1)S(1)}, u32[]{:S(2)}, u32[]{:S(2)}) collective-permute-start(bf16[2,256,128]{2,1,0:T(8,128)(2,1)S(1)} %pad_maximum_fusion.3), channel_id=1, source_target_pairs={{0,4},{1,5},{2,6},{3,7},{4,36},{5,37},{6,38},{7,39},{8,12},{9,13},... | collective-permute-start | bytes 393224 | tf_op jit(solution)/shard_map/ppermute | solution.py:41
  13.7 7.6 %collective-permute-done = bf16[2,256,128]{2,1,0:T(8,128)(2,1)S(1)} collective-permute-done((bf16[2,256,128]{2,1,0:T(8,128)(2,1)S(1)}, bf16[2,256,128]{2,1,0:T(8,128)(2,1)S(1)}, u32[]{:S(2)}, u32[]{:S(2)}) %collective-permute-start) | collective-permute-done | bytes 131104 | tf_op jit(solution)/shard_map/ppermute | solution.py:41
  21.3 3.1 %collective-permute-start.3 = (bf16[2,256,128]{2,1,0:T(8,128)(2,1)S(1)}, bf16[2,256,128]{2,1,0:T(8,128)(2,1)S(1)}, u32[]{:S(2)}, u32[]{:S(2)}) collective-permute-start(bf16[2,256,128]{2,1,0:T(8,128)(2,1)S(1)} %collective-permute-done), channel_id=1, source_target_pairs={{0,24},{1,25},{2,26},{3,27},{4,28},{5,29},{6,30},{7,31},{8,0},{9,1... | collective-permute-start | bytes 393224 | tf_op jit(solution)/shard_map/ppermute | solution.py:41
  24.4 2.1 %collective-permute-start.2 = (bf16[2,256,128]{2,1,0:T(8,128)(2,1)S(1)}, bf16[2,256,128]{2,1,0:T(8,128)(2,1)S(1)}, u32[]{:S(2)}, u32[]{:S(2)}) collective-permute-start(bf16[2,256,128]{2,1,0:T(8,128)(2,1)S(1)} %collective-permute-done), channel_id=1, source_target_pairs={{0,16},{1,17},{2,18},{3,19},{4,20},{5,21},{6,22},{7,23},{8,24},{9,... | collective-permute-start | bytes 393224 | tf_op jit(solution)/shard_map/ppermute | solution.py:41
  26.5 1.3 collective-permute-start.1
  27.8 1.2 collective-permute-done.3
  29.0 8.2 %collective-permute-done.2 = bf16[2,256,128]{2,1,0:T(8,128)(2,1)S(1)} collective-permute-done((bf16[2,256,128]{2,1,0:T(8,128)(2,1)S(1)}, bf16[2,256,128]{2,1,0:T(8,128)(2,1)S(1)}, u32[]{:S(2)}, u32[]{:S(2)}) %collective-permute-start.2) | collective-permute-done | bytes 131104 | tf_op jit(solution)/shard_map/ppermute | solution.py:41
  37.3 1.7 collective-permute-start.4
  38.9 1.7 collective-permute-start.5
  40.6 8.8 %collective-permute-done.4.refs_2_ = bf16[4,2,256,128]{3,2,1,0:T(8,128)(2,1)S(1)} collective-permute-done((bf16[4,2,256,128]{3,2,1,0:T(8,128)(2,1)S(1)}, bf16[4,2,256,128]{3,2,1,0:T(8,128)(2,1)S(1)}, u32[]{:S(2)}, u32[]{:S(2)}) %collective-permute-start.4) | collective-permute-done | bytes 524320 | tf_op jit(solution)/shard_map/ppermute | solution.py:41
  49.4 1.5 collective-permute-start.6
  50.9 1.8 %collective-permute-start.7 = (bf16[2,2,256,128]{3,2,1,0:T(8,128)(2,1)S(1)}, bf16[2,2,256,128]{3,2,1,0:T(8,128)(2,1)}, u32[]{:S(2)}, u32[]{:S(2)}) collective-permute-start(bf16[2,2,256,128]{3,2,1,0:T(8,128)(2,1)S(1)} %slice.66), channel_id=1, source_target_pairs={{0,6},{1,7},{2,0},{3,1},{4,2},{5,3},{6,4},{7,5},{8,14},{9,15},{10,... | collective-permute-start | bytes 786440 | tf_op jit(solution)/shard_map/ppermute | solution.py:41
  52.8 0.5 collective-permute-start.9
  53.3 3.7 %collective-permute-done.6.refs_4_ = bf16[2,2,256,128]{3,2,1,0:T(8,128)(2,1)S(1)} collective-permute-done((bf16[2,2,256,128]{3,2,1,0:T(8,128)(2,1)S(1)}, bf16[2,2,256,128]{3,2,1,0:T(8,128)(2,1)S(1)}, u32[]{:S(2)}, u32[]{:S(2)}) %collective-permute-start.6) | collective-permute-done | bytes 262176 | tf_op jit(solution)/shard_map/ppermute | solution.py:41
  57.0 0.5 collective-permute-done.7.refs_5_
  57.7 1.0 collective-permute-done.11.refs_9_
  58.7 0.7 collective-permute-done.12.refs_10_
  59.4 1.9 %copy-done = bf16[6144,256]{1,0:T(8,128)(2,1)S(1)} copy-done((bf16[6144,256]{1,0:T(8,128)(2,1)S(1)}, bf16[6144,256]{1,0:T(8,128)(2,1)}, u32[]{:S(2)}) %copy-start) | copy-done | bytes 3145752
  61.3 2.3 %partial_sent.1 = bf16[3,256,256]{2,1,0:T(8,128)(2,1)S(1)} custom-call(s32[5]{0:T(128)S(1)} %stack.47.refs_0_.place, bf16[4,2,256,128]{3,2,1,0:T(8,128)(2,1)S(1)} %pad_maximum_fusion.refs_1_, bf16[4,2,256,128]{3,2,1,0:T(8,128)(2,1)S(1)} %collective-permute-done.4.refs_2_, bf16[4,2,256,128]{3,2,1,0:T(8,128)(2,1)S(1)} %collective-permute-done.5.refs_3_, ...), custom_call_target="tpu_custom_call" | custom-call | tf_op jit(solution)/shard_map/partial_sent/pallas_call | solution.py:245
  63.6 6.1 %collective-permute-start.13 = (bf16[3,256,256]{2,1,0:T(8,128)(2,1)S(1)}, bf16[3,256,256]{2,1,0:T(8,128)(2,1)}, u32[]{:S(2)}, u32[]{:S(2)}) collective-permute-start(bf16[3,256,256]{2,1,0:T(8,128)(2,1)S(1)} %partial_sent.1), channel_id=1, source_target_pairs={{0,32},{1,33},{2,34},{3,35},{4,36},{5,37},{6,38},{7,39},{8,40},{9,... | collective-permute-start | bytes 1179656 | tf_op jit(solution)/shard_map/ppermute | solution.py:41
  69.8 2.4 %partial_own.1.own = f32[3,256,256]{2,1,0:T(8,128)S(1)} custom-call(s32[5]{0:T(128)S(1)} %stack.47.refs_0_.place, bf16[4,2,256,128]{3,2,1,0:T(8,128)(2,1)S(1)} %pad_maximum_fusion.refs_1_, bf16[4,2,256,128]{3,2,1,0:T(8,128)(2,1)S(1)} %collective-permute-done.4.refs_2_, bf16[4,2,256,128]{3,2,1,0:T(8,128)(2,1)S(1)} %collective-permute-done.5.refs_3_, ...), custom_call_target="tpu_custom_call" | custom-call | tf_op jit(solution)/shard_map/partial_own/pallas_call | solution.py:245
  72.2 0.9 copy-done.23
  73.1 13.8 %collective-permute-done.13.sent = bf16[3,256,256]{2,1,0:T(8,128)(2,1)} collective-permute-done((bf16[3,256,256]{2,1,0:T(8,128)(2,1)S(1)}, bf16[3,256,256]{2,1,0:T(8,128)(2,1)}, u32[]{:S(2)}, u32[]{:S(2)}) %collective-permute-start.13) | collective-permute-done | bytes 393248 | tf_op jit(solution)/shard_map/ppermute | solution.py:41
  86.9 2.2 %gated.1.refs_11_.refs_1_ = bf16[3,256,256]{2,1,0:T(8,128)(2,1)} custom-call(f32[3,256,256]{2,1,0:T(8,128)} %copy-done.23, bf16[3,256,256]{2,1,0:T(8,128)(2,1)} %collective-permute-done.13.sent), custom_call_target="tpu_custom_call" | custom-call | tf_op jit(solution)/shard_map/gated/pallas_call | solution.py:268
  89.1 6.5 %collective-permute-start.14 = (bf16[3,256,256]{2,1,0:T(8,128)(2,1)}, bf16[3,256,256]{2,1,0:T(8,128)(2,1)S(1)}, u32[]{:S(2)}, u32[]{:S(2)}) collective-permute-start(bf16[3,256,256]{2,1,0:T(8,128)(2,1)} %gated.1.refs_11_.refs_1_), channel_id=1, source_target_pairs={{0,32},{1,33},{2,34},{3,35},{4,36},{5,37},{6,38},{7,39},{8,40},{9,... | collective-permute-start | bytes 1179656 | tf_op jit(solution)/shard_map/ppermute | solution.py:41
  95.6 1.0 copy-done.3
  96.6 1.0 copy-done.6
  97.7 1.0 copy-done.9
  98.7 1.0 copy-done.12
  99.7 1.0 copy-done.15
  100.8 1.0 copy-done.18
  101.8 1.0 copy-done.22
  102.8 2.4 %own_grads.1.refs_12_ = bf16[4,3,512,256]{3,2,1,0:T(8,128)(2,1)S(1)} custom-call(s32[5]{0:T(128)S(1)} %stack.47.refs_0_.place, bf16[4,2,256,128]{3,2,1,0:T(8,128)(2,1)S(1)} %copy-done.3, bf16[4,2,256,128]{3,2,1,0:T(8,128)(2,1)S(1)} %copy-done.6, bf16[4,2,256,128]{3,2,1,0:T(8,128)(2,1)S(1)} %copy-done.9, ...), custom_call_target="tpu_custom_call" | custom-call | tf_op jit(solution)/shard_map/own_grads/pallas_call | solution.py:368
  105.3 2.3 %outputs_sent_kept.1 = (bf16[2,4,2,256,128]{4,3,2,1,0:T(8,128)(2,1)S(1)}, bf16[2,4,2,256,128]{4,3,2,1,0:T(8,128)(2,1)S(1)}) custom-call(s32[5]{0:T(128)S(1)} %stack.47.refs_0_.place, bf16[3,256,256]{2,1,0:T(8,128)(2,1)S(1)} %copy-done.22, bf16[4,3,512,256]{3,2,1,0:T(8,128)(2,1)S(1)} %bitcast.62), custom_call_target="tpu_custom_call" | custom-call | tf_op jit(solution)/shard_map/outputs_sent_kept/pallas_call | solution.py:300
  107.7 1.0 copy-done.24
  108.7 0.2 collective-permute-done.14.refs_1_.refs_11_
  108.8 0.8 copy-done.26
  109.7 2.8 %arrived_grads.1 = bf16[4,3,512,256]{3,2,1,0:T(8,128)(2,1)S(1)} custom-call(s32[5]{0:T(128)S(1)} %stack.47.refs_0_.place, bf16[4,2,256,128]{3,2,1,0:T(8,128)(2,1)S(1)} %copy-done.3, bf16[4,2,256,128]{3,2,1,0:T(8,128)(2,1)S(1)} %copy-done.7, bf16[4,2,256,128]{3,2,1,0:T(8,128)(2,1)S(1)} %copy-done.10, ...), custom_call_target="tpu_custom_call" | custom-call | tf_op jit(solution)/shard_map/arrived_grads/pallas_call | solution.py:368
  112.4 1.6 copy-done.4
  114.1 0.1 collective-permute-start.15
  114.2 0.9 copy-done.21
  115.0 1.5 outputs_sent.1
  116.6 0.3 collective-permute-start.16
  116.9 1.5 outputs_kept.1.arrived_kept
  118.4 1.1 collective-permute-done.16.arrived_got
  119.6 1.1 combine.1
  120.6 0.1 slice_bitcast_fusion.6
  120.7 1.7 collective-permute-start.17
  122.4 1.8 collective-permute-start.19
  124.2 6.5 %collective-permute-done.17 = bf16[2,2,256,128]{3,2,1,0:T(8,128)(2,1)S(1)} collective-permute-done((bf16[2,2,256,128]{3,2,1,0:T(8,128)(2,1)S(1)}, bf16[2,2,256,128]{3,2,1,0:T(8,128)(2,1)S(1)}, u32[]{:S(2)}, u32[]{:S(2)}) %collective-permute-start.17) | collective-permute-done | bytes 262176 | tf_op jit(solution)/shard_map/ppermute | solution.py:41
  130.8 0.1 fusion.2
  131.0 3.1 %collective-permute-start.20 = (bf16[4,2,256,128]{3,2,1,0:T(8,128)(2,1)S(1)}, bf16[4,2,256,128]{3,2,1,0:T(8,128)(2,1)S(1)}, u32[]{:S(2)}, u32[]{:S(2)}) collective-permute-start(bf16[4,2,256,128]{3,2,1,0:T(8,128)(2,1)S(1)} %pad_maximum_fusion.2), channel_id=1, source_target_pairs={{0,6},{1,7},{2,0},{3,1},{4,2},{5,3},{6,4},{7,5},{8,14},{9,15},{10,... | collective-permute-start | bytes 1572872 | tf_op jit(solution)/shard_map/ppermute | solution.py:41
  134.2 10.5 %collective-permute-done.20 = bf16[4,2,256,128]{3,2,1,0:T(8,128)(2,1)S(1)} collective-permute-done((bf16[4,2,256,128]{3,2,1,0:T(8,128)(2,1)S(1)}, bf16[4,2,256,128]{3,2,1,0:T(8,128)(2,1)S(1)}, u32[]{:S(2)}, u32[]{:S(2)}) %collective-permute-start.20) | collective-permute-done | bytes 524320 | tf_op jit(solution)/shard_map/ppermute | solution.py:41
  144.7 3.5 %collective-permute-done.18 = bf16[4,2,256,128]{3,2,1,0:T(8,128)(2,1)S(1)} collective-permute-done((bf16[4,2,256,128]{3,2,1,0:T(8,128)(2,1)S(1)}, bf16[4,2,256,128]{3,2,1,0:T(8,128)(2,1)S(1)}, u32[]{:S(2)}, u32[]{:S(2)}) %collective-permute-start.18) | collective-permute-done | bytes 524320 | tf_op jit(solution)/shard_map/ppermute | solution.py:41
  148.3 0.2 fusion.7
  148.6 2.2 %collective-permute-start.22 = (bf16[2,256,128]{2,1,0:T(8,128)(2,1)S(1)}, bf16[2,256,128]{2,1,0:T(8,128)(2,1)S(1)}, u32[]{:S(2)}, u32[]{:S(2)}) collective-permute-start(bf16[2,256,128]{2,1,0:T(8,128)(2,1)S(1)} %get-tuple-element.54), channel_id=1, source_target_pairs={{0,16},{1,17},{2,18},{3,19},{4,20},{5,21},{6,22},{7,23},{8,24},{9,... | collective-permute-start | bytes 393224 | tf_op jit(solution)/shard_map/ppermute | solution.py:41
  150.8 1.9 %collective-permute-start.21 = (bf16[2,256,128]{2,1,0:T(8,128)(2,1)S(1)}, bf16[2,256,128]{2,1,0:T(8,128)(2,1)S(1)}, u32[]{:S(2)}, u32[]{:S(2)}) collective-permute-start(bf16[2,256,128]{2,1,0:T(8,128)(2,1)S(1)} %get-tuple-element.52), channel_id=1, source_target_pairs={{0,8},{1,9},{2,10},{3,11},{4,12},{5,13},{6,14},{7,15},{8,16},{9,17... | collective-permute-start | bytes 393224 | tf_op jit(solution)/shard_map/ppermute | solution.py:41
  152.7 1.0 collective-permute-done.23
  153.7 7.2 %collective-permute-done.22 = bf16[2,256,128]{2,1,0:T(8,128)(2,1)S(1)} collective-permute-done((bf16[2,256,128]{2,1,0:T(8,128)(2,1)S(1)}, bf16[2,256,128]{2,1,0:T(8,128)(2,1)S(1)}, u32[]{:S(2)}, u32[]{:S(2)}) %collective-permute-start.22) | collective-permute-done | bytes 131104 | tf_op jit(solution)/shard_map/ppermute | solution.py:41
  161.0 4.8 %collective-permute-start.24 = (bf16[2,256,128]{2,1,0:T(8,128)(2,1)S(1)}, bf16[2,256,128]{2,1,0:T(8,128)(2,1)S(1)}, u32[]{:S(2)}, u32[]{:S(2)}) collective-permute-start(bf16[2,256,128]{2,1,0:T(8,128)(2,1)S(1)} %fusion.6), channel_id=1, source_target_pairs={{0,32},{1,33},{2,34},{3,35},{4,0},{5,1},{6,2},{7,3},{8,40},{9,41},... | collective-permute-start | bytes 393224 | tf_op jit(solution)/shard_map/ppermute | solution.py:41
  165.8 4.5 %gu_adam.1 = (f32[2,512,256]{2,1,0:T(8,128)}, f32[2,512,256]{2,1,0:T(8,128)}, f32[2,512,256]{2,1,0:T(8,128)}, bf16[2,512,256]{2,1,0:T(8,128)(2,1)}) custom-call(bf16[3,512,256]{2,1,0:T(8,128)(2,1)} %bitcast.67, f32[2,512,256]{2,1,0:T(8,128)} %master.2, f32[2,512,256]{2,1,0:T(8,128)} %first.2, f32[2,512,256]{2,1,0:T(8,128)} %second.2, s32[2,128,256]{2,1,0:T(8,128)} %codes.2, ...), custom_call_target="tpu_custom_call" | custom-call | tf_op jit(solution)/shard_map/gu_adam/pallas_call | solution.py:159
  170.3 3.5 %down_adam.1 = (f32[256,512]{1,0:T(8,128)}, f32[256,512]{1,0:T(8,128)}, f32[256,512]{1,0:T(8,128)}, bf16[256,512]{1,0:T(8,128)(2,1)}) custom-call(bf16[3,512,256]{2,1,0:T(8,128)(2,1)} %bitcast.68, f32[256,512]{1,0:T(8,128)} %master.3, f32[256,512]{1,0:T(8,128)} %first.3, f32[256,512]{1,0:T(8,128)} %second.3, s32[64,512]{1,0:T(8,128)} %codes.3, s32[1,512]{1,0:T(1,128)} %bitcast.76), custom_call_target="tpu_custom_call" | custom-call | tf_op jit(solution)/shard_map/down_adam/pallas_call | solution.py:176
  173.8 0.7 slice_bitcast_fusion.11
  (75 shorter events, 0.9 us)
Async XLA Ops:
  7.2 3.2 %copy-start.27 = (bf16[256,128]{1,0:T(8,128)(2,1)S(1)}, bf16[256,128]{1,0:T(8,128)(2,1)}, u32[]{:S(2)}) copy-start(bf16[256,128]{1,0:T(8,128)(2,1)} %param.13) | copy-start | bytes 196612
  7.2 3.2 %copy-start.28 = (bf16[256,128]{1,0:T(8,128)(2,1)S(1)}, bf16[256,128]{1,0:T(8,128)(2,1)}, u32[]{:S(2)}) copy-start(bf16[256,128]{1,0:T(8,128)(2,1)} %param.12) | copy-start | bytes 196612
  7.2 50.3 %all-gather.2.cloned.1.call-start = ((), (), s32[]{:S(2)}) async-start(), calls=%async_computation.1 | async-start | bytes 3932160 | tf_op jit(solution)/shard_map/all_gather | solution.py:430
  10.3 155.4 %reduce-scatter.2.cloned.1.call-start = ((), (), s32[]{:S(2)}) async-start(), calls=%async_computation.2 | async-start | bytes 3932160 | tf_op jit(solution)/shard_map/reduce_scatter | solution.py:446
  10.4 10.9 %collective-permute-start = (bf16[2,256,128]{2,1,0:T(8,128)(2,1)S(1)}, bf16[2,256,128]{2,1,0:T(8,128)(2,1)S(1)}, u32[]{:S(2)}, u32[]{:S(2)}) collective-permute-start(bf16[2,256,128]{2,1,0:T(8,128)(2,1)S(1)} %pad_maximum_fusion.3), channel_id=1, source_target_pairs={{0,4},{1,5},{2,6},{3,7},{4,36},{5,37},{6,38},{7,39},{8,12},{9,13},... | collective-permute-start | bytes 393224 | tf_op jit(solution)/shard_map/ppermute | solution.py:41
  21.3 7.7 %collective-permute-start.3 = (bf16[2,256,128]{2,1,0:T(8,128)(2,1)S(1)}, bf16[2,256,128]{2,1,0:T(8,128)(2,1)S(1)}, u32[]{:S(2)}, u32[]{:S(2)}) collective-permute-start(bf16[2,256,128]{2,1,0:T(8,128)(2,1)S(1)} %collective-permute-done), channel_id=1, source_target_pairs={{0,24},{1,25},{2,26},{3,27},{4,28},{5,29},{6,30},{7,31},{8,0},{9,1... | collective-permute-start | bytes 393224 | tf_op jit(solution)/shard_map/ppermute | solution.py:41
  24.4 12.8 %collective-permute-start.2 = (bf16[2,256,128]{2,1,0:T(8,128)(2,1)S(1)}, bf16[2,256,128]{2,1,0:T(8,128)(2,1)S(1)}, u32[]{:S(2)}, u32[]{:S(2)}) collective-permute-start(bf16[2,256,128]{2,1,0:T(8,128)(2,1)S(1)} %collective-permute-done), channel_id=1, source_target_pairs={{0,16},{1,17},{2,18},{3,19},{4,20},{5,21},{6,22},{7,23},{8,24},{9,... | collective-permute-start | bytes 393224 | tf_op jit(solution)/shard_map/ppermute | solution.py:41
  26.5 10.7 %collective-permute-start.1 = (bf16[2,256,128]{2,1,0:T(8,128)(2,1)S(1)}, bf16[2,256,128]{2,1,0:T(8,128)(2,1)S(1)}, u32[]{:S(2)}, u32[]{:S(2)}) collective-permute-start(bf16[2,256,128]{2,1,0:T(8,128)(2,1)S(1)} %collective-permute-done), channel_id=1, source_target_pairs={{0,8},{1,9},{2,10},{3,11},{4,12},{5,13},{6,14},{7,15},{8,16},{9,17... | collective-permute-start | bytes 393224 | tf_op jit(solution)/shard_map/ppermute | solution.py:41
  37.3 32.5 %copy-start.2 = (bf16[4,2,256,128]{3,2,1,0:T(8,128)(2,1)}, bf16[4,2,256,128]{3,2,1,0:T(8,128)(2,1)S(1)}, u32[]{:S(2)}) copy-start(bf16[4,2,256,128]{3,2,1,0:T(8,128)(2,1)S(1)} %pad_maximum_fusion.refs_1_) | copy-start | bytes 1572868
  37.3 12.1 %collective-permute-start.4 = (bf16[4,2,256,128]{3,2,1,0:T(8,128)(2,1)S(1)}, bf16[4,2,256,128]{3,2,1,0:T(8,128)(2,1)S(1)}, u32[]{:S(2)}, u32[]{:S(2)}) collective-permute-start(bf16[4,2,256,128]{3,2,1,0:T(8,128)(2,1)S(1)} %pad_maximum_fusion.refs_1_), channel_id=1, source_target_pairs={{0,2},{1,3},{2,4},{3,5},{4,6},{5,7},{6,0},{7,1},{8,10},{9,11},{10,... | collective-permute-start | bytes 1572872 | tf_op jit(solution)/shard_map/ppermute | solution.py:41
  38.9 12.0 %collective-permute-start.5 = (bf16[4,2,256,128]{3,2,1,0:T(8,128)(2,1)S(1)}, bf16[4,2,256,128]{3,2,1,0:T(8,128)(2,1)S(1)}, u32[]{:S(2)}, u32[]{:S(2)}) collective-permute-start(bf16[4,2,256,128]{3,2,1,0:T(8,128)(2,1)S(1)} %pad_maximum_fusion.refs_1_), channel_id=1, source_target_pairs={{0,6},{1,7},{2,0},{3,1},{4,2},{5,3},{6,4},{7,5},{8,14},{9,15},{10,... | collective-permute-start | bytes 1572872 | tf_op jit(solution)/shard_map/ppermute | solution.py:41
  49.3 20.4 %copy-start.5 = (bf16[4,2,256,128]{3,2,1,0:T(8,128)(2,1)}, bf16[4,2,256,128]{3,2,1,0:T(8,128)(2,1)S(1)}, u32[]{:S(2)}) copy-start(bf16[4,2,256,128]{3,2,1,0:T(8,128)(2,1)S(1)} %collective-permute-done.4.refs_2_) | copy-start | bytes 1572868
  49.4 7.7 %collective-permute-start.6 = (bf16[2,2,256,128]{3,2,1,0:T(8,128)(2,1)S(1)}, bf16[2,2,256,128]{3,2,1,0:T(8,128)(2,1)S(1)}, u32[]{:S(2)}, u32[]{:S(2)}) collective-permute-start(bf16[2,2,256,128]{3,2,1,0:T(8,128)(2,1)S(1)} %slice.65), channel_id=1, source_target_pairs={{0,2},{1,3},{2,4},{3,5},{4,6},{5,7},{6,0},{7,1},{8,10},{9,11},{10,... | collective-permute-start | bytes 786440 | tf_op jit(solution)/shard_map/ppermute | solution.py:41
  50.9 18.8 %copy-start.8 = (bf16[4,2,256,128]{3,2,1,0:T(8,128)(2,1)}, bf16[4,2,256,128]{3,2,1,0:T(8,128)(2,1)S(1)}, u32[]{:S(2)}) copy-start(bf16[4,2,256,128]{3,2,1,0:T(8,128)(2,1)S(1)} %collective-permute-done.5.refs_3_) | copy-start | bytes 1572868
  50.9 6.6 %collective-permute-start.7 = (bf16[2,2,256,128]{3,2,1,0:T(8,128)(2,1)S(1)}, bf16[2,2,256,128]{3,2,1,0:T(8,128)(2,1)}, u32[]{:S(2)}, u32[]{:S(2)}) collective-permute-start(bf16[2,2,256,128]{3,2,1,0:T(8,128)(2,1)S(1)} %slice.66), channel_id=1, source_target_pairs={{0,6},{1,7},{2,0},{3,1},{4,2},{5,3},{6,4},{7,5},{8,14},{9,15},{10,... | collective-permute-start | bytes 786440 | tf_op jit(solution)/shard_map/ppermute | solution.py:41
  52.8 4.8 %collective-permute-start.8 = (bf16[4,2,256,128]{3,2,1,0:T(8,128)(2,1)S(1)}, bf16[4,2,256,128]{3,2,1,0:T(8,128)(2,1)S(1)}, u32[]{:S(2)}, u32[]{:S(2)}) collective-permute-start(bf16[4,2,256,128]{3,2,1,0:T(8,128)(2,1)S(1)} %pad_maximum_fusion.refs_1_), channel_id=1, source_target_pairs={{0,1},{1,0},{2,3},{3,2},{4,5},{5,4},{6,7},{7,6},{8,9},{9,8},{10,11... | collective-permute-start | bytes 1572872 | tf_op jit(solution)/shard_map/ppermute | solution.py:41
  52.8 4.8 %collective-permute-start.9 = (bf16[4,2,256,128]{3,2,1,0:T(8,128)(2,1)S(1)}, bf16[4,2,256,128]{3,2,1,0:T(8,128)(2,1)S(1)}, u32[]{:S(2)}, u32[]{:S(2)}) collective-permute-start(bf16[4,2,256,128]{3,2,1,0:T(8,128)(2,1)S(1)} %collective-permute-done.4.refs_2_), channel_id=1, source_target_pairs={{0,1},{1,0},{2,3},{3,2},{4,5},{5,4},{6,7},{7,6},{8,9},{9,8},{10,11... | collective-permute-start | bytes 1572872 | tf_op jit(solution)/shard_map/ppermute | solution.py:41
  53.3 4.4 %collective-permute-start.10 = (bf16[4,2,256,128]{3,2,1,0:T(8,128)(2,1)S(1)}, bf16[4,2,256,128]{3,2,1,0:T(8,128)(2,1)S(1)}, u32[]{:S(2)}, u32[]{:S(2)}) collective-permute-start(bf16[4,2,256,128]{3,2,1,0:T(8,128)(2,1)S(1)} %collective-permute-done.5.refs_3_), channel_id=1, source_target_pairs={{0,1},{1,0},{2,3},{3,2},{4,5},{5,4},{6,7},{7,6},{8,9},{9,8},{10,11... | collective-permute-start | bytes 1572872 | tf_op jit(solution)/shard_map/ppermute | solution.py:41
  57.0 1.7 collective-permute-start.11
  57.5 1.9 %collective-permute-start.12 = (bf16[2,2,256,128]{3,2,1,0:T(8,128)(2,1)}, bf16[2,2,256,128]{3,2,1,0:T(8,128)(2,1)}, u32[]{:S(2)}, u32[]{:S(2)}) collective-permute-start(bf16[2,2,256,128]{3,2,1,0:T(8,128)(2,1)} %collective-permute-done.7.refs_5_), channel_id=1, source_target_pairs={{0,1},{1,0},{2,3},{3,2},{4,5},{5,4},{6,7},{7,6},{8,9},{9,8},{10,11... | collective-permute-start | bytes 786440 | tf_op jit(solution)/shard_map/ppermute | solution.py:41
  57.6 12.1 %copy-start.11 = (bf16[4,2,256,128]{3,2,1,0:T(8,128)(2,1)}, bf16[4,2,256,128]{3,2,1,0:T(8,128)(2,1)S(1)}, u32[]{:S(2)}) copy-start(bf16[4,2,256,128]{3,2,1,0:T(8,128)(2,1)S(1)} %collective-permute-done.8.refs_6_) | copy-start | bytes 1572868
  57.6 12.1 %copy-start.14 = (bf16[4,2,256,128]{3,2,1,0:T(8,128)(2,1)}, bf16[4,2,256,128]{3,2,1,0:T(8,128)(2,1)S(1)}, u32[]{:S(2)}) copy-start(bf16[4,2,256,128]{3,2,1,0:T(8,128)(2,1)S(1)} %collective-permute-done.9.refs_7_) | copy-start | bytes 1572868
  57.6 12.1 %copy-start.17 = (bf16[4,2,256,128]{3,2,1,0:T(8,128)(2,1)}, bf16[4,2,256,128]{3,2,1,0:T(8,128)(2,1)S(1)}, u32[]{:S(2)}) copy-start(bf16[4,2,256,128]{3,2,1,0:T(8,128)(2,1)S(1)} %collective-permute-done.10.refs_8_) | copy-start | bytes 1572868
  59.4 1.9 %copy-start = (bf16[6144,256]{1,0:T(8,128)(2,1)S(1)}, bf16[6144,256]{1,0:T(8,128)(2,1)}, u32[]{:S(2)}) copy-start(bf16[6144,256]{1,0:T(8,128)(2,1)} %all-gather.2.cloned.1.call-done) | copy-start | bytes 9437188
  63.6 23.3 %collective-permute-start.13 = (bf16[3,256,256]{2,1,0:T(8,128)(2,1)S(1)}, bf16[3,256,256]{2,1,0:T(8,128)(2,1)}, u32[]{:S(2)}, u32[]{:S(2)}) collective-permute-start(bf16[3,256,256]{2,1,0:T(8,128)(2,1)S(1)} %partial_sent.1), channel_id=1, source_target_pairs={{0,32},{1,33},{2,34},{3,35},{4,36},{5,37},{6,38},{7,39},{8,40},{9,... | collective-permute-start | bytes 1179656 | tf_op jit(solution)/shard_map/ppermute | solution.py:41
  72.2 0.9 copy-start.23
  89.1 16.2 %copy-start.1 = (bf16[6144,256]{1,0:T(8,128)(2,1)S(1)}, bf16[6144,256]{1,0:T(8,128)(2,1)}, u32[]{:S(2)}) copy-start(bf16[6144,256]{1,0:T(8,128)(2,1)} %all-gather.2.cloned.1.call-done) | copy-start | bytes 9437188
  89.1 19.8 %collective-permute-start.14 = (bf16[3,256,256]{2,1,0:T(8,128)(2,1)}, bf16[3,256,256]{2,1,0:T(8,128)(2,1)S(1)}, u32[]{:S(2)}, u32[]{:S(2)}) collective-permute-start(bf16[3,256,256]{2,1,0:T(8,128)(2,1)} %gated.1.refs_11_.refs_1_), channel_id=1, source_target_pairs={{0,32},{1,33},{2,34},{3,35},{4,36},{5,37},{6,38},{7,39},{8,40},{9,... | collective-permute-start | bytes 1179656 | tf_op jit(solution)/shard_map/ppermute | solution.py:41
  95.6 1.0 copy-start.3
  96.6 1.0 copy-start.6
  97.7 1.0 copy-start.9
  98.7 1.0 copy-start.12
  99.7 1.0 copy-start.15
  100.8 1.0 copy-start.18
  101.8 1.0 copy-start.22
  105.3 4.3 %copy-start.7 = (bf16[4,2,256,128]{3,2,1,0:T(8,128)(2,1)S(1)}, bf16[4,2,256,128]{3,2,1,0:T(8,128)(2,1)}, u32[]{:S(2)}) copy-start(bf16[4,2,256,128]{3,2,1,0:T(8,128)(2,1)} %copy-done.5) | copy-start | bytes 1572868
  105.3 4.3 %copy-start.10 = (bf16[4,2,256,128]{3,2,1,0:T(8,128)(2,1)S(1)}, bf16[4,2,256,128]{3,2,1,0:T(8,128)(2,1)}, u32[]{:S(2)}) copy-start(bf16[4,2,256,128]{3,2,1,0:T(8,128)(2,1)} %copy-done.8) | copy-start | bytes 1572868
  105.3 4.3 %copy-start.13 = (bf16[4,2,256,128]{3,2,1,0:T(8,128)(2,1)S(1)}, bf16[4,2,256,128]{3,2,1,0:T(8,128)(2,1)}, u32[]{:S(2)}) copy-start(bf16[4,2,256,128]{3,2,1,0:T(8,128)(2,1)} %copy-done.11) | copy-start | bytes 1572868
  105.3 4.3 %copy-start.16 = (bf16[4,2,256,128]{3,2,1,0:T(8,128)(2,1)S(1)}, bf16[4,2,256,128]{3,2,1,0:T(8,128)(2,1)}, u32[]{:S(2)}) copy-start(bf16[4,2,256,128]{3,2,1,0:T(8,128)(2,1)} %copy-done.14) | copy-start | bytes 1572868
  105.3 4.3 %copy-start.19 = (bf16[4,2,256,128]{3,2,1,0:T(8,128)(2,1)S(1)}, bf16[4,2,256,128]{3,2,1,0:T(8,128)(2,1)}, u32[]{:S(2)}) copy-start(bf16[4,2,256,128]{3,2,1,0:T(8,128)(2,1)} %copy-done.17) | copy-start | bytes 1572868
  107.7 1.0 copy-start.24
  108.6 1.0 copy-start.26
  109.6 2.8 %copy-start.20 = (bf16[3,256,256]{2,1,0:T(8,128)(2,1)}, bf16[3,256,256]{2,1,0:T(8,128)(2,1)S(1)}, u32[]{:S(2)}) copy-start(bf16[3,256,256]{2,1,0:T(8,128)(2,1)S(1)} %collective-permute-done.14.refs_1_.refs_11_) | copy-start | bytes 1179652
  112.4 1.6 copy-start.4
  114.1 1.0 copy-start.21
  114.1 4.3 %collective-permute-start.15 = (bf16[2,4,2,256,128]{4,3,2,1,0:T(8,128)(2,1)}, bf16[2,4,2,256,128]{4,3,2,1,0:T(8,128)(2,1)S(1)}, u32[]{:S(2)}, u32[]{:S(2)}) collective-permute-start(bf16[2,4,2,256,128]{4,3,2,1,0:T(8,128)(2,1)} %copy-done.26), channel_id=1, source_target_pairs={{0,1},{1,0},{2,3},{3,2},{4,5},{5,4},{6,7},{7,6},{8,9},{9,8},{10,11... | collective-permute-start | bytes 3145736 | tf_op jit(solution)/shard_map/ppermute | solution.py:41
  116.6 3.0 %copy-start.25 = (bf16[2,4,2,256,128]{4,3,2,1,0:T(8,128)(2,1)S(1)}, bf16[2,4,2,256,128]{4,3,2,1,0:T(8,128)(2,1)}, u32[]{:S(2)}) copy-start(bf16[2,4,2,256,128]{4,3,2,1,0:T(8,128)(2,1)} %copy-done.24) | copy-start | bytes 3145732
  116.6 3.0 %collective-permute-start.16 = (bf16[2,4,2,256,128]{4,3,2,1,0:T(8,128)(2,1)S(1)}, bf16[2,4,2,256,128]{4,3,2,1,0:T(8,128)(2,1)S(1)}, u32[]{:S(2)}, u32[]{:S(2)}) collective-permute-start(bf16[2,4,2,256,128]{4,3,2,1,0:T(8,128)(2,1)S(1)} %outputs_sent.1), channel_id=1, source_target_pairs={{0,1},{1,0},{2,3},{3,2},{4,5},{5,4},{6,7},{7,6},{8,9},{9,8},{10,11... | collective-permute-start | bytes 3145736 | tf_op jit(solution)/shard_map/ppermute | solution.py:41
  120.7 10.0 %collective-permute-start.17 = (bf16[2,2,256,128]{3,2,1,0:T(8,128)(2,1)S(1)}, bf16[2,2,256,128]{3,2,1,0:T(8,128)(2,1)S(1)}, u32[]{:S(2)}, u32[]{:S(2)}) collective-permute-start(bf16[2,2,256,128]{3,2,1,0:T(8,128)(2,1)S(1)} %get-tuple-element.48), channel_id=1, source_target_pairs={{0,2},{1,3},{2,4},{3,5},{4,6},{5,7},{6,0},{7,1},{8,10},{9,11},{10,... | collective-permute-start | bytes 786440 | tf_op jit(solution)/shard_map/ppermute | solution.py:41
  122.4 8.3 %collective-permute-start.19 = (bf16[2,2,256,128]{3,2,1,0:T(8,128)(2,1)S(1)}, bf16[2,2,256,128]{3,2,1,0:T(8,128)(2,1)S(1)}, u32[]{:S(2)}, u32[]{:S(2)}) collective-permute-start(bf16[2,2,256,128]{3,2,1,0:T(8,128)(2,1)S(1)} %get-tuple-element.49), channel_id=1, source_target_pairs={{0,6},{1,7},{2,0},{3,1},{4,2},{5,3},{6,4},{7,5},{8,14},{9,15},{10,... | collective-permute-start | bytes 786440 | tf_op jit(solution)/shard_map/ppermute | solution.py:41
  131.0 13.8 %collective-permute-start.20 = (bf16[4,2,256,128]{3,2,1,0:T(8,128)(2,1)S(1)}, bf16[4,2,256,128]{3,2,1,0:T(8,128)(2,1)S(1)}, u32[]{:S(2)}, u32[]{:S(2)}) collective-permute-start(bf16[4,2,256,128]{3,2,1,0:T(8,128)(2,1)S(1)} %pad_maximum_fusion.2), channel_id=1, source_target_pairs={{0,6},{1,7},{2,0},{3,1},{4,2},{5,3},{6,4},{7,5},{8,14},{9,15},{10,... | collective-permute-start | bytes 1572872 | tf_op jit(solution)/shard_map/ppermute | solution.py:41
  134.1 14.1 %collective-permute-start.18 = (bf16[4,2,256,128]{3,2,1,0:T(8,128)(2,1)S(1)}, bf16[4,2,256,128]{3,2,1,0:T(8,128)(2,1)S(1)}, u32[]{:S(2)}, u32[]{:S(2)}) collective-permute-start(bf16[4,2,256,128]{3,2,1,0:T(8,128)(2,1)S(1)} %pad_maximum_fusion.1), channel_id=1, source_target_pairs={{0,2},{1,3},{2,4},{3,5},{4,6},{5,7},{6,0},{7,1},{8,10},{9,11},{10,... | collective-permute-start | bytes 1572872 | tf_op jit(solution)/shard_map/ppermute | solution.py:41
  148.5 5.2 %collective-permute-start.23 = (bf16[2,256,128]{2,1,0:T(8,128)(2,1)S(1)}, bf16[2,256,128]{2,1,0:T(8,128)(2,1)S(1)}, u32[]{:S(2)}, u32[]{:S(2)}) collective-permute-start(bf16[2,256,128]{2,1,0:T(8,128)(2,1)S(1)} %get-tuple-element.53), channel_id=1, source_target_pairs={{0,24},{1,25},{2,26},{3,27},{4,28},{5,29},{6,30},{7,31},{8,0},{9,1... | collective-permute-start | bytes 393224 | tf_op jit(solution)/shard_map/ppermute | solution.py:41
  148.6 12.3 %collective-permute-start.22 = (bf16[2,256,128]{2,1,0:T(8,128)(2,1)S(1)}, bf16[2,256,128]{2,1,0:T(8,128)(2,1)S(1)}, u32[]{:S(2)}, u32[]{:S(2)}) collective-permute-start(bf16[2,256,128]{2,1,0:T(8,128)(2,1)S(1)} %get-tuple-element.54), channel_id=1, source_target_pairs={{0,16},{1,17},{2,18},{3,19},{4,20},{5,21},{6,22},{7,23},{8,24},{9,... | collective-permute-start | bytes 393224 | tf_op jit(solution)/shard_map/ppermute | solution.py:41
  150.8 10.1 %collective-permute-start.21 = (bf16[2,256,128]{2,1,0:T(8,128)(2,1)S(1)}, bf16[2,256,128]{2,1,0:T(8,128)(2,1)S(1)}, u32[]{:S(2)}, u32[]{:S(2)}) collective-permute-start(bf16[2,256,128]{2,1,0:T(8,128)(2,1)S(1)} %get-tuple-element.52), channel_id=1, source_target_pairs={{0,8},{1,9},{2,10},{3,11},{4,12},{5,13},{6,14},{7,15},{8,16},{9,17... | collective-permute-start | bytes 393224 | tf_op jit(solution)/shard_map/ppermute | solution.py:41
  161.0 12.8 %collective-permute-start.24 = (bf16[2,256,128]{2,1,0:T(8,128)(2,1)S(1)}, bf16[2,256,128]{2,1,0:T(8,128)(2,1)S(1)}, u32[]{:S(2)}, u32[]{:S(2)}) collective-permute-start(bf16[2,256,128]{2,1,0:T(8,128)(2,1)S(1)} %fusion.6), channel_id=1, source_target_pairs={{0,32},{1,33},{2,34},{3,35},{4,0},{5,1},{6,2},{7,3},{8,40},{9,41},... | collective-permute-start | bytes 393224 | tf_op jit(solution)/shard_map/ppermute | solution.py:41
Sparse Core Ops, SparseCore 0:
  10.5 44.2 all-gather.1
  114.2 40.8 reduce-scatter.1

commit v5 on v4

--- a/solution.py
+++ b/solution.py
@@ -387,7 +387,7 @@
     return own + tuple(move(piece, other_core) for piece in own), weights
 
 
-def scatter_outputs(total):
+def scatter_outputs(total, ready):
     f32 = lambda value: value.astype(F32)
     low = move(total[2, :2], along_y(1))
     high = move(total[2, 2:], along_y(-1))
@@ -397,10 +397,12 @@
     from_after = move(behind, along_y(-1))
     line = f32(total[0]) + f32(from_before) + f32(from_after)
     leaving = line[1:].astype(BF16)
+    arrived = [move(leaving[step - 1], along_lo(step)) for step in (1, 2, 3)]
+    arrived[0], arrived[1], arrived[2], ready = lax.optimization_barrier((*arrived, ready))
     result = line[0]
-    for step in (1, 2, 3):
-        result = result + f32(move(leaving[step - 1], along_lo(step)))
-    return result.astype(BF16)
+    for piece in arrived:
+        result = result + f32(piece)
+    return result.astype(BF16), ready
 
 
 def shards(
@@ -449,14 +451,15 @@
     (sent,) = outputs(("sent",), place, rows_other, weights)
     got = move(sent, other_core)
     (kept,) = outputs(("kept",), place, rows_other, weights)
-    both = scatter_outputs(combine(place, own_kept, own_got, kept, got))
+    down_new, down_first_new, down_second_new, down_copy = down_update(
+        grad, down_master, down_first, down_second, down_codes, down_expo
+    )
+    total = combine(place, own_kept, own_got, got, kept)
+    both, down_copy = scatter_outputs(total, down_copy)
     gu_new, gu_first_new, gu_second_new, gu_copy = gu_update(
         grad, gu_master, gu_first, gu_second, gu_codes, gu_expo
     )
-    down_new, down_first_new, down_second_new, down_copy = down_update(
-        grad, down_master, down_first, down_second, down_codes, down_expo
-    )
-    both = after(move(both, from_half), gu_copy, down_copy)
+    both = after(move(both, from_half), gu_copy)
     return (
         both[0],
         both[1],

time: 182 us -> 180 us (0.989); the launches traced: 181 us -> 177 us
  waiting for transfers between devices: 75.6 us -> 70 us
    ppermute x25, waiting for transfers between devices: 75.6 us -> 68.5 us  [move(): return lax.ppermute(value, ALL, pairs)]
where the time goes in v5:
time: 180 us; the launch traced here: 177 us
  waiting for transfers between devices  70 us (39%)
  starting transfers between devices  47.4 us (26%)
  Pallas kernels  29.6 us (16%)
  local copies, waits for them, and re-layouts  15.2 us (8%)
  between operations  14.4 us (8%)
    ppermute x25, waiting for transfers between devices, move(): return lax.ppermute(value, ALL, pairs)  68.5 us
    ppermute x25, starting transfers between devices, move(): return lax.ppermute(value, ALL, pairs)  47.4 us
    unnamed x58, local copies, waits for them, and re-layouts  14.3 us
    pallas_call x3, Pallas kernels, outputs(): pl.pallas_call(lambda *refs: outputs_kernel(sides, *refs), in_specs=[SMEM...  5.36 us
    pallas_call x2, Pallas kernels, grads(): pl.pallas_call(lambda *refs: grads_kernel(own_rows, inverse_scale, *refs)...  5.19 us
    pallas_call x2, Pallas kernels, partial(): pl.pallas_call(lambda *refs: partial_kernel(mine, *refs), in_specs=[SMEM]...  4.75 us
    pallas_call x1, Pallas kernels, gu_update(): pl.pallas_call(gu_adam_kernel, grid=(parts, 1), in_specs=[block, block, b...  4.52 us
  transfers between devices with their start and end apart: 27, of which 16 were waited for; matrix products, arithmetic and copies ran while one was open for 0% of the time, Pallas kernels for 11%

profile of v5, /device:TPU:2, one launch (start us, length us, event | category | flops | bytes accessed | tf_op | source)
XLA Modules:
  0.0 177.3 jit_solution(4631952380522291183)
XLA Ops:
  7.2 3.1 %quantize.1 = bf16[3,512,256]{2,1,0:T(8,128)(2,1)} custom-call(f32[2,512,256]{2,1,0:T(8,128)} %master.3, s32[2,128,256]{2,1,0:T(8,128)} %codes.3, s32[2,256]{1,0:T(2,128)} %expo.1, f32[256,512]{1,0:T(8,128)} %master.2, s32[64,512]{1,0:T(8,128)} %codes.2, s32[1,512]{1,0:T(1,128)} %bitcast.75), custom_call_target="tpu_custom_call" | custom-call | tf_op jit(solution)/shard_map/quantize/pallas_call | solution.py:425
  10.4 3.3 %collective-permute-start = (bf16[2,256,128]{2,1,0:T(8,128)(2,1)S(1)}, bf16[2,256,128]{2,1,0:T(8,128)(2,1)S(1)}, u32[]{:S(2)}, u32[]{:S(2)}) collective-permute-start(bf16[2,256,128]{2,1,0:T(8,128)(2,1)S(1)} %pad_maximum_fusion.3), channel_id=1, source_target_pairs={{0,4},{1,5},{2,6},{3,7},{4,36},{5,37},{6,38},{7,39},{8,12},{9,13},... | collective-permute-start | bytes 393224 | tf_op jit(solution)/shard_map/ppermute | solution.py:41
  13.7 7.6 %collective-permute-done = bf16[2,256,128]{2,1,0:T(8,128)(2,1)S(1)} collective-permute-done((bf16[2,256,128]{2,1,0:T(8,128)(2,1)S(1)}, bf16[2,256,128]{2,1,0:T(8,128)(2,1)S(1)}, u32[]{:S(2)}, u32[]{:S(2)}) %collective-permute-start) | collective-permute-done | bytes 131104 | tf_op jit(solution)/shard_map/ppermute | solution.py:41
  21.3 3.1 %collective-permute-start.3 = (bf16[2,256,128]{2,1,0:T(8,128)(2,1)S(1)}, bf16[2,256,128]{2,1,0:T(8,128)(2,1)S(1)}, u32[]{:S(2)}, u32[]{:S(2)}) collective-permute-start(bf16[2,256,128]{2,1,0:T(8,128)(2,1)S(1)} %collective-permute-done), channel_id=1, source_target_pairs={{0,24},{1,25},{2,26},{3,27},{4,28},{5,29},{6,30},{7,31},{8,0},{9,1... | collective-permute-start | bytes 393224 | tf_op jit(solution)/shard_map/ppermute | solution.py:41
  24.4 2.1 %collective-permute-start.2 = (bf16[2,256,128]{2,1,0:T(8,128)(2,1)S(1)}, bf16[2,256,128]{2,1,0:T(8,128)(2,1)S(1)}, u32[]{:S(2)}, u32[]{:S(2)}) collective-permute-start(bf16[2,256,128]{2,1,0:T(8,128)(2,1)S(1)} %collective-permute-done), channel_id=1, source_target_pairs={{0,16},{1,17},{2,18},{3,19},{4,20},{5,21},{6,22},{7,23},{8,24},{9,... | collective-permute-start | bytes 393224 | tf_op jit(solution)/shard_map/ppermute | solution.py:41
  26.5 1.3 collective-permute-start.1
  27.8 1.2 collective-permute-done.3
  29.0 8.2 %collective-permute-done.2 = bf16[2,256,128]{2,1,0:T(8,128)(2,1)S(1)} collective-permute-done((bf16[2,256,128]{2,1,0:T(8,128)(2,1)S(1)}, bf16[2,256,128]{2,1,0:T(8,128)(2,1)S(1)}, u32[]{:S(2)}, u32[]{:S(2)}) %collective-permute-start.2) | collective-permute-done | bytes 131104 | tf_op jit(solution)/shard_map/ppermute | solution.py:41
  37.3 1.7 collective-permute-start.4
  38.9 1.7 collective-permute-start.5
  40.6 8.8 %collective-permute-done.4.refs_2_ = bf16[4,2,256,128]{3,2,1,0:T(8,128)(2,1)S(1)} collective-permute-done((bf16[4,2,256,128]{3,2,1,0:T(8,128)(2,1)S(1)}, bf16[4,2,256,128]{3,2,1,0:T(8,128)(2,1)S(1)}, u32[]{:S(2)}, u32[]{:S(2)}) %collective-permute-start.4) | collective-permute-done | bytes 524320 | tf_op jit(solution)/shard_map/ppermute | solution.py:41
  49.4 1.5 collective-permute-start.6
  50.9 1.8 %collective-permute-start.7 = (bf16[2,2,256,128]{3,2,1,0:T(8,128)(2,1)S(1)}, bf16[2,2,256,128]{3,2,1,0:T(8,128)(2,1)}, u32[]{:S(2)}, u32[]{:S(2)}) collective-permute-start(bf16[2,2,256,128]{3,2,1,0:T(8,128)(2,1)S(1)} %slice.66), channel_id=1, source_target_pairs={{0,6},{1,7},{2,0},{3,1},{4,2},{5,3},{6,4},{7,5},{8,14},{9,15},{10,... | collective-permute-start | bytes 786440 | tf_op jit(solution)/shard_map/ppermute | solution.py:41
  52.8 0.5 collective-permute-start.9
  53.3 3.7 %collective-permute-done.6.refs_4_ = bf16[2,2,256,128]{3,2,1,0:T(8,128)(2,1)S(1)} collective-permute-done((bf16[2,2,256,128]{3,2,1,0:T(8,128)(2,1)S(1)}, bf16[2,2,256,128]{3,2,1,0:T(8,128)(2,1)S(1)}, u32[]{:S(2)}, u32[]{:S(2)}) %collective-permute-start.6) | collective-permute-done | bytes 262176 | tf_op jit(solution)/shard_map/ppermute | solution.py:41
  57.0 0.5 collective-permute-done.7.refs_5_
  57.7 1.0 collective-permute-done.11.refs_9_
  58.7 0.7 collective-permute-done.12.refs_10_
  59.4 1.9 %copy-done = bf16[6144,256]{1,0:T(8,128)(2,1)S(1)} copy-done((bf16[6144,256]{1,0:T(8,128)(2,1)S(1)}, bf16[6144,256]{1,0:T(8,128)(2,1)}, u32[]{:S(2)}) %copy-start) | copy-done | bytes 3145752
  61.3 2.3 %partial_sent.1 = bf16[3,256,256]{2,1,0:T(8,128)(2,1)S(1)} custom-call(s32[5]{0:T(128)S(1)} %stack.47.refs_0_.place, bf16[4,2,256,128]{3,2,1,0:T(8,128)(2,1)S(1)} %pad_maximum_fusion.refs_1_, bf16[4,2,256,128]{3,2,1,0:T(8,128)(2,1)S(1)} %collective-permute-done.4.refs_2_, bf16[4,2,256,128]{3,2,1,0:T(8,128)(2,1)S(1)} %collective-permute-done.5.refs_3_, ...), custom_call_target="tpu_custom_call" | custom-call | tf_op jit(solution)/shard_map/partial_sent/pallas_call | solution.py:245
  63.6 6.1 %collective-permute-start.13 = (bf16[3,256,256]{2,1,0:T(8,128)(2,1)S(1)}, bf16[3,256,256]{2,1,0:T(8,128)(2,1)}, u32[]{:S(2)}, u32[]{:S(2)}) collective-permute-start(bf16[3,256,256]{2,1,0:T(8,128)(2,1)S(1)} %partial_sent.1), channel_id=1, source_target_pairs={{0,32},{1,33},{2,34},{3,35},{4,36},{5,37},{6,38},{7,39},{8,40},{9,... | collective-permute-start | bytes 1179656 | tf_op jit(solution)/shard_map/ppermute | solution.py:41
  69.8 2.4 %partial_own.1.own = f32[3,256,256]{2,1,0:T(8,128)S(1)} custom-call(s32[5]{0:T(128)S(1)} %stack.47.refs_0_.place, bf16[4,2,256,128]{3,2,1,0:T(8,128)(2,1)S(1)} %pad_maximum_fusion.refs_1_, bf16[4,2,256,128]{3,2,1,0:T(8,128)(2,1)S(1)} %collective-permute-done.4.refs_2_, bf16[4,2,256,128]{3,2,1,0:T(8,128)(2,1)S(1)} %collective-permute-done.5.refs_3_, ...), custom_call_target="tpu_custom_call" | custom-call | tf_op jit(solution)/shard_map/partial_own/pallas_call | solution.py:245
  72.2 0.9 copy-done.23
  73.1 13.8 %collective-permute-done.13.sent = bf16[3,256,256]{2,1,0:T(8,128)(2,1)} collective-permute-done((bf16[3,256,256]{2,1,0:T(8,128)(2,1)S(1)}, bf16[3,256,256]{2,1,0:T(8,128)(2,1)}, u32[]{:S(2)}, u32[]{:S(2)}) %collective-permute-start.13) | collective-permute-done | bytes 393248 | tf_op jit(solution)/shard_map/ppermute | solution.py:41
  86.9 2.2 %gated.1.refs_11_.refs_1_ = bf16[3,256,256]{2,1,0:T(8,128)(2,1)} custom-call(f32[3,256,256]{2,1,0:T(8,128)} %copy-done.23, bf16[3,256,256]{2,1,0:T(8,128)(2,1)} %collective-permute-done.13.sent), custom_call_target="tpu_custom_call" | custom-call | tf_op jit(solution)/shard_map/gated/pallas_call | solution.py:268
  89.1 6.5 %collective-permute-start.14 = (bf16[3,256,256]{2,1,0:T(8,128)(2,1)}, bf16[3,256,256]{2,1,0:T(8,128)(2,1)S(1)}, u32[]{:S(2)}, u32[]{:S(2)}) collective-permute-start(bf16[3,256,256]{2,1,0:T(8,128)(2,1)} %gated.1.refs_11_.refs_1_), channel_id=1, source_target_pairs={{0,32},{1,33},{2,34},{3,35},{4,36},{5,37},{6,38},{7,39},{8,40},{9,... | collective-permute-start | bytes 1179656 | tf_op jit(solution)/shard_map/ppermute | solution.py:41
  95.6 1.0 copy-done.3
  96.6 1.0 copy-done.6
  97.7 1.0 copy-done.9
  98.7 1.0 copy-done.12
  99.7 1.0 copy-done.15
  100.8 1.0 copy-done.18
  101.8 1.0 copy-done.22
  102.8 2.4 %own_grads.1.refs_12_ = bf16[4,3,512,256]{3,2,1,0:T(8,128)(2,1)S(1)} custom-call(s32[5]{0:T(128)S(1)} %stack.47.refs_0_.place, bf16[4,2,256,128]{3,2,1,0:T(8,128)(2,1)S(1)} %copy-done.3, bf16[4,2,256,128]{3,2,1,0:T(8,128)(2,1)S(1)} %copy-done.6, bf16[4,2,256,128]{3,2,1,0:T(8,128)(2,1)S(1)} %copy-done.9, ...), custom_call_target="tpu_custom_call" | custom-call | tf_op jit(solution)/shard_map/own_grads/pallas_call | solution.py:368
  105.3 2.3 %outputs_sent_kept.1 = (bf16[2,4,2,256,128]{4,3,2,1,0:T(8,128)(2,1)S(1)}, bf16[2,4,2,256,128]{4,3,2,1,0:T(8,128)(2,1)S(1)}) custom-call(s32[5]{0:T(128)S(1)} %stack.47.refs_0_.place, bf16[3,256,256]{2,1,0:T(8,128)(2,1)S(1)} %copy-done.22, bf16[4,3,512,256]{3,2,1,0:T(8,128)(2,1)S(1)} %bitcast.62), custom_call_target="tpu_custom_call" | custom-call | tf_op jit(solution)/shard_map/outputs_sent_kept/pallas_call | solution.py:300
  107.7 1.0 copy-done.24
  108.7 0.2 collective-permute-done.14.refs_1_.refs_11_
  108.8 0.8 copy-done.26
  109.7 2.8 %arrived_grads.1 = bf16[4,3,512,256]{3,2,1,0:T(8,128)(2,1)S(1)} custom-call(s32[5]{0:T(128)S(1)} %stack.47.refs_0_.place, bf16[4,2,256,128]{3,2,1,0:T(8,128)(2,1)S(1)} %copy-done.3, bf16[4,2,256,128]{3,2,1,0:T(8,128)(2,1)S(1)} %copy-done.7, bf16[4,2,256,128]{3,2,1,0:T(8,128)(2,1)S(1)} %copy-done.10, ...), custom_call_target="tpu_custom_call" | custom-call | tf_op jit(solution)/shard_map/arrived_grads/pallas_call | solution.py:368
  112.4 1.6 copy-done.4
  114.1 0.1 collective-permute-start.15
  114.2 0.9 copy-done.21
  115.0 1.5 outputs_sent.1
  116.6 0.3 collective-permute-start.16
  116.9 1.5 outputs_kept.1.arrived_got
  118.4 1.1 collective-permute-done.16.arrived_kept
  119.6 1.1 combine.1
  120.6 0.1 slice_bitcast_fusion.6
  120.7 1.7 collective-permute-start.17
  122.4 1.8 %collective-permute-start.19 = (bf16[2,2,256,128]{3,2,1,0:T(8,128)(2,1)S(1)}, bf16[2,2,256,128]{3,2,1,0:T(8,128)(2,1)S(1)}, u32[]{:S(2)}, u32[]{:S(2)}) collective-permute-start(bf16[2,2,256,128]{3,2,1,0:T(8,128)(2,1)S(1)} %get-tuple-element.57), channel_id=1, source_target_pairs={{0,6},{1,7},{2,0},{3,1},{4,2},{5,3},{6,4},{7,5},{8,14},{9,15},{10,... | collective-permute-start | bytes 786440 | tf_op jit(solution)/shard_map/ppermute | solution.py:41
  124.2 6.5 %collective-permute-done.17 = bf16[2,2,256,128]{3,2,1,0:T(8,128)(2,1)S(1)} collective-permute-done((bf16[2,2,256,128]{3,2,1,0:T(8,128)(2,1)S(1)}, bf16[2,2,256,128]{3,2,1,0:T(8,128)(2,1)S(1)}, u32[]{:S(2)}, u32[]{:S(2)}) %collective-permute-start.17) | collective-permute-done | bytes 262176 | tf_op jit(solution)/shard_map/ppermute | solution.py:41
  130.8 0.1 fusion.2
  131.0 3.1 %collective-permute-start.20 = (bf16[4,2,256,128]{3,2,1,0:T(8,128)(2,1)S(1)}, bf16[4,2,256,128]{3,2,1,0:T(8,128)(2,1)S(1)}, u32[]{:S(2)}, u32[]{:S(2)}) collective-permute-start(bf16[4,2,256,128]{3,2,1,0:T(8,128)(2,1)S(1)} %pad_maximum_fusion.2), channel_id=1, source_target_pairs={{0,6},{1,7},{2,0},{3,1},{4,2},{5,3},{6,4},{7,5},{8,14},{9,15},{10,... | collective-permute-start | bytes 1572872 | tf_op jit(solution)/shard_map/ppermute | solution.py:41
  134.2 10.5 %collective-permute-done.20 = bf16[4,2,256,128]{3,2,1,0:T(8,128)(2,1)S(1)} collective-permute-done((bf16[4,2,256,128]{3,2,1,0:T(8,128)(2,1)S(1)}, bf16[4,2,256,128]{3,2,1,0:T(8,128)(2,1)S(1)}, u32[]{:S(2)}, u32[]{:S(2)}) %collective-permute-start.20) | collective-permute-done | bytes 524320 | tf_op jit(solution)/shard_map/ppermute | solution.py:41
  144.7 3.5 %collective-permute-done.18 = bf16[4,2,256,128]{3,2,1,0:T(8,128)(2,1)S(1)} collective-permute-done((bf16[4,2,256,128]{3,2,1,0:T(8,128)(2,1)S(1)}, bf16[4,2,256,128]{3,2,1,0:T(8,128)(2,1)S(1)}, u32[]{:S(2)}, u32[]{:S(2)}) %collective-permute-start.18) | collective-permute-done | bytes 524320 | tf_op jit(solution)/shard_map/ppermute | solution.py:41
  148.3 0.2 fusion.7
  148.6 2.2 %collective-permute-start.22 = (bf16[2,256,128]{2,1,0:T(8,128)(2,1)S(1)}, bf16[2,256,128]{2,1,0:T(8,128)(2,1)S(1)}, u32[]{:S(2)}, u32[]{:S(2)}) collective-permute-start(bf16[2,256,128]{2,1,0:T(8,128)(2,1)S(1)} %get-tuple-element.61), channel_id=1, source_target_pairs={{0,16},{1,17},{2,18},{3,19},{4,20},{5,21},{6,22},{7,23},{8,24},{9,... | collective-permute-start | bytes 393224 | tf_op jit(solution)/shard_map/ppermute | solution.py:41
  150.8 2.8 %collective-permute-start.23 = (bf16[2,256,128]{2,1,0:T(8,128)(2,1)S(1)}, bf16[2,256,128]{2,1,0:T(8,128)(2,1)S(1)}, u32[]{:S(2)}, u32[]{:S(2)}) collective-permute-start(bf16[2,256,128]{2,1,0:T(8,128)(2,1)S(1)} %get-tuple-element.60), channel_id=1, source_target_pairs={{0,24},{1,25},{2,26},{3,27},{4,28},{5,29},{6,30},{7,31},{8,0},{9,1... | collective-permute-start | bytes 393224 | tf_op jit(solution)/shard_map/ppermute | solution.py:41
  153.6 1.5 reduce-scatter.2.cloned.1.call-done
  155.1 3.5 %down_adam.1 = (f32[256,512]{1,0:T(8,128)}, f32[256,512]{1,0:T(8,128)}, f32[256,512]{1,0:T(8,128)}, bf16[256,512]{1,0:T(8,128)(2,1)}) custom-call(bf16[3,512,256]{2,1,0:T(8,128)(2,1)} %bitcast.67, f32[256,512]{1,0:T(8,128)} %master.2, f32[256,512]{1,0:T(8,128)} %first.2, f32[256,512]{1,0:T(8,128)} %second.2, s32[64,512]{1,0:T(8,128)} %codes.2, s32[1,512]{1,0:T(1,128)} %bitcast.76), custom_call_target="tpu_custom_call" | custom-call | tf_op jit(solution)/shard_map/down_adam/pallas_call | solution.py:176
  158.6 1.1 collective-permute-done.22
  159.8 5.5 %collective-permute-start.24 = (bf16[2,256,128]{2,1,0:T(8,128)(2,1)S(1)}, bf16[2,256,128]{2,1,0:T(8,128)(2,1)S(1)}, u32[]{:S(2)}, u32[]{:S(2)}) collective-permute-start(bf16[2,256,128]{2,1,0:T(8,128)(2,1)S(1)} %fusion.6), channel_id=1, source_target_pairs={{0,32},{1,33},{2,34},{3,35},{4,0},{5,1},{6,2},{7,3},{8,40},{9,41},... | collective-permute-start | bytes 393224 | tf_op jit(solution)/shard_map/ppermute | solution.py:41
  165.3 4.5 %gu_adam.1 = (f32[2,512,256]{2,1,0:T(8,128)}, f32[2,512,256]{2,1,0:T(8,128)}, f32[2,512,256]{2,1,0:T(8,128)}, bf16[2,512,256]{2,1,0:T(8,128)(2,1)}) custom-call(bf16[3,512,256]{2,1,0:T(8,128)(2,1)} %bitcast.68, f32[2,512,256]{2,1,0:T(8,128)} %master.3, f32[2,512,256]{2,1,0:T(8,128)} %first.3, f32[2,512,256]{2,1,0:T(8,128)} %second.3, s32[2,128,256]{2,1,0:T(8,128)} %codes.3, ...), custom_call_target="tpu_custom_call" | custom-call | tf_op jit(solution)/shard_map/gu_adam/pallas_call | solution.py:159
  169.8 0.7 slice_bitcast_fusion.11
  (75 shorter events, 0.9 us)
Async XLA Ops:
  7.2 3.2 %copy-start.27 = (bf16[256,128]{1,0:T(8,128)(2,1)S(1)}, bf16[256,128]{1,0:T(8,128)(2,1)}, u32[]{:S(2)}) copy-start(bf16[256,128]{1,0:T(8,128)(2,1)} %param.13) | copy-start | bytes 196612
  7.2 3.2 %copy-start.28 = (bf16[256,128]{1,0:T(8,128)(2,1)S(1)}, bf16[256,128]{1,0:T(8,128)(2,1)}, u32[]{:S(2)}) copy-start(bf16[256,128]{1,0:T(8,128)(2,1)} %param.12) | copy-start | bytes 196612
  7.2 50.3 %all-gather.2.cloned.1.call-start = ((), (), s32[]{:S(2)}) async-start(), calls=%async_computation.1 | async-start | bytes 3932160 | tf_op jit(solution)/shard_map/all_gather | solution.py:432
  10.3 144.8 %reduce-scatter.2.cloned.1.call-start = ((), (), s32[]{:S(2)}) async-start(), calls=%async_computation.2 | async-start | bytes 3932160 | tf_op jit(solution)/shard_map/reduce_scatter | solution.py:448
  10.4 10.9 %collective-permute-start = (bf16[2,256,128]{2,1,0:T(8,128)(2,1)S(1)}, bf16[2,256,128]{2,1,0:T(8,128)(2,1)S(1)}, u32[]{:S(2)}, u32[]{:S(2)}) collective-permute-start(bf16[2,256,128]{2,1,0:T(8,128)(2,1)S(1)} %pad_maximum_fusion.3), channel_id=1, source_target_pairs={{0,4},{1,5},{2,6},{3,7},{4,36},{5,37},{6,38},{7,39},{8,12},{9,13},... | collective-permute-start | bytes 393224 | tf_op jit(solution)/shard_map/ppermute | solution.py:41
  21.3 7.7 %collective-permute-start.3 = (bf16[2,256,128]{2,1,0:T(8,128)(2,1)S(1)}, bf16[2,256,128]{2,1,0:T(8,128)(2,1)S(1)}, u32[]{:S(2)}, u32[]{:S(2)}) collective-permute-start(bf16[2,256,128]{2,1,0:T(8,128)(2,1)S(1)} %collective-permute-done), channel_id=1, source_target_pairs={{0,24},{1,25},{2,26},{3,27},{4,28},{5,29},{6,30},{7,31},{8,0},{9,1... | collective-permute-start | bytes 393224 | tf_op jit(solution)/shard_map/ppermute | solution.py:41
  24.4 12.8 %collective-permute-start.2 = (bf16[2,256,128]{2,1,0:T(8,128)(2,1)S(1)}, bf16[2,256,128]{2,1,0:T(8,128)(2,1)S(1)}, u32[]{:S(2)}, u32[]{:S(2)}) collective-permute-start(bf16[2,256,128]{2,1,0:T(8,128)(2,1)S(1)} %collective-permute-done), channel_id=1, source_target_pairs={{0,16},{1,17},{2,18},{3,19},{4,20},{5,21},{6,22},{7,23},{8,24},{9,... | collective-permute-start | bytes 393224 | tf_op jit(solution)/shard_map/ppermute | solution.py:41
  26.5 10.7 %collective-permute-start.1 = (bf16[2,256,128]{2,1,0:T(8,128)(2,1)S(1)}, bf16[2,256,128]{2,1,0:T(8,128)(2,1)S(1)}, u32[]{:S(2)}, u32[]{:S(2)}) collective-permute-start(bf16[2,256,128]{2,1,0:T(8,128)(2,1)S(1)} %collective-permute-done), channel_id=1, source_target_pairs={{0,8},{1,9},{2,10},{3,11},{4,12},{5,13},{6,14},{7,15},{8,16},{9,17... | collective-permute-start | bytes 393224 | tf_op jit(solution)/shard_map/ppermute | solution.py:41
  37.3 32.5 %copy-start.2 = (bf16[4,2,256,128]{3,2,1,0:T(8,128)(2,1)}, bf16[4,2,256,128]{3,2,1,0:T(8,128)(2,1)S(1)}, u32[]{:S(2)}) copy-start(bf16[4,2,256,128]{3,2,1,0:T(8,128)(2,1)S(1)} %pad_maximum_fusion.refs_1_) | copy-start | bytes 1572868
  37.3 12.1 %collective-permute-start.4 = (bf16[4,2,256,128]{3,2,1,0:T(8,128)(2,1)S(1)}, bf16[4,2,256,128]{3,2,1,0:T(8,128)(2,1)S(1)}, u32[]{:S(2)}, u32[]{:S(2)}) collective-permute-start(bf16[4,2,256,128]{3,2,1,0:T(8,128)(2,1)S(1)} %pad_maximum_fusion.refs_1_), channel_id=1, source_target_pairs={{0,2},{1,3},{2,4},{3,5},{4,6},{5,7},{6,0},{7,1},{8,10},{9,11},{10,... | collective-permute-start | bytes 1572872 | tf_op jit(solution)/shard_map/ppermute | solution.py:41
  38.9 12.0 %collective-permute-start.5 = (bf16[4,2,256,128]{3,2,1,0:T(8,128)(2,1)S(1)}, bf16[4,2,256,128]{3,2,1,0:T(8,128)(2,1)S(1)}, u32[]{:S(2)}, u32[]{:S(2)}) collective-permute-start(bf16[4,2,256,128]{3,2,1,0:T(8,128)(2,1)S(1)} %pad_maximum_fusion.refs_1_), channel_id=1, source_target_pairs={{0,6},{1,7},{2,0},{3,1},{4,2},{5,3},{6,4},{7,5},{8,14},{9,15},{10,... | collective-permute-start | bytes 1572872 | tf_op jit(solution)/shard_map/ppermute | solution.py:41
  49.3 20.4 %copy-start.5 = (bf16[4,2,256,128]{3,2,1,0:T(8,128)(2,1)}, bf16[4,2,256,128]{3,2,1,0:T(8,128)(2,1)S(1)}, u32[]{:S(2)}) copy-start(bf16[4,2,256,128]{3,2,1,0:T(8,128)(2,1)S(1)} %collective-permute-done.4.refs_2_) | copy-start | bytes 1572868
  49.4 7.7 %collective-permute-start.6 = (bf16[2,2,256,128]{3,2,1,0:T(8,128)(2,1)S(1)}, bf16[2,2,256,128]{3,2,1,0:T(8,128)(2,1)S(1)}, u32[]{:S(2)}, u32[]{:S(2)}) collective-permute-start(bf16[2,2,256,128]{3,2,1,0:T(8,128)(2,1)S(1)} %slice.65), channel_id=1, source_target_pairs={{0,2},{1,3},{2,4},{3,5},{4,6},{5,7},{6,0},{7,1},{8,10},{9,11},{10,... | collective-permute-start | bytes 786440 | tf_op jit(solution)/shard_map/ppermute | solution.py:41
  50.9 18.8 %copy-start.8 = (bf16[4,2,256,128]{3,2,1,0:T(8,128)(2,1)}, bf16[4,2,256,128]{3,2,1,0:T(8,128)(2,1)S(1)}, u32[]{:S(2)}) copy-start(bf16[4,2,256,128]{3,2,1,0:T(8,128)(2,1)S(1)} %collective-permute-done.5.refs_3_) | copy-start | bytes 1572868
  50.9 6.6 %collective-permute-start.7 = (bf16[2,2,256,128]{3,2,1,0:T(8,128)(2,1)S(1)}, bf16[2,2,256,128]{3,2,1,0:T(8,128)(2,1)}, u32[]{:S(2)}, u32[]{:S(2)}) collective-permute-start(bf16[2,2,256,128]{3,2,1,0:T(8,128)(2,1)S(1)} %slice.66), channel_id=1, source_target_pairs={{0,6},{1,7},{2,0},{3,1},{4,2},{5,3},{6,4},{7,5},{8,14},{9,15},{10,... | collective-permute-start | bytes 786440 | tf_op jit(solution)/shard_map/ppermute | solution.py:41
  52.8 4.8 %collective-permute-start.8 = (bf16[4,2,256,128]{3,2,1,0:T(8,128)(2,1)S(1)}, bf16[4,2,256,128]{3,2,1,0:T(8,128)(2,1)S(1)}, u32[]{:S(2)}, u32[]{:S(2)}) collective-permute-start(bf16[4,2,256,128]{3,2,1,0:T(8,128)(2,1)S(1)} %pad_maximum_fusion.refs_1_), channel_id=1, source_target_pairs={{0,1},{1,0},{2,3},{3,2},{4,5},{5,4},{6,7},{7,6},{8,9},{9,8},{10,11... | collective-permute-start | bytes 1572872 | tf_op jit(solution)/shard_map/ppermute | solution.py:41
  52.8 4.8 %collective-permute-start.9 = (bf16[4,2,256,128]{3,2,1,0:T(8,128)(2,1)S(1)}, bf16[4,2,256,128]{3,2,1,0:T(8,128)(2,1)S(1)}, u32[]{:S(2)}, u32[]{:S(2)}) collective-permute-start(bf16[4,2,256,128]{3,2,1,0:T(8,128)(2,1)S(1)} %collective-permute-done.4.refs_2_), channel_id=1, source_target_pairs={{0,1},{1,0},{2,3},{3,2},{4,5},{5,4},{6,7},{7,6},{8,9},{9,8},{10,11... | collective-permute-start | bytes 1572872 | tf_op jit(solution)/shard_map/ppermute | solution.py:41
  53.3 4.4 %collective-permute-start.10 = (bf16[4,2,256,128]{3,2,1,0:T(8,128)(2,1)S(1)}, bf16[4,2,256,128]{3,2,1,0:T(8,128)(2,1)S(1)}, u32[]{:S(2)}, u32[]{:S(2)}) collective-permute-start(bf16[4,2,256,128]{3,2,1,0:T(8,128)(2,1)S(1)} %collective-permute-done.5.refs_3_), channel_id=1, source_target_pairs={{0,1},{1,0},{2,3},{3,2},{4,5},{5,4},{6,7},{7,6},{8,9},{9,8},{10,11... | collective-permute-start | bytes 1572872 | tf_op jit(solution)/shard_map/ppermute | solution.py:41
  57.0 1.7 collective-permute-start.11
  57.5 1.9 %collective-permute-start.12 = (bf16[2,2,256,128]{3,2,1,0:T(8,128)(2,1)}, bf16[2,2,256,128]{3,2,1,0:T(8,128)(2,1)}, u32[]{:S(2)}, u32[]{:S(2)}) collective-permute-start(bf16[2,2,256,128]{3,2,1,0:T(8,128)(2,1)} %collective-permute-done.7.refs_5_), channel_id=1, source_target_pairs={{0,1},{1,0},{2,3},{3,2},{4,5},{5,4},{6,7},{7,6},{8,9},{9,8},{10,11... | collective-permute-start | bytes 786440 | tf_op jit(solution)/shard_map/ppermute | solution.py:41
  57.6 12.1 %copy-start.11 = (bf16[4,2,256,128]{3,2,1,0:T(8,128)(2,1)}, bf16[4,2,256,128]{3,2,1,0:T(8,128)(2,1)S(1)}, u32[]{:S(2)}) copy-start(bf16[4,2,256,128]{3,2,1,0:T(8,128)(2,1)S(1)} %collective-permute-done.8.refs_6_) | copy-start | bytes 1572868
  57.6 12.1 %copy-start.14 = (bf16[4,2,256,128]{3,2,1,0:T(8,128)(2,1)}, bf16[4,2,256,128]{3,2,1,0:T(8,128)(2,1)S(1)}, u32[]{:S(2)}) copy-start(bf16[4,2,256,128]{3,2,1,0:T(8,128)(2,1)S(1)} %collective-permute-done.9.refs_7_) | copy-start | bytes 1572868
  57.6 12.1 %copy-start.17 = (bf16[4,2,256,128]{3,2,1,0:T(8,128)(2,1)}, bf16[4,2,256,128]{3,2,1,0:T(8,128)(2,1)S(1)}, u32[]{:S(2)}) copy-start(bf16[4,2,256,128]{3,2,1,0:T(8,128)(2,1)S(1)} %collective-permute-done.10.refs_8_) | copy-start | bytes 1572868
  59.4 1.9 %copy-start = (bf16[6144,256]{1,0:T(8,128)(2,1)S(1)}, bf16[6144,256]{1,0:T(8,128)(2,1)}, u32[]{:S(2)}) copy-start(bf16[6144,256]{1,0:T(8,128)(2,1)} %all-gather.2.cloned.1.call-done) | copy-start | bytes 9437188
  63.6 23.3 %collective-permute-start.13 = (bf16[3,256,256]{2,1,0:T(8,128)(2,1)S(1)}, bf16[3,256,256]{2,1,0:T(8,128)(2,1)}, u32[]{:S(2)}, u32[]{:S(2)}) collective-permute-start(bf16[3,256,256]{2,1,0:T(8,128)(2,1)S(1)} %partial_sent.1), channel_id=1, source_target_pairs={{0,32},{1,33},{2,34},{3,35},{4,36},{5,37},{6,38},{7,39},{8,40},{9,... | collective-permute-start | bytes 1179656 | tf_op jit(solution)/shard_map/ppermute | solution.py:41
  72.2 0.9 copy-start.23
  89.1 16.2 %copy-start.1 = (bf16[6144,256]{1,0:T(8,128)(2,1)S(1)}, bf16[6144,256]{1,0:T(8,128)(2,1)}, u32[]{:S(2)}) copy-start(bf16[6144,256]{1,0:T(8,128)(2,1)} %all-gather.2.cloned.1.call-done) | copy-start | bytes 9437188
  89.1 19.8 %collective-permute-start.14 = (bf16[3,256,256]{2,1,0:T(8,128)(2,1)}, bf16[3,256,256]{2,1,0:T(8,128)(2,1)S(1)}, u32[]{:S(2)}, u32[]{:S(2)}) collective-permute-start(bf16[3,256,256]{2,1,0:T(8,128)(2,1)} %gated.1.refs_11_.refs_1_), channel_id=1, source_target_pairs={{0,32},{1,33},{2,34},{3,35},{4,36},{5,37},{6,38},{7,39},{8,40},{9,... | collective-permute-start | bytes 1179656 | tf_op jit(solution)/shard_map/ppermute | solution.py:41
  95.6 1.0 copy-start.3
  96.6 1.0 copy-start.6
  97.7 1.0 copy-start.9
  98.7 1.0 copy-start.12
  99.7 1.0 copy-start.15
  100.8 1.0 copy-start.18
  101.8 1.0 copy-start.22
  105.3 4.3 %copy-start.7 = (bf16[4,2,256,128]{3,2,1,0:T(8,128)(2,1)S(1)}, bf16[4,2,256,128]{3,2,1,0:T(8,128)(2,1)}, u32[]{:S(2)}) copy-start(bf16[4,2,256,128]{3,2,1,0:T(8,128)(2,1)} %copy-done.5) | copy-start | bytes 1572868
  105.3 4.3 %copy-start.10 = (bf16[4,2,256,128]{3,2,1,0:T(8,128)(2,1)S(1)}, bf16[4,2,256,128]{3,2,1,0:T(8,128)(2,1)}, u32[]{:S(2)}) copy-start(bf16[4,2,256,128]{3,2,1,0:T(8,128)(2,1)} %copy-done.8) | copy-start | bytes 1572868
  105.3 4.3 %copy-start.13 = (bf16[4,2,256,128]{3,2,1,0:T(8,128)(2,1)S(1)}, bf16[4,2,256,128]{3,2,1,0:T(8,128)(2,1)}, u32[]{:S(2)}) copy-start(bf16[4,2,256,128]{3,2,1,0:T(8,128)(2,1)} %copy-done.11) | copy-start | bytes 1572868
  105.3 4.3 %copy-start.16 = (bf16[4,2,256,128]{3,2,1,0:T(8,128)(2,1)S(1)}, bf16[4,2,256,128]{3,2,1,0:T(8,128)(2,1)}, u32[]{:S(2)}) copy-start(bf16[4,2,256,128]{3,2,1,0:T(8,128)(2,1)} %copy-done.14) | copy-start | bytes 1572868
  105.3 4.3 %copy-start.19 = (bf16[4,2,256,128]{3,2,1,0:T(8,128)(2,1)S(1)}, bf16[4,2,256,128]{3,2,1,0:T(8,128)(2,1)}, u32[]{:S(2)}) copy-start(bf16[4,2,256,128]{3,2,1,0:T(8,128)(2,1)} %copy-done.17) | copy-start | bytes 1572868
  107.7 1.0 copy-start.24
  108.6 1.0 copy-start.26
  109.6 2.8 %copy-start.20 = (bf16[3,256,256]{2,1,0:T(8,128)(2,1)}, bf16[3,256,256]{2,1,0:T(8,128)(2,1)S(1)}, u32[]{:S(2)}) copy-start(bf16[3,256,256]{2,1,0:T(8,128)(2,1)S(1)} %collective-permute-done.14.refs_1_.refs_11_) | copy-start | bytes 1179652
  112.4 1.6 copy-start.4
  114.1 1.0 copy-start.21
  114.1 4.3 %collective-permute-start.15 = (bf16[2,4,2,256,128]{4,3,2,1,0:T(8,128)(2,1)}, bf16[2,4,2,256,128]{4,3,2,1,0:T(8,128)(2,1)S(1)}, u32[]{:S(2)}, u32[]{:S(2)}) collective-permute-start(bf16[2,4,2,256,128]{4,3,2,1,0:T(8,128)(2,1)} %copy-done.26), channel_id=1, source_target_pairs={{0,1},{1,0},{2,3},{3,2},{4,5},{5,4},{6,7},{7,6},{8,9},{9,8},{10,11... | collective-permute-start | bytes 3145736 | tf_op jit(solution)/shard_map/ppermute | solution.py:41
  116.6 3.0 %copy-start.25 = (bf16[2,4,2,256,128]{4,3,2,1,0:T(8,128)(2,1)S(1)}, bf16[2,4,2,256,128]{4,3,2,1,0:T(8,128)(2,1)}, u32[]{:S(2)}) copy-start(bf16[2,4,2,256,128]{4,3,2,1,0:T(8,128)(2,1)} %copy-done.24) | copy-start | bytes 3145732
  116.6 3.0 %collective-permute-start.16 = (bf16[2,4,2,256,128]{4,3,2,1,0:T(8,128)(2,1)S(1)}, bf16[2,4,2,256,128]{4,3,2,1,0:T(8,128)(2,1)S(1)}, u32[]{:S(2)}, u32[]{:S(2)}) collective-permute-start(bf16[2,4,2,256,128]{4,3,2,1,0:T(8,128)(2,1)S(1)} %outputs_sent.1), channel_id=1, source_target_pairs={{0,1},{1,0},{2,3},{3,2},{4,5},{5,4},{6,7},{7,6},{8,9},{9,8},{10,11... | collective-permute-start | bytes 3145736 | tf_op jit(solution)/shard_map/ppermute | solution.py:41
  120.7 10.0 %collective-permute-start.17 = (bf16[2,2,256,128]{3,2,1,0:T(8,128)(2,1)S(1)}, bf16[2,2,256,128]{3,2,1,0:T(8,128)(2,1)S(1)}, u32[]{:S(2)}, u32[]{:S(2)}) collective-permute-start(bf16[2,2,256,128]{3,2,1,0:T(8,128)(2,1)S(1)} %get-tuple-element.56), channel_id=1, source_target_pairs={{0,2},{1,3},{2,4},{3,5},{4,6},{5,7},{6,0},{7,1},{8,10},{9,11},{10,... | collective-permute-start | bytes 786440 | tf_op jit(solution)/shard_map/ppermute | solution.py:41
  122.4 8.3 %collective-permute-start.19 = (bf16[2,2,256,128]{3,2,1,0:T(8,128)(2,1)S(1)}, bf16[2,2,256,128]{3,2,1,0:T(8,128)(2,1)S(1)}, u32[]{:S(2)}, u32[]{:S(2)}) collective-permute-start(bf16[2,2,256,128]{3,2,1,0:T(8,128)(2,1)S(1)} %get-tuple-element.57), channel_id=1, source_target_pairs={{0,6},{1,7},{2,0},{3,1},{4,2},{5,3},{6,4},{7,5},{8,14},{9,15},{10,... | collective-permute-start | bytes 786440 | tf_op jit(solution)/shard_map/ppermute | solution.py:41
  131.0 13.8 %collective-permute-start.20 = (bf16[4,2,256,128]{3,2,1,0:T(8,128)(2,1)S(1)}, bf16[4,2,256,128]{3,2,1,0:T(8,128)(2,1)S(1)}, u32[]{:S(2)}, u32[]{:S(2)}) collective-permute-start(bf16[4,2,256,128]{3,2,1,0:T(8,128)(2,1)S(1)} %pad_maximum_fusion.2), channel_id=1, source_target_pairs={{0,6},{1,7},{2,0},{3,1},{4,2},{5,3},{6,4},{7,5},{8,14},{9,15},{10,... | collective-permute-start | bytes 1572872 | tf_op jit(solution)/shard_map/ppermute | solution.py:41
  134.1 14.1 %collective-permute-start.18 = (bf16[4,2,256,128]{3,2,1,0:T(8,128)(2,1)S(1)}, bf16[4,2,256,128]{3,2,1,0:T(8,128)(2,1)S(1)}, u32[]{:S(2)}, u32[]{:S(2)}) collective-permute-start(bf16[4,2,256,128]{3,2,1,0:T(8,128)(2,1)S(1)} %pad_maximum_fusion.1), channel_id=1, source_target_pairs={{0,2},{1,3},{2,4},{3,5},{4,6},{5,7},{6,0},{7,1},{8,10},{9,11},{10,... | collective-permute-start | bytes 1572872 | tf_op jit(solution)/shard_map/ppermute | solution.py:41
  148.5 10.1 %collective-permute-start.21 = (bf16[2,256,128]{2,1,0:T(8,128)(2,1)S(1)}, bf16[2,256,128]{2,1,0:T(8,128)(2,1)S(1)}, u32[]{:S(2)}, u32[]{:S(2)}) collective-permute-start(bf16[2,256,128]{2,1,0:T(8,128)(2,1)S(1)} %get-tuple-element.62), channel_id=1, source_target_pairs={{0,8},{1,9},{2,10},{3,11},{4,12},{5,13},{6,14},{7,15},{8,16},{9,17... | collective-permute-start | bytes 393224 | tf_op jit(solution)/shard_map/ppermute | solution.py:41
  148.6 11.1 %collective-permute-start.22 = (bf16[2,256,128]{2,1,0:T(8,128)(2,1)S(1)}, bf16[2,256,128]{2,1,0:T(8,128)(2,1)S(1)}, u32[]{:S(2)}, u32[]{:S(2)}) collective-permute-start(bf16[2,256,128]{2,1,0:T(8,128)(2,1)S(1)} %get-tuple-element.61), channel_id=1, source_target_pairs={{0,16},{1,17},{2,18},{3,19},{4,20},{5,21},{6,22},{7,23},{8,24},{9,... | collective-permute-start | bytes 393224 | tf_op jit(solution)/shard_map/ppermute | solution.py:41
  150.8 8.9 %collective-permute-start.23 = (bf16[2,256,128]{2,1,0:T(8,128)(2,1)S(1)}, bf16[2,256,128]{2,1,0:T(8,128)(2,1)S(1)}, u32[]{:S(2)}, u32[]{:S(2)}) collective-permute-start(bf16[2,256,128]{2,1,0:T(8,128)(2,1)S(1)} %get-tuple-element.60), channel_id=1, source_target_pairs={{0,24},{1,25},{2,26},{3,27},{4,28},{5,29},{6,30},{7,31},{8,0},{9,1... | collective-permute-start | bytes 393224 | tf_op jit(solution)/shard_map/ppermute | solution.py:41
  159.8 10.1 %collective-permute-start.24 = (bf16[2,256,128]{2,1,0:T(8,128)(2,1)S(1)}, bf16[2,256,128]{2,1,0:T(8,128)(2,1)S(1)}, u32[]{:S(2)}, u32[]{:S(2)}) collective-permute-start(bf16[2,256,128]{2,1,0:T(8,128)(2,1)S(1)} %fusion.6), channel_id=1, source_target_pairs={{0,32},{1,33},{2,34},{3,35},{4,0},{5,1},{6,2},{7,3},{8,40},{9,41},... | collective-permute-start | bytes 393224 | tf_op jit(solution)/shard_map/ppermute | solution.py:41
Sparse Core Ops, SparseCore 0:
  10.5 44.2 all-gather.1
  114.2 40.8 reduce-scatter.1

commit v6 on v5

--- a/solution.py
+++ b/solution.py
@@ -440,10 +440,8 @@
     rows_other = move(rows_own, other_hi)
     inverse_scale = 1.0 / (tokens.shape[0] * lax.axis_size("dp"))
     grad = grads(True, inverse_scale, place, pieces, rows_own)
-    rows_own, grad = lax.optimization_barrier((rows_own, grad))
     own_sent, own_kept = outputs(("sent", "kept"), place, rows_own, weights)
     own_got = move(own_sent, other_core)
-    rows_other, own_kept = lax.optimization_barrier((rows_other, own_kept))
     grad = grads(False, inverse_scale, place, pieces, rows_other, grad)
     grad = lax.psum_scatter(
         grad.reshape(6144, 256), "dp", scatter_dimension=0, tiled=True, axis_index_groups=X_GROUPS

time: 180 us -> 183 us (1.017); the launches traced: 177 us -> 183 us
  waiting for transfers between devices: 70 us -> 82.2 us
  local copies, waits for them, and re-layouts: 15.2 us -> 9.25 us
    ppermute x25, waiting for transfers between devices: 68.5 us -> 82.1 us  [move(): return lax.ppermute(value, ALL, pairs)]
    unnamed x58 -> x20, local copies, waits for them, and re-layouts: 14.3 us -> 8.35 us
  transfers between devices with their start and end apart: 27 -> 27, of which waited for: 16 -> 15; matrix products, arithmetic and copies ran while one was open for 0% -> 0% of each run, Pallas kernels for 11% -> 11%
where the time goes in v6:
time: 183 us
  waiting for transfers between devices  82.2 us (45%)
  starting transfers between devices  46.9 us (26%)
  Pallas kernels  29.6 us (16%)
  between operations  14.3 us (8%)
  local copies, waits for them, and re-layouts  9.25 us (5%)
    ppermute x25, waiting for transfers between devices, move(): return lax.ppermute(value, ALL, pairs)  82.1 us
    ppermute x25, starting transfers between devices, move(): return lax.ppermute(value, ALL, pairs)  46.8 us
    unnamed x20, local copies, waits for them, and re-layouts  8.35 us
    pallas_call x3, Pallas kernels, outputs(): pl.pallas_call(lambda *refs: outputs_kernel(sides, *refs), in_specs=[SMEM...  5.35 us
    pallas_call x2, Pallas kernels, grads(): pl.pallas_call(lambda *refs: grads_kernel(own_rows, inverse_scale, *refs)...  5.19 us
    pallas_call x2, Pallas kernels, partial(): pl.pallas_call(lambda *refs: partial_kernel(mine, *refs), in_specs=[SMEM]...  4.74 us
    pallas_call x1, Pallas kernels, gu_update(): pl.pallas_call(gu_adam_kernel, grid=(parts, 1), in_specs=[block, block, b...  4.52 us
  transfers between devices with their start and end apart: 27, of which 15 were waited for; matrix products, arithmetic and copies ran while one was open for 0% of the time, Pallas kernels for 11%

profile of v6, /device:TPU:2, one launch (start us, length us, event | category | flops | bytes accessed | tf_op | source)
XLA Modules:
  0.0 182.8 jit_solution(16676928935859233657)
XLA Ops:
  7.2 0.0 all-gather.2.cloned.1.call-start
  7.2 3.1 %quantize.1 = bf16[3,512,256]{2,1,0:T(8,128)(2,1)} custom-call(f32[2,512,256]{2,1,0:T(8,128)} %master.3, s32[2,128,256]{2,1,0:T(8,128)} %codes.3, s32[2,256]{1,0:T(2,128)} %expo.1, f32[256,512]{1,0:T(8,128)} %master.2, s32[64,512]{1,0:T(8,128)} %codes.2, s32[1,512]{1,0:T(1,128)} %bitcast.75), custom_call_target="tpu_custom_call" | custom-call | tf_op jit(solution)/shard_map/quantize/pallas_call | solution.py:425
  10.3 0.0 reduce-scatter.2.cloned.1.call-start
  10.4 3.3 %collective-permute-start = (bf16[2,256,128]{2,1,0:T(8,128)(2,1)S(1)}, bf16[2,256,128]{2,1,0:T(8,128)(2,1)S(1)}, u32[]{:S(2)}, u32[]{:S(2)}) collective-permute-start(bf16[2,256,128]{2,1,0:T(8,128)(2,1)S(1)} %pad_maximum_fusion.3), channel_id=1, source_target_pairs={{0,4},{1,5},{2,6},{3,7},{4,36},{5,37},{6,38},{7,39},{8,12},{9,13},... | collective-permute-start | bytes 393224 | tf_op jit(solution)/shard_map/ppermute | solution.py:41
  13.7 7.6 %collective-permute-done = bf16[2,256,128]{2,1,0:T(8,128)(2,1)S(1)} collective-permute-done((bf16[2,256,128]{2,1,0:T(8,128)(2,1)S(1)}, bf16[2,256,128]{2,1,0:T(8,128)(2,1)S(1)}, u32[]{:S(2)}, u32[]{:S(2)}) %collective-permute-start) | collective-permute-done | bytes 131104 | tf_op jit(solution)/shard_map/ppermute | solution.py:41
  21.3 3.1 %collective-permute-start.3 = (bf16[2,256,128]{2,1,0:T(8,128)(2,1)S(1)}, bf16[2,256,128]{2,1,0:T(8,128)(2,1)S(1)}, u32[]{:S(2)}, u32[]{:S(2)}) collective-permute-start(bf16[2,256,128]{2,1,0:T(8,128)(2,1)S(1)} %collective-permute-done), channel_id=1, source_target_pairs={{0,24},{1,25},{2,26},{3,27},{4,28},{5,29},{6,30},{7,31},{8,0},{9,1... | collective-permute-start | bytes 393224 | tf_op jit(solution)/shard_map/ppermute | solution.py:41
  24.4 2.1 %collective-permute-start.2 = (bf16[2,256,128]{2,1,0:T(8,128)(2,1)S(1)}, bf16[2,256,128]{2,1,0:T(8,128)(2,1)S(1)}, u32[]{:S(2)}, u32[]{:S(2)}) collective-permute-start(bf16[2,256,128]{2,1,0:T(8,128)(2,1)S(1)} %collective-permute-done), channel_id=1, source_target_pairs={{0,16},{1,17},{2,18},{3,19},{4,20},{5,21},{6,22},{7,23},{8,24},{9,... | collective-permute-start | bytes 393224 | tf_op jit(solution)/shard_map/ppermute | solution.py:41
  26.5 1.3 collective-permute-start.1
  27.8 1.2 collective-permute-done.3
  29.0 8.2 %collective-permute-done.2 = bf16[2,256,128]{2,1,0:T(8,128)(2,1)S(1)} collective-permute-done((bf16[2,256,128]{2,1,0:T(8,128)(2,1)S(1)}, bf16[2,256,128]{2,1,0:T(8,128)(2,1)S(1)}, u32[]{:S(2)}, u32[]{:S(2)}) %collective-permute-start.2) | collective-permute-done | bytes 131104 | tf_op jit(solution)/shard_map/ppermute | solution.py:41
  37.2 0.1 pad_maximum_fusion.refs_1_
  37.3 1.7 collective-permute-start.4
  38.9 1.7 collective-permute-start.5
  40.6 8.8 %collective-permute-done.4.refs_2_ = bf16[4,2,256,128]{3,2,1,0:T(8,128)(2,1)S(1)} collective-permute-done((bf16[4,2,256,128]{3,2,1,0:T(8,128)(2,1)S(1)}, bf16[4,2,256,128]{3,2,1,0:T(8,128)(2,1)S(1)}, u32[]{:S(2)}, u32[]{:S(2)}) %collective-permute-start.4) | collective-permute-done | bytes 524320 | tf_op jit(solution)/shard_map/ppermute | solution.py:41
  49.3 1.5 collective-permute-start.6
  50.9 1.8 %collective-permute-start.7 = (bf16[2,2,256,128]{3,2,1,0:T(8,128)(2,1)S(1)}, bf16[2,2,256,128]{3,2,1,0:T(8,128)(2,1)}, u32[]{:S(2)}, u32[]{:S(2)}) collective-permute-start(bf16[2,2,256,128]{3,2,1,0:T(8,128)(2,1)S(1)} %slice.66), channel_id=1, source_target_pairs={{0,6},{1,7},{2,0},{3,1},{4,2},{5,3},{6,4},{7,5},{8,14},{9,15},{10,... | collective-permute-start | bytes 786440 | tf_op jit(solution)/shard_map/ppermute | solution.py:41
  52.8 0.5 collective-permute-start.10
  53.3 3.7 %collective-permute-done.6.refs_4_ = bf16[2,2,256,128]{3,2,1,0:T(8,128)(2,1)S(1)} collective-permute-done((bf16[2,2,256,128]{3,2,1,0:T(8,128)(2,1)S(1)}, bf16[2,2,256,128]{3,2,1,0:T(8,128)(2,1)S(1)}, u32[]{:S(2)}, u32[]{:S(2)}) %collective-permute-start.6) | collective-permute-done | bytes 262176 | tf_op jit(solution)/shard_map/ppermute | solution.py:41
  57.0 0.5 collective-permute-done.7.refs_5_
  57.5 0.0 collective-permute-start.12
  57.5 0.1 stack.47.refs_0_.place
  57.6 1.1 collective-permute-done.11.refs_9_
  58.7 0.7 collective-permute-done.12.refs_10_
  59.4 1.9 %copy-done = bf16[6144,256]{1,0:T(8,128)(2,1)S(1)} copy-done((bf16[6144,256]{1,0:T(8,128)(2,1)S(1)}, bf16[6144,256]{1,0:T(8,128)(2,1)}, u32[]{:S(2)}) %copy-start) | copy-done | bytes 3145752
  61.2 2.3 %partial_sent.1 = bf16[3,256,256]{2,1,0:T(8,128)(2,1)S(1)} custom-call(s32[5]{0:T(128)S(1)} %stack.47.refs_0_.place, bf16[4,2,256,128]{3,2,1,0:T(8,128)(2,1)S(1)} %pad_maximum_fusion.refs_1_, bf16[4,2,256,128]{3,2,1,0:T(8,128)(2,1)S(1)} %collective-permute-done.4.refs_2_, bf16[4,2,256,128]{3,2,1,0:T(8,128)(2,1)S(1)} %collective-permute-done.5.refs_3_, ...), custom_call_target="tpu_custom_call" | custom-call | tf_op jit(solution)/shard_map/partial_sent/pallas_call | solution.py:245
  63.6 6.1 %collective-permute-start.13 = (bf16[3,256,256]{2,1,0:T(8,128)(2,1)S(1)}, bf16[3,256,256]{2,1,0:T(8,128)(2,1)}, u32[]{:S(2)}, u32[]{:S(2)}) collective-permute-start(bf16[3,256,256]{2,1,0:T(8,128)(2,1)S(1)} %partial_sent.1), channel_id=1, source_target_pairs={{0,32},{1,33},{2,34},{3,35},{4,36},{5,37},{6,38},{7,39},{8,40},{9,... | collective-permute-start | bytes 1179656 | tf_op jit(solution)/shard_map/ppermute | solution.py:41
  69.7 2.4 %partial_own.1.own = f32[3,256,256]{2,1,0:T(8,128)S(1)} custom-call(s32[5]{0:T(128)S(1)} %stack.47.refs_0_.place, bf16[4,2,256,128]{3,2,1,0:T(8,128)(2,1)S(1)} %pad_maximum_fusion.refs_1_, bf16[4,2,256,128]{3,2,1,0:T(8,128)(2,1)S(1)} %collective-permute-done.4.refs_2_, bf16[4,2,256,128]{3,2,1,0:T(8,128)(2,1)S(1)} %collective-permute-done.5.refs_3_, ...), custom_call_target="tpu_custom_call" | custom-call | tf_op jit(solution)/shard_map/partial_own/pallas_call | solution.py:245
  72.1 0.9 copy-done.7
  73.0 13.9 %collective-permute-done.13.sent = bf16[3,256,256]{2,1,0:T(8,128)(2,1)} collective-permute-done((bf16[3,256,256]{2,1,0:T(8,128)(2,1)S(1)}, bf16[3,256,256]{2,1,0:T(8,128)(2,1)}, u32[]{:S(2)}, u32[]{:S(2)}) %collective-permute-start.13) | collective-permute-done | bytes 393248 | tf_op jit(solution)/shard_map/ppermute | solution.py:41
  86.9 2.2 %gated.1.refs_1_.refs_11_ = bf16[3,256,256]{2,1,0:T(8,128)(2,1)} custom-call(f32[3,256,256]{2,1,0:T(8,128)} %copy-done.7, bf16[3,256,256]{2,1,0:T(8,128)(2,1)} %collective-permute-done.13.sent), custom_call_target="tpu_custom_call" | custom-call | tf_op jit(solution)/shard_map/gated/pallas_call | solution.py:268
  89.0 6.5 %collective-permute-start.15 = (bf16[3,256,256]{2,1,0:T(8,128)(2,1)}, bf16[3,256,256]{2,1,0:T(8,128)(2,1)S(1)}, u32[]{:S(2)}, u32[]{:S(2)}) collective-permute-start(bf16[3,256,256]{2,1,0:T(8,128)(2,1)} %gated.1.refs_1_.refs_11_), channel_id=1, source_target_pairs={{0,32},{1,33},{2,34},{3,35},{4,36},{5,37},{6,38},{7,39},{8,40},{9,... | collective-permute-start | bytes 1179656 | tf_op jit(solution)/shard_map/ppermute | solution.py:41
  95.6 1.0 copy-done.5
  96.6 2.5 %own_grads.1.refs_12_ = bf16[4,3,512,256]{3,2,1,0:T(8,128)(2,1)S(1)} custom-call(s32[5]{0:T(128)S(1)} %stack.47.refs_0_.place, bf16[4,2,256,128]{3,2,1,0:T(8,128)(2,1)S(1)} %pad_maximum_fusion.refs_1_, bf16[4,2,256,128]{3,2,1,0:T(8,128)(2,1)S(1)} %collective-permute-done.4.refs_2_, bf16[4,2,256,128]{3,2,1,0:T(8,128)(2,1)S(1)} %collective-permute-done.5.refs_3_, ...), custom_call_target="tpu_custom_call" | custom-call | tf_op jit(solution)/shard_map/own_grads/pallas_call | solution.py:368
  99.0 9.8 %collective-permute-done.15.refs_1_.refs_11_ = bf16[3,256,256]{2,1,0:T(8,128)(2,1)S(1)} collective-permute-done((bf16[3,256,256]{2,1,0:T(8,128)(2,1)}, bf16[3,256,256]{2,1,0:T(8,128)(2,1)S(1)}, u32[]{:S(2)}, u32[]{:S(2)}) %collective-permute-start.15) | collective-permute-done | bytes 393248 | tf_op jit(solution)/shard_map/ppermute | solution.py:41
  108.8 2.7 %arrived_grads.1 = bf16[4,3,512,256]{3,2,1,0:T(8,128)(2,1)S(1)} custom-call(s32[5]{0:T(128)S(1)} %stack.47.refs_0_.place, bf16[4,2,256,128]{3,2,1,0:T(8,128)(2,1)S(1)} %pad_maximum_fusion.refs_1_, bf16[4,2,256,128]{3,2,1,0:T(8,128)(2,1)S(1)} %collective-permute-done.4.refs_2_, bf16[4,2,256,128]{3,2,1,0:T(8,128)(2,1)S(1)} %collective-permute-done.5.refs_3_, ...), custom_call_target="tpu_custom_call" | custom-call | tf_op jit(solution)/shard_map/arrived_grads/pallas_call | solution.py:368
  111.6 1.7 copy-done.2
  113.3 1.9 %copy-done.1 = bf16[6144,256]{1,0:T(8,128)(2,1)S(1)} copy-done((bf16[6144,256]{1,0:T(8,128)(2,1)S(1)}, bf16[6144,256]{1,0:T(8,128)(2,1)}, u32[]{:S(2)}) %copy-start.1) | copy-done | bytes 3145752
  115.2 1.0 copy-done.6
  116.2 2.3 %outputs_sent_kept.1 = (bf16[2,4,2,256,128]{4,3,2,1,0:T(8,128)(2,1)S(1)}, bf16[2,4,2,256,128]{4,3,2,1,0:T(8,128)(2,1)S(1)}) custom-call(s32[5]{0:T(128)S(1)} %stack.47.refs_0_.place, bf16[3,256,256]{2,1,0:T(8,128)(2,1)S(1)} %copy-done.6, bf16[4,3,512,256]{3,2,1,0:T(8,128)(2,1)S(1)} %bitcast.62), custom_call_target="tpu_custom_call" | custom-call | tf_op jit(solution)/shard_map/outputs_sent_kept/pallas_call | solution.py:300
  118.5 0.1 collective-permute-start.14
  118.6 1.5 outputs_sent.1
  120.1 0.8 collective-permute-start.16
  120.9 1.5 outputs_kept.1.arrived_got
  122.4 0.8 collective-permute-done.16.arrived_kept
  123.2 1.1 combine.1
  124.3 0.1 slice_bitcast_fusion.6
  124.4 1.7 collective-permute-start.17
  126.1 1.8 collective-permute-start.19
  127.8 6.7 %collective-permute-done.17 = bf16[2,2,256,128]{3,2,1,0:T(8,128)(2,1)S(1)} collective-permute-done((bf16[2,2,256,128]{3,2,1,0:T(8,128)(2,1)S(1)}, bf16[2,2,256,128]{3,2,1,0:T(8,128)(2,1)S(1)}, u32[]{:S(2)}, u32[]{:S(2)}) %collective-permute-start.17) | collective-permute-done | bytes 262176 | tf_op jit(solution)/shard_map/ppermute | solution.py:41
  134.6 0.1 fusion.2
  134.8 3.1 %collective-permute-start.20 = (bf16[4,2,256,128]{3,2,1,0:T(8,128)(2,1)S(1)}, bf16[4,2,256,128]{3,2,1,0:T(8,128)(2,1)S(1)}, u32[]{:S(2)}, u32[]{:S(2)}) collective-permute-start(bf16[4,2,256,128]{3,2,1,0:T(8,128)(2,1)S(1)} %pad_maximum_fusion.2), channel_id=1, source_target_pairs={{0,6},{1,7},{2,0},{3,1},{4,2},{5,3},{6,4},{7,5},{8,14},{9,15},{10,... | collective-permute-start | bytes 1572872 | tf_op jit(solution)/shard_map/ppermute | solution.py:41
  138.0 0.1 collective-permute-start.18
  138.1 10.8 %collective-permute-done.20 = bf16[4,2,256,128]{3,2,1,0:T(8,128)(2,1)S(1)} collective-permute-done((bf16[4,2,256,128]{3,2,1,0:T(8,128)(2,1)S(1)}, bf16[4,2,256,128]{3,2,1,0:T(8,128)(2,1)S(1)}, u32[]{:S(2)}, u32[]{:S(2)}) %collective-permute-start.20) | collective-permute-done | bytes 524320 | tf_op jit(solution)/shard_map/ppermute | solution.py:41
  148.8 3.5 %collective-permute-done.18 = bf16[4,2,256,128]{3,2,1,0:T(8,128)(2,1)S(1)} collective-permute-done((bf16[4,2,256,128]{3,2,1,0:T(8,128)(2,1)S(1)}, bf16[4,2,256,128]{3,2,1,0:T(8,128)(2,1)S(1)}, u32[]{:S(2)}, u32[]{:S(2)}) %collective-permute-start.18) | collective-permute-done | bytes 524320 | tf_op jit(solution)/shard_map/ppermute | solution.py:41
  152.4 0.2 fusion.7
  152.6 0.1 collective-permute-start.23
  152.7 3.0 %collective-permute-start.22 = (bf16[2,256,128]{2,1,0:T(8,128)(2,1)S(1)}, bf16[2,256,128]{2,1,0:T(8,128)(2,1)S(1)}, u32[]{:S(2)}, u32[]{:S(2)}) collective-permute-start(bf16[2,256,128]{2,1,0:T(8,128)(2,1)S(1)} %get-tuple-element.53), channel_id=1, source_target_pairs={{0,16},{1,17},{2,18},{3,19},{4,20},{5,21},{6,22},{7,23},{8,24},{9,... | collective-permute-start | bytes 393224 | tf_op jit(solution)/shard_map/ppermute | solution.py:41
  155.7 1.9 %collective-permute-start.21 = (bf16[2,256,128]{2,1,0:T(8,128)(2,1)S(1)}, bf16[2,256,128]{2,1,0:T(8,128)(2,1)S(1)}, u32[]{:S(2)}, u32[]{:S(2)}) collective-permute-start(bf16[2,256,128]{2,1,0:T(8,128)(2,1)S(1)} %get-tuple-element.54), channel_id=1, source_target_pairs={{0,8},{1,9},{2,10},{3,11},{4,12},{5,13},{6,14},{7,15},{8,16},{9,17... | collective-permute-start | bytes 393224 | tf_op jit(solution)/shard_map/ppermute | solution.py:41
  157.7 3.5 %down_adam.1 = (f32[256,512]{1,0:T(8,128)}, f32[256,512]{1,0:T(8,128)}, f32[256,512]{1,0:T(8,128)}, bf16[256,512]{1,0:T(8,128)(2,1)}) custom-call(bf16[3,512,256]{2,1,0:T(8,128)(2,1)} %bitcast.67, f32[256,512]{1,0:T(8,128)} %master.2, f32[256,512]{1,0:T(8,128)} %first.2, f32[256,512]{1,0:T(8,128)} %second.2, s32[64,512]{1,0:T(8,128)} %codes.2, s32[1,512]{1,0:T(1,128)} %bitcast.76), custom_call_target="tpu_custom_call" | custom-call | tf_op jit(solution)/shard_map/down_adam/pallas_call | solution.py:176
  161.1 4.9 %collective-permute-done.22 = bf16[2,256,128]{2,1,0:T(8,128)(2,1)S(1)} collective-permute-done((bf16[2,256,128]{2,1,0:T(8,128)(2,1)S(1)}, bf16[2,256,128]{2,1,0:T(8,128)(2,1)S(1)}, u32[]{:S(2)}, u32[]{:S(2)}) %collective-permute-start.22) | collective-permute-done | bytes 131104 | tf_op jit(solution)/shard_map/ppermute | solution.py:41
  166.1 0.1 fusion.6
  166.2 4.6 %collective-permute-start.24 = (bf16[2,256,128]{2,1,0:T(8,128)(2,1)S(1)}, bf16[2,256,128]{2,1,0:T(8,128)(2,1)S(1)}, u32[]{:S(2)}, u32[]{:S(2)}) collective-permute-start(bf16[2,256,128]{2,1,0:T(8,128)(2,1)S(1)} %fusion.6), channel_id=1, source_target_pairs={{0,32},{1,33},{2,34},{3,35},{4,0},{5,1},{6,2},{7,3},{8,40},{9,41},... | collective-permute-start | bytes 393224 | tf_op jit(solution)/shard_map/ppermute | solution.py:41
  170.7 4.5 %gu_adam.1 = (f32[2,512,256]{2,1,0:T(8,128)}, f32[2,512,256]{2,1,0:T(8,128)}, f32[2,512,256]{2,1,0:T(8,128)}, bf16[2,512,256]{2,1,0:T(8,128)(2,1)}) custom-call(bf16[3,512,256]{2,1,0:T(8,128)(2,1)} %bitcast.68, f32[2,512,256]{2,1,0:T(8,128)} %master.3, f32[2,512,256]{2,1,0:T(8,128)} %first.3, f32[2,512,256]{2,1,0:T(8,128)} %second.3, s32[2,128,256]{2,1,0:T(8,128)} %codes.3, ...), custom_call_target="tpu_custom_call" | custom-call | tf_op jit(solution)/shard_map/gu_adam/pallas_call | solution.py:159
  175.3 0.7 slice_bitcast_fusion.11
  (37 shorter events, 0.3 us)
Async XLA Ops:
  7.2 3.2 %copy-start.8 = (bf16[256,128]{1,0:T(8,128)(2,1)S(1)}, bf16[256,128]{1,0:T(8,128)(2,1)}, u32[]{:S(2)}) copy-start(bf16[256,128]{1,0:T(8,128)(2,1)} %param.13) | copy-start | bytes 196612
  7.2 3.2 %copy-start.9 = (bf16[256,128]{1,0:T(8,128)(2,1)S(1)}, bf16[256,128]{1,0:T(8,128)(2,1)}, u32[]{:S(2)}) copy-start(bf16[256,128]{1,0:T(8,128)(2,1)} %param.12) | copy-start | bytes 196612
  7.2 50.3 %all-gather.2.cloned.1.call-start = ((), (), s32[]{:S(2)}) async-start(), calls=%async_computation.1 | async-start | bytes 3932160 | tf_op jit(solution)/shard_map/all_gather | solution.py:432
  10.3 147.3 %reduce-scatter.2.cloned.1.call-start = ((), (), s32[]{:S(2)}) async-start(), calls=%async_computation.2 | async-start | bytes 3932160 | tf_op jit(solution)/shard_map/reduce_scatter | solution.py:446
  10.4 10.9 %collective-permute-start = (bf16[2,256,128]{2,1,0:T(8,128)(2,1)S(1)}, bf16[2,256,128]{2,1,0:T(8,128)(2,1)S(1)}, u32[]{:S(2)}, u32[]{:S(2)}) collective-permute-start(bf16[2,256,128]{2,1,0:T(8,128)(2,1)S(1)} %pad_maximum_fusion.3), channel_id=1, source_target_pairs={{0,4},{1,5},{2,6},{3,7},{4,36},{5,37},{6,38},{7,39},{8,12},{9,13},... | collective-permute-start | bytes 393224 | tf_op jit(solution)/shard_map/ppermute | solution.py:41
  21.3 7.7 %collective-permute-start.3 = (bf16[2,256,128]{2,1,0:T(8,128)(2,1)S(1)}, bf16[2,256,128]{2,1,0:T(8,128)(2,1)S(1)}, u32[]{:S(2)}, u32[]{:S(2)}) collective-permute-start(bf16[2,256,128]{2,1,0:T(8,128)(2,1)S(1)} %collective-permute-done), channel_id=1, source_target_pairs={{0,24},{1,25},{2,26},{3,27},{4,28},{5,29},{6,30},{7,31},{8,0},{9,1... | collective-permute-start | bytes 393224 | tf_op jit(solution)/shard_map/ppermute | solution.py:41
  24.4 12.8 %collective-permute-start.2 = (bf16[2,256,128]{2,1,0:T(8,128)(2,1)S(1)}, bf16[2,256,128]{2,1,0:T(8,128)(2,1)S(1)}, u32[]{:S(2)}, u32[]{:S(2)}) collective-permute-start(bf16[2,256,128]{2,1,0:T(8,128)(2,1)S(1)} %collective-permute-done), channel_id=1, source_target_pairs={{0,16},{1,17},{2,18},{3,19},{4,20},{5,21},{6,22},{7,23},{8,24},{9,... | collective-permute-start | bytes 393224 | tf_op jit(solution)/shard_map/ppermute | solution.py:41
  26.5 10.7 %collective-permute-start.1 = (bf16[2,256,128]{2,1,0:T(8,128)(2,1)S(1)}, bf16[2,256,128]{2,1,0:T(8,128)(2,1)S(1)}, u32[]{:S(2)}, u32[]{:S(2)}) collective-permute-start(bf16[2,256,128]{2,1,0:T(8,128)(2,1)S(1)} %collective-permute-done), channel_id=1, source_target_pairs={{0,8},{1,9},{2,10},{3,11},{4,12},{5,13},{6,14},{7,15},{8,16},{9,17... | collective-permute-start | bytes 393224 | tf_op jit(solution)/shard_map/ppermute | solution.py:41
  37.3 12.1 %collective-permute-start.4 = (bf16[4,2,256,128]{3,2,1,0:T(8,128)(2,1)S(1)}, bf16[4,2,256,128]{3,2,1,0:T(8,128)(2,1)S(1)}, u32[]{:S(2)}, u32[]{:S(2)}) collective-permute-start(bf16[4,2,256,128]{3,2,1,0:T(8,128)(2,1)S(1)} %pad_maximum_fusion.refs_1_), channel_id=1, source_target_pairs={{0,2},{1,3},{2,4},{3,5},{4,6},{5,7},{6,0},{7,1},{8,10},{9,11},{10,... | collective-permute-start | bytes 1572872 | tf_op jit(solution)/shard_map/ppermute | solution.py:41
  38.9 12.0 %collective-permute-start.5 = (bf16[4,2,256,128]{3,2,1,0:T(8,128)(2,1)S(1)}, bf16[4,2,256,128]{3,2,1,0:T(8,128)(2,1)S(1)}, u32[]{:S(2)}, u32[]{:S(2)}) collective-permute-start(bf16[4,2,256,128]{3,2,1,0:T(8,128)(2,1)S(1)} %pad_maximum_fusion.refs_1_), channel_id=1, source_target_pairs={{0,6},{1,7},{2,0},{3,1},{4,2},{5,3},{6,4},{7,5},{8,14},{9,15},{10,... | collective-permute-start | bytes 1572872 | tf_op jit(solution)/shard_map/ppermute | solution.py:41
  49.3 7.7 %collective-permute-start.6 = (bf16[2,2,256,128]{3,2,1,0:T(8,128)(2,1)S(1)}, bf16[2,2,256,128]{3,2,1,0:T(8,128)(2,1)S(1)}, u32[]{:S(2)}, u32[]{:S(2)}) collective-permute-start(bf16[2,2,256,128]{3,2,1,0:T(8,128)(2,1)S(1)} %slice.65), channel_id=1, source_target_pairs={{0,2},{1,3},{2,4},{3,5},{4,6},{5,7},{6,0},{7,1},{8,10},{9,11},{10,... | collective-permute-start | bytes 786440 | tf_op jit(solution)/shard_map/ppermute | solution.py:41
  50.9 6.6 %collective-permute-start.7 = (bf16[2,2,256,128]{3,2,1,0:T(8,128)(2,1)S(1)}, bf16[2,2,256,128]{3,2,1,0:T(8,128)(2,1)}, u32[]{:S(2)}, u32[]{:S(2)}) collective-permute-start(bf16[2,2,256,128]{3,2,1,0:T(8,128)(2,1)S(1)} %slice.66), channel_id=1, source_target_pairs={{0,6},{1,7},{2,0},{3,1},{4,2},{5,3},{6,4},{7,5},{8,14},{9,15},{10,... | collective-permute-start | bytes 786440 | tf_op jit(solution)/shard_map/ppermute | solution.py:41
  52.8 4.8 %collective-permute-start.8 = (bf16[4,2,256,128]{3,2,1,0:T(8,128)(2,1)S(1)}, bf16[4,2,256,128]{3,2,1,0:T(8,128)(2,1)S(1)}, u32[]{:S(2)}, u32[]{:S(2)}) collective-permute-start(bf16[4,2,256,128]{3,2,1,0:T(8,128)(2,1)S(1)} %pad_maximum_fusion.refs_1_), channel_id=1, source_target_pairs={{0,1},{1,0},{2,3},{3,2},{4,5},{5,4},{6,7},{7,6},{8,9},{9,8},{10,11... | collective-permute-start | bytes 1572872 | tf_op jit(solution)/shard_map/ppermute | solution.py:41
  52.8 4.8 %collective-permute-start.10 = (bf16[4,2,256,128]{3,2,1,0:T(8,128)(2,1)S(1)}, bf16[4,2,256,128]{3,2,1,0:T(8,128)(2,1)S(1)}, u32[]{:S(2)}, u32[]{:S(2)}) collective-permute-start(bf16[4,2,256,128]{3,2,1,0:T(8,128)(2,1)S(1)} %collective-permute-done.5.refs_3_), channel_id=1, source_target_pairs={{0,1},{1,0},{2,3},{3,2},{4,5},{5,4},{6,7},{7,6},{8,9},{9,8},{10,11... | collective-permute-start | bytes 1572872 | tf_op jit(solution)/shard_map/ppermute | solution.py:41
  53.3 5.4 %collective-permute-start.9 = (bf16[4,2,256,128]{3,2,1,0:T(8,128)(2,1)S(1)}, bf16[4,2,256,128]{3,2,1,0:T(8,128)(2,1)S(1)}, u32[]{:S(2)}, u32[]{:S(2)}) collective-permute-start(bf16[4,2,256,128]{3,2,1,0:T(8,128)(2,1)S(1)} %collective-permute-done.4.refs_2_), channel_id=1, source_target_pairs={{0,1},{1,0},{2,3},{3,2},{4,5},{5,4},{6,7},{7,6},{8,9},{9,8},{10,11... | collective-permute-start | bytes 1572872 | tf_op jit(solution)/shard_map/ppermute | solution.py:41
  57.0 1.7 collective-permute-start.11
  57.5 1.9 %collective-permute-start.12 = (bf16[2,2,256,128]{3,2,1,0:T(8,128)(2,1)}, bf16[2,2,256,128]{3,2,1,0:T(8,128)(2,1)}, u32[]{:S(2)}, u32[]{:S(2)}) collective-permute-start(bf16[2,2,256,128]{3,2,1,0:T(8,128)(2,1)} %collective-permute-done.7.refs_5_), channel_id=1, source_target_pairs={{0,1},{1,0},{2,3},{3,2},{4,5},{5,4},{6,7},{7,6},{8,9},{9,8},{10,11... | collective-permute-start | bytes 786440 | tf_op jit(solution)/shard_map/ppermute | solution.py:41
  59.4 1.9 %copy-start = (bf16[6144,256]{1,0:T(8,128)(2,1)S(1)}, bf16[6144,256]{1,0:T(8,128)(2,1)}, u32[]{:S(2)}) copy-start(bf16[6144,256]{1,0:T(8,128)(2,1)} %all-gather.2.cloned.1.call-done) | copy-start | bytes 9437188
  63.6 23.3 %collective-permute-start.13 = (bf16[3,256,256]{2,1,0:T(8,128)(2,1)S(1)}, bf16[3,256,256]{2,1,0:T(8,128)(2,1)}, u32[]{:S(2)}, u32[]{:S(2)}) collective-permute-start(bf16[3,256,256]{2,1,0:T(8,128)(2,1)S(1)} %partial_sent.1), channel_id=1, source_target_pairs={{0,32},{1,33},{2,34},{3,35},{4,36},{5,37},{6,38},{7,39},{8,40},{9,... | collective-permute-start | bytes 1179656 | tf_op jit(solution)/shard_map/ppermute | solution.py:41
  72.1 0.9 copy-start.7
  89.0 19.8 %collective-permute-start.15 = (bf16[3,256,256]{2,1,0:T(8,128)(2,1)}, bf16[3,256,256]{2,1,0:T(8,128)(2,1)S(1)}, u32[]{:S(2)}, u32[]{:S(2)}) collective-permute-start(bf16[3,256,256]{2,1,0:T(8,128)(2,1)} %gated.1.refs_1_.refs_11_), channel_id=1, source_target_pairs={{0,32},{1,33},{2,34},{3,35},{4,36},{5,37},{6,38},{7,39},{8,40},{9,... | collective-permute-start | bytes 1179656 | tf_op jit(solution)/shard_map/ppermute | solution.py:41
  95.6 1.0 copy-start.5
  108.8 2.8 %copy-start.3 = (bf16[3,256,256]{2,1,0:T(8,128)(2,1)}, bf16[3,256,256]{2,1,0:T(8,128)(2,1)S(1)}, u32[]{:S(2)}) copy-start(bf16[3,256,256]{2,1,0:T(8,128)(2,1)S(1)} %collective-permute-done.15.refs_1_.refs_11_) | copy-start | bytes 1179652
  111.6 1.7 copy-start.2
  113.3 1.9 %copy-start.1 = (bf16[6144,256]{1,0:T(8,128)(2,1)S(1)}, bf16[6144,256]{1,0:T(8,128)(2,1)}, u32[]{:S(2)}) copy-start(bf16[6144,256]{1,0:T(8,128)(2,1)} %all-gather.2.cloned.1.call-done) | copy-start | bytes 9437188
  115.2 1.0 copy-start.6
  116.2 2.4 %copy-start.4 = (bf16[3,256,256]{2,1,0:T(8,128)(2,1)S(1)}, bf16[3,256,256]{2,1,0:T(8,128)(2,1)}, u32[]{:S(2)}) copy-start(bf16[3,256,256]{2,1,0:T(8,128)(2,1)} %copy-done.3) | copy-start | bytes 1179652
  118.5 3.9 %collective-permute-start.14 = (bf16[2,4,2,256,128]{4,3,2,1,0:T(8,128)(2,1)S(1)}, bf16[2,4,2,256,128]{4,3,2,1,0:T(8,128)(2,1)S(1)}, u32[]{:S(2)}, u32[]{:S(2)}) collective-permute-start(bf16[2,4,2,256,128]{4,3,2,1,0:T(8,128)(2,1)S(1)} %get-tuple-element.30), channel_id=1, source_target_pairs={{0,1},{1,0},{2,3},{3,2},{4,5},{5,4},{6,7},{7,6},{8,9},{9,8},{10,11... | collective-permute-start | bytes 3145736 | tf_op jit(solution)/shard_map/ppermute | solution.py:41
  120.1 3.1 %collective-permute-start.16 = (bf16[2,4,2,256,128]{4,3,2,1,0:T(8,128)(2,1)S(1)}, bf16[2,4,2,256,128]{4,3,2,1,0:T(8,128)(2,1)S(1)}, u32[]{:S(2)}, u32[]{:S(2)}) collective-permute-start(bf16[2,4,2,256,128]{4,3,2,1,0:T(8,128)(2,1)S(1)} %outputs_sent.1), channel_id=1, source_target_pairs={{0,1},{1,0},{2,3},{3,2},{4,5},{5,4},{6,7},{7,6},{8,9},{9,8},{10,11... | collective-permute-start | bytes 3145736 | tf_op jit(solution)/shard_map/ppermute | solution.py:41
  124.4 10.2 %collective-permute-start.17 = (bf16[2,2,256,128]{3,2,1,0:T(8,128)(2,1)S(1)}, bf16[2,2,256,128]{3,2,1,0:T(8,128)(2,1)S(1)}, u32[]{:S(2)}, u32[]{:S(2)}) collective-permute-start(bf16[2,2,256,128]{3,2,1,0:T(8,128)(2,1)S(1)} %get-tuple-element.48), channel_id=1, source_target_pairs={{0,2},{1,3},{2,4},{3,5},{4,6},{5,7},{6,0},{7,1},{8,10},{9,11},{10,... | collective-permute-start | bytes 786440 | tf_op jit(solution)/shard_map/ppermute | solution.py:41
  126.1 8.5 %collective-permute-start.19 = (bf16[2,2,256,128]{3,2,1,0:T(8,128)(2,1)S(1)}, bf16[2,2,256,128]{3,2,1,0:T(8,128)(2,1)S(1)}, u32[]{:S(2)}, u32[]{:S(2)}) collective-permute-start(bf16[2,2,256,128]{3,2,1,0:T(8,128)(2,1)S(1)} %get-tuple-element.49), channel_id=1, source_target_pairs={{0,6},{1,7},{2,0},{3,1},{4,2},{5,3},{6,4},{7,5},{8,14},{9,15},{10,... | collective-permute-start | bytes 786440 | tf_op jit(solution)/shard_map/ppermute | solution.py:41
  134.8 14.0 %collective-permute-start.20 = (bf16[4,2,256,128]{3,2,1,0:T(8,128)(2,1)S(1)}, bf16[4,2,256,128]{3,2,1,0:T(8,128)(2,1)S(1)}, u32[]{:S(2)}, u32[]{:S(2)}) collective-permute-start(bf16[4,2,256,128]{3,2,1,0:T(8,128)(2,1)S(1)} %pad_maximum_fusion.2), channel_id=1, source_target_pairs={{0,6},{1,7},{2,0},{3,1},{4,2},{5,3},{6,4},{7,5},{8,14},{9,15},{10,... | collective-permute-start | bytes 1572872 | tf_op jit(solution)/shard_map/ppermute | solution.py:41
  138.0 14.4 %collective-permute-start.18 = (bf16[4,2,256,128]{3,2,1,0:T(8,128)(2,1)S(1)}, bf16[4,2,256,128]{3,2,1,0:T(8,128)(2,1)S(1)}, u32[]{:S(2)}, u32[]{:S(2)}) collective-permute-start(bf16[4,2,256,128]{3,2,1,0:T(8,128)(2,1)S(1)} %pad_maximum_fusion.1), channel_id=1, source_target_pairs={{0,2},{1,3},{2,4},{3,5},{4,6},{5,7},{6,0},{7,1},{8,10},{9,11},{10,... | collective-permute-start | bytes 1572872 | tf_op jit(solution)/shard_map/ppermute | solution.py:41
  152.6 8.5 %collective-permute-start.23 = (bf16[2,256,128]{2,1,0:T(8,128)(2,1)S(1)}, bf16[2,256,128]{2,1,0:T(8,128)(2,1)S(1)}, u32[]{:S(2)}, u32[]{:S(2)}) collective-permute-start(bf16[2,256,128]{2,1,0:T(8,128)(2,1)S(1)} %get-tuple-element.52), channel_id=1, source_target_pairs={{0,24},{1,25},{2,26},{3,27},{4,28},{5,29},{6,30},{7,31},{8,0},{9,1... | collective-permute-start | bytes 393224 | tf_op jit(solution)/shard_map/ppermute | solution.py:41
  152.7 13.4 %collective-permute-start.22 = (bf16[2,256,128]{2,1,0:T(8,128)(2,1)S(1)}, bf16[2,256,128]{2,1,0:T(8,128)(2,1)S(1)}, u32[]{:S(2)}, u32[]{:S(2)}) collective-permute-start(bf16[2,256,128]{2,1,0:T(8,128)(2,1)S(1)} %get-tuple-element.53), channel_id=1, source_target_pairs={{0,16},{1,17},{2,18},{3,19},{4,20},{5,21},{6,22},{7,23},{8,24},{9,... | collective-permute-start | bytes 393224 | tf_op jit(solution)/shard_map/ppermute | solution.py:41
  155.7 10.3 %collective-permute-start.21 = (bf16[2,256,128]{2,1,0:T(8,128)(2,1)S(1)}, bf16[2,256,128]{2,1,0:T(8,128)(2,1)S(1)}, u32[]{:S(2)}, u32[]{:S(2)}) collective-permute-start(bf16[2,256,128]{2,1,0:T(8,128)(2,1)S(1)} %get-tuple-element.54), channel_id=1, source_target_pairs={{0,8},{1,9},{2,10},{3,11},{4,12},{5,13},{6,14},{7,15},{8,16},{9,17... | collective-permute-start | bytes 393224 | tf_op jit(solution)/shard_map/ppermute | solution.py:41
  166.2 9.1 %collective-permute-start.24 = (bf16[2,256,128]{2,1,0:T(8,128)(2,1)S(1)}, bf16[2,256,128]{2,1,0:T(8,128)(2,1)S(1)}, u32[]{:S(2)}, u32[]{:S(2)}) collective-permute-start(bf16[2,256,128]{2,1,0:T(8,128)(2,1)S(1)} %fusion.6), channel_id=1, source_target_pairs={{0,32},{1,33},{2,34},{3,35},{4,0},{5,1},{6,2},{7,3},{8,40},{9,41},... | collective-permute-start | bytes 393224 | tf_op jit(solution)/shard_map/ppermute | solution.py:41
Sparse Core Ops, SparseCore 0:
  10.5 44.2 all-gather.1
  113.4 41.6 reduce-scatter.1
